TPU v7x, 32 devices: a whole 2x2x4 slice. The times are simulated.
32 devices in a mesh: ctx: 8 (over z, y), head: 4 (over x, core).
Axes of the slice: x: 2, y: 2, z: 4, core: 2. Of those that a mesh axis runs over, the one named last changes fastest.
Arguments:
- lin_q: bfloat16 [1024, 32, 128], P('ctx', 'head'), may hold values from -4 to 4
- lin_k: bfloat16 [1024, 32, 128], P('ctx', 'head'), may hold values from -4 to 4
- lin_v: bfloat16 [1024, 32, 128], P('ctx', 'head'), may hold values from -16 to 16
- lin_decay: float32 [32, 1024], P('head', 'ctx'), may hold values from -1.5 to 0
- norm_gain: float32 [32, 128], P('head'), may hold values from 0.1 to 1.9
- soft_q: bfloat16 [1024, 32, 128], P('ctx', 'head'), may hold values from -5 to 5
- soft_k: bfloat16 [1024, 32, 128], P('ctx', 'head'), may hold values from -5 to 5
- soft_v: bfloat16 [1024, 32, 128], P('ctx', 'head'), may hold values from -5 to 5
- out_grad: bfloat16 [1024, 32, 128], P('ctx', 'head'), may hold values from -5 to 5
- block_lists: int32 [8, 16], P('ctx'), may hold values from 0 to 6, as said below
- block_counts: int32 [8], P('ctx'), may hold values from 0 to 7, as said below
Outputs:
- lin_dq: bfloat16 [1024, 32, 128], P('ctx', 'head')
- lin_dk: bfloat16 [1024, 32, 128], P('ctx', 'head')
- lin_dv: bfloat16 [1024, 32, 128], P('ctx', 'head')
- soft_dq: bfloat16 [1024, 32, 128], P('ctx', 'head')
- soft_dk: bfloat16 [1024, 32, 128], P('ctx', 'head')
- soft_dv: bfloat16 [1024, 32, 128], P('ctx', 'head')
Inputs may be any that keep to these rules, and one draw needn't show every extreme that they name: `block_lists`: entries past block_counts[b] are 0. The first block_counts[b] entries of query block b are distinct blocks that lie before the span of 128 tokens holding b. All query blocks of one span name together at most one block of each other span. In every span after the first, some query block names every block that its span names; from the second span on these include block 0, and from the third on also the last block before the span. `block_counts`: in span i of 128 tokens some query block has the count min(i, 16); every count is at most that; counts are 0 only in the first span.
All inputs are finite; a program needn't handle non-finite values.
Results may differ from a plain program's by a relative error of at most 0.011.
Values may be sent and summed in bfloat16 or wider, within the bound.
No kernel may reach another device: no remote copies, remote signals or barrier semaphores. Data moves between devices by JAX's collectives and lax.ppermute only.
A program may use at most 128 MiB of HBM per device.

v0:
```python
import functools

import jax
import jax.numpy as jnp
from jax import lax
from jax.experimental import pallas as pl
from jax.experimental.pallas import tpu as pltpu
from jax.sharding import PartitionSpec as P

BLK = 128
NSEL = 16
PAD = 16
GROUP = 2
COST = 1024
VMEM_BYTES = (24 * 1024 * 1024, 56 * 1024 * 1024)


epsilon = 1e-05
exact_precision = lax.Precision.HIGHEST


def carried_in(part, axis, combine, identity, reverse):
    count = lax.axis_size(axis)
    place = lax.axis_index(axis)
    ahead = count - 1 - place if reverse else place
    gathered = jax.tree.map(lambda a: lax.all_gather(a, axis), part)
    state = jax.tree.map(lambda a, e: jnp.zeros_like(a) + jnp.asarray(e, a.dtype), part, identity)

    def one(lap, state):
        source = count - 1 - lap if reverse else lap
        return combine(
            state, jax.tree.map(lambda a: lax.dynamic_index_in_dim(a, source, 0, False), gathered)
        )

    return lax.fori_loop(0, ahead, one, state)


def decay_tables(decays):
    running = jnp.cumsum(decays, axis=1)
    finish = running[:, -1]
    length = decays.shape[1]
    below_diag = (jnp.arange(length)[:, None] >= jnp.arange(length)[None, :])[None]
    spread = running[:, :, None] - running[:, None, :]
    within = jnp.where(below_diag, jnp.exp(jnp.where(below_diag, spread, 0.0)), 0.0)
    return (jnp.exp(finish), jnp.exp(finish[:, None] - running), jnp.exp(running), within)


def chain_join(earlier, later):
    return (earlier[0] * later[0], later[0][:, None, None] * earlier[1] + later[1])


def sparse_grads(queries, grads_out, key_rows, value_rows, allowed):
    score_scale = queries.shape[-1] ** (-0.5)
    scores = (
        jnp.einsum("bqhd,bkhd->bhqk", queries, key_rows, preferred_element_type=jnp.float32)
        * score_scale
    )
    key_mask = allowed[:, None]
    scores = jnp.where(key_mask, scores, -1e30)
    row_max = jnp.max(scores, axis=-1, keepdims=True)
    weights = jnp.where(key_mask, jnp.exp(scores - row_max), 0.0)
    softmax_probs = weights / jnp.sum(weights, axis=-1, keepdims=True)
    rounded = softmax_probs.astype(jnp.bfloat16)
    outputs = jnp.einsum("bhqk,bkhd->bqhd", rounded, value_rows, preferred_element_type=jnp.float32)
    row_delta = jnp.sum(grads_out.astype(jnp.float32) * outputs, axis=-1)
    grad_probs = jnp.einsum(
        "bqhd,bkhd->bhqk", grads_out, value_rows, preferred_element_type=jnp.float32
    )
    grad_scores = (
        softmax_probs * (grad_probs - jnp.transpose(row_delta, (0, 2, 1))[..., None])
    ).astype(jnp.bfloat16)
    query_gradient = (
        jnp.einsum("bhqk,bkhd->bqhd", grad_scores, key_rows, preferred_element_type=jnp.float32)
        * score_scale
    )
    key_gradient = (
        jnp.einsum("bhqk,bqhd->bkhd", grad_scores, queries, preferred_element_type=jnp.float32)
        * score_scale
    )
    value_gradient = jnp.einsum(
        "bhqk,bqhd->bkhd", rounded, grads_out, preferred_element_type=jnp.float32
    )
    return (query_gradient, key_gradient, value_gradient)


def local(
    lin_q,
    lin_k,
    lin_v,
    lin_decay,
    norm_gain,
    soft_q,
    soft_k,
    soft_v,
    out_grad,
    block_lists,
    block_counts,
):
    tok_rows, heads_here, head_width = lin_q.shape
    blocks_here = tok_rows // BLK
    span_count = lax.axis_size("ctx")
    own_span = lax.axis_index("ctx")
    total_width = heads_here * lax.axis_size("head") * head_width
    complete_query = lin_q.astype(jnp.float32)
    complete_key = lin_k.astype(jnp.float32)
    complete_value = lin_v.astype(jnp.float32)
    carry_decay, trailing_decay, leading_decay, within = decay_tables(lin_decay)
    state_here = jnp.einsum(
        "boz,bor->ozr",
        complete_key * trailing_decay.T[:, :, None],
        complete_value,
        precision=exact_precision,
    )
    identity = (jnp.ones_like(carry_decay), jnp.zeros_like(state_here))
    incoming_state = carried_in((carry_decay, state_here), "ctx", chain_join, identity, False)[1]
    pair_weights = (
        jnp.einsum("thk,shk->hts", lin_q, lin_k, preferred_element_type=jnp.float32) * within
    )
    layer_out = jnp.einsum("hts,shv->thv", pair_weights, complete_value, precision=exact_precision)
    layer_out = layer_out + leading_decay.T[:, :, None] * jnp.einsum(
        "wfg,fgl->wfl", complete_query, incoming_state, precision=exact_precision
    )
    squares = lax.psum(jnp.sum(layer_out * layer_out, axis=(1, 2)), "head")
    root_mean = jnp.sqrt(squares / total_width + epsilon)
    norm_scale = norm_gain[None]
    all_lists, all_counts = (
        lax.all_gather(block_lists, "ctx", axis=0, tiled=True),
        lax.all_gather(block_counts, "ctx", axis=0, tiled=True),
    )
    entries = blocks_here * NSEL
    every_live = (
        jnp.arange(NSEL)[None, None, :] < all_counts.reshape(span_count, blocks_here)[:, :, None]
    ).reshape(span_count, entries)
    owner_hits = every_live & (all_lists // blocks_here == own_span)
    wanted_here = jnp.max(jnp.where(owner_hits, all_lists % blocks_here, -1), axis=1)
    my_live = jnp.arange(NSEL)[None, :] < block_counts[:, None]
    flat_owner = (block_lists // blocks_here).reshape(entries)
    flat_live = my_live.reshape(entries)
    key_blocks = soft_k.reshape(blocks_here, BLK, heads_here, head_width)
    value_blocks = soft_v.reshape(blocks_here, BLK, heads_here, head_width)
    picked = jnp.clip(wanted_here, 0, blocks_here - 1)
    present = (wanted_here >= 0)[:, None, None, None]
    nothing = jnp.zeros((), jnp.bfloat16)
    send_keys = jnp.where(present, key_blocks[picked], nothing)
    send_values = jnp.where(present, value_blocks[picked], nothing)
    got_keys, got_values = (
        lax.all_to_all(send_keys, "ctx", split_axis=0, concat_axis=0, tiled=True),
        lax.all_to_all(send_values, "ctx", split_axis=0, concat_axis=0, tiled=True),
    )
    listed_keys = jnp.take(got_keys, flat_owner, axis=0).reshape(
        blocks_here, NSEL * BLK, heads_here, head_width
    )
    listed_values = jnp.take(got_values, flat_owner, axis=0).reshape(
        blocks_here, NSEL * BLK, heads_here, head_width
    )
    key_rows = jnp.concatenate([key_blocks, listed_keys], axis=1)
    value_rows = jnp.concatenate([value_blocks, listed_values], axis=1)
    causal = jnp.arange(BLK)[:, None] >= jnp.arange(BLK)[None, :]
    remote_mask = jnp.broadcast_to(
        jnp.repeat(my_live, BLK, axis=1)[:, None, :], (blocks_here, BLK, NSEL * BLK)
    )
    allowed = jnp.concatenate(
        [jnp.broadcast_to(causal, (blocks_here, BLK, BLK)), remote_mask], axis=2
    )
    query_blocks = soft_q.reshape(blocks_here, BLK, heads_here, head_width)
    grad_blocks = out_grad.reshape(blocks_here, BLK, heads_here, head_width)
    query_gradient, key_gradient, value_gradient = sparse_grads(
        query_blocks, grad_blocks, key_rows, value_rows, allowed
    )
    soft_dq = query_gradient.reshape(tok_rows, heads_here, head_width).astype(jnp.bfloat16)
    routing = (
        flat_live[None, :] & (flat_owner[None, :] == jnp.arange(span_count)[:, None])
    ).astype(jnp.float32)
    remote_key = key_gradient[:, BLK:].reshape(entries, BLK, heads_here, head_width)
    remote_value = value_gradient[:, BLK:].reshape(entries, BLK, heads_here, head_width)
    part_key = jnp.einsum("oe,exhd->oxhd", routing, remote_key, precision=exact_precision).astype(
        jnp.bfloat16
    )
    part_value = jnp.einsum(
        "oe,exhd->oxhd", routing, remote_value, precision=exact_precision
    ).astype(jnp.bfloat16)
    back_key, back_value = (
        lax.all_to_all(part_key, "ctx", split_axis=0, concat_axis=0, tiled=True),
        lax.all_to_all(part_value, "ctx", split_axis=0, concat_axis=0, tiled=True),
    )
    placing = (wanted_here[:, None] == jnp.arange(blocks_here)[None, :]).astype(jnp.float32)
    added_key = jnp.einsum(
        "rb,rxhd->bxhd", placing, back_key.astype(jnp.float32), precision=exact_precision
    ).reshape(tok_rows, heads_here, head_width)
    added_value = jnp.einsum(
        "rb,rxhd->bxhd", placing, back_value.astype(jnp.float32), precision=exact_precision
    ).reshape(tok_rows, heads_here, head_width)
    soft_dk = (key_gradient[:, :BLK].reshape(tok_rows, heads_here, head_width) + added_key).astype(
        jnp.bfloat16
    )
    value_total = value_gradient[:, :BLK].reshape(tok_rows, heads_here, head_width) + added_value
    soft_dv = value_total.astype(jnp.bfloat16)
    cotangent = out_grad.astype(jnp.float32) + value_total
    inner_total = lax.psum(jnp.sum(norm_scale * cotangent * layer_out, axis=(1, 2)), "head")
    linear_cotangent = (
        norm_scale * cotangent / root_mean[:, None, None]
        - layer_out * (inner_total / (total_width * root_mean**3))[:, None, None]
    )
    reverse_state = carried_in(
        (
            carry_decay,
            jnp.einsum(
                "boz,bor->ozr",
                complete_query * leading_decay.T[:, :, None],
                linear_cotangent,
                precision=exact_precision,
            ),
        ),
        "ctx",
        chain_join,
        identity,
        True,
    )[1]
    grad_pair = (
        jnp.einsum("thv,shv->hts", linear_cotangent, complete_value, precision=exact_precision)
        * within
    )
    lin_dq = jnp.einsum("hts,shk->thk", grad_pair, complete_key, precision=exact_precision)
    lin_dq = lin_dq + leading_decay.T[:, :, None] * jnp.einsum(
        "fqs,qrs->fqr", linear_cotangent, incoming_state, precision=exact_precision
    )
    lin_dk = jnp.einsum("hts,thk->shk", grad_pair, complete_query, precision=exact_precision)
    lin_dk = lin_dk + trailing_decay.T[:, :, None] * jnp.einsum(
        "fut,ujt->fuj", complete_value, reverse_state, precision=exact_precision
    )
    lin_dv = jnp.einsum("hts,thv->shv", pair_weights, linear_cotangent, precision=exact_precision)
    lin_dv = lin_dv + trailing_decay.T[:, :, None] * jnp.einsum(
        "zpu,pux->zpx", complete_key, reverse_state, precision=exact_precision
    )
    return (
        lin_dq.astype(jnp.bfloat16),
        lin_dk.astype(jnp.bfloat16),
        lin_dv.astype(jnp.bfloat16),
        soft_dq,
        soft_dk,
        soft_dv,
    )


def triple(x):
    top = x.astype(jnp.bfloat16)
    rest = x - top.astype(jnp.float32)
    middle = rest.astype(jnp.bfloat16)
    low = (rest - middle.astype(jnp.float32)).astype(jnp.bfloat16)
    return top, middle, low


def nt(a, b):
    return lax.dot_general(a, b, (((1,), (1,)), ((), ())), preferred_element_type=jnp.float32)


def nn(a, b):
    return lax.dot_general(a, b, (((1,), (0,)), ((), ())), preferred_element_type=jnp.float32)


def tn(a, b):
    return lax.dot_general(a, b, (((0,), (0,)), ((), ())), preferred_element_type=jnp.float32)


def later(half):
    return lax.axis_index("ctx") >= half


def place_in(half):
    return lax.rem(lax.axis_index("ctx"), half)


def spread(source, scratch):
    rows, heads, width = source.shape
    scratch[...] = source[...].astype(jnp.float32).reshape(rows * heads, width)


def head_of(scratch, head, heads):
    return scratch[pl.ds(head, scratch.shape[0] // heads, stride=heads), :]


def soft_head(place, half):
    return 2 * place if place < half else 2 * (place - half) + 1


def pack_soft_kernel(half, *refs):
    sources, sent, scratch = refs[:4], refs[4], refs[5]
    rows, heads, _ = sources[0].shape
    for place, source in enumerate(sources):
        spread(source, scratch)
        for dest in range(2 * half):
            sent[dest, pl.ds(place * rows, rows), :] = head_of(
                scratch, soft_head(dest, half), heads
            ).astype(jnp.bfloat16)


def put_heads(half, outs, scratch, first, second, rows, heads):
    late, me = later(half), place_in(half)
    for step, out in enumerate(outs):
        head = 2 * jnp.bitwise_xor(me, step)
        even, odd = head_of(scratch, head, heads), head_of(scratch, head + 1, heads)
        out[pl.ds(first * rows, rows), :] = jnp.where(late, odd, even).astype(jnp.bfloat16)
        out[pl.ds(second * rows, rows), :] = jnp.where(late, even, odd).astype(jnp.bfloat16)


def pack_lin_kernel(half, *refs):
    sources, decay_ref, gain_ref, outs = refs[:3], refs[3], refs[4], refs[5 : 5 + half]
    scratches, parts_scr = refs[5 + half : 8 + half], refs[8 + half]
    late, me = later(half), place_in(half)
    rows, heads, width = sources[0].shape
    for place, (source, scratch) in enumerate(zip(sources, scratches)):
        spread(source, scratch)
        put_heads(half, outs, scratch, place, 3 + place, rows, heads)
    parts = [*triple(decay_ref[...]), *triple(gain_ref[...])]
    for place, part in enumerate(parts):
        parts_scr[pl.ds(place * heads, heads), :] = part.astype(jnp.float32)
    line = lax.broadcasted_iota(jnp.int32, (PAD, width), 0)
    for step, out in enumerate(outs):
        blocks = []
        for head in range(2):
            at = 2 * jnp.bitwise_xor(me, step) + head
            block = jnp.zeros((PAD, width), jnp.float32)
            for place in range(len(parts)):
                block = jnp.where(line == place, parts_scr[pl.ds(place * heads + at, 1), :], block)
            blocks.append(block)
        even, odd = blocks
        out[pl.ds(6 * rows, PAD), :] = jnp.where(late, odd, even).astype(jnp.bfloat16)
        out[pl.ds(6 * rows + PAD, PAD), :] = jnp.where(late, even, odd).astype(jnp.bfloat16)


def unpack_soft_kernel(half, packed, *refs):
    outs, scratch = refs[:-1], refs[-1]
    rows, heads, width = outs[0].shape
    for place, out in enumerate(outs):
        for source in range(2 * half):
            scratch[pl.ds(soft_head(source, half), rows, stride=heads), :] = packed[
                source, pl.ds(place * rows, rows), :
            ].astype(jnp.float32)
        out[...] = scratch[...].reshape(rows, heads, width).astype(jnp.bfloat16)


def unpack_lin_kernel(half, *refs):
    steps, outs, scratch = refs[:half], refs[half:-1], refs[-1]
    late, me = later(half), place_in(half)
    rows, heads, width = outs[0].shape
    for place, out in enumerate(outs):
        for step, ref in enumerate(steps):
            head = 2 * jnp.bitwise_xor(me, step)
            first = ref[pl.ds(place * rows, rows), :].astype(jnp.float32)
            second = ref[pl.ds((3 + place) * rows, rows), :].astype(jnp.float32)
            scratch[pl.ds(head, rows, stride=heads), :] = jnp.where(late, second, first)
            scratch[pl.ds(head + 1, rows, stride=heads), :] = jnp.where(late, first, second)
        out[...] = scratch[...].reshape(rows, heads, width).astype(jnp.bfloat16)


def soft_part(x_ref, place):
    rows, width = x_ref.shape[1] // 4, x_ref.shape[2]

    def take(tile):
        return x_ref[pl.ds(tile * GROUP, GROUP), pl.ds(place * rows, rows), :].reshape(
            GROUP * rows, width
        )

    return take


def tile_scores(k, q, i, j):
    scores = nt(k(i), q(j))
    if i < j:
        return scores
    key_at = lax.broadcasted_iota(jnp.int32, scores.shape, 0)
    query_at = lax.broadcasted_iota(jnp.int32, scores.shape, 1)
    return jnp.where(key_at <= query_at, scores, -1e30)


def soft_forward_kernel(half, x_ref, lines_ref, dv_ref, own_ref, give_ref, scr, total_scr):
    late = later(half)
    spans, rows, width = dv_ref.shape
    wide, scale = GROUP * rows, width**-0.5
    q, k, v, g = (soft_part(x_ref, place) for place in range(4))
    lines_ref[...] = jnp.zeros_like(lines_ref)
    for j in range(spans // GROUP):
        top = None
        for i in range(j + 1):
            scores = tile_scores(k, q, i, j)
            scr[i] = scores
            here = jnp.max(scores, axis=0, keepdims=True)
            top = here if top is None else jnp.maximum(top, here)
        total = jnp.zeros_like(top)
        for i in range(j + 1):
            weights = jnp.exp((scr[i] - top) * scale)
            scr[i] = weights
            total = total + jnp.sum(weights, axis=0, keepdims=True)
        inverse = 1.0 / total
        out_t = None
        for i in range(j + 1):
            low = (scr[i] * inverse).astype(jnp.bfloat16)
            part = tn(v(i), low)
            out_t = part if out_t is None else out_t + part
            part = nn(low, g(j))
            total_scr[i] = part if i == j else total_scr[i] + part
        delta = jnp.sum(jnp.transpose(g(j).astype(jnp.float32)) * out_t, axis=0, keepdims=True)
        for place, line in enumerate((top, inverse, delta)):
            lines_ref[pl.ds(place, 1), pl.ds(j * wide, wide)] = line
    for i in range(spans // GROUP):
        dv_ref[pl.ds(i * GROUP, GROUP)] = (
            total_scr[i].astype(jnp.bfloat16).reshape(GROUP, rows, width)
        )
        total_scr[i] = total_scr[i] + g(i).astype(jnp.float32)
    tiles = half // GROUP
    for i in range(tiles):
        early, after = total_scr[i], total_scr[tiles + i]
        at = pl.ds(i * wide, wide)
        own_ref[at, :] = jnp.where(late, after, early)
        give_ref[at, :] = jnp.where(late, early, after).astype(jnp.bfloat16)


def soft_backward_kernel(x_ref, lines_ref, dv_ref, packed, dk_scr):
    spans, rows, width = dv_ref.shape
    wide, scale = GROUP * rows, width**-0.5
    q, k, v, g = (soft_part(x_ref, place) for place in range(4))
    for j in range(spans // GROUP):
        top, inverse, delta = (
            lines_ref[pl.ds(place, 1), pl.ds(j * wide, wide)] for place in range(3)
        )
        dq_t = None
        for i in range(j + 1):
            probs = jnp.exp((tile_scores(k, q, i, j) - top) * scale) * inverse
            grad_scores = (probs * (nt(v(i), g(j)) - delta)).astype(jnp.bfloat16)
            part = tn(k(i), grad_scores)
            dq_t = part if dq_t is None else dq_t + part
            part = nn(grad_scores, q(j))
            dk_scr[i] = part if i == j else dk_scr[i] + part
        dq = (jnp.transpose(dq_t) * scale).astype(jnp.bfloat16)
        packed[pl.ds(j * GROUP, GROUP), pl.ds(0, rows), :] = dq.reshape(GROUP, rows, width)
    for i in range(spans // GROUP):
        dk = (dk_scr[i] * scale).astype(jnp.bfloat16)
        packed[pl.ds(i * GROUP, GROUP), pl.ds(rows, rows), :] = dk.reshape(GROUP, rows, width)
    packed[:, pl.ds(2 * rows, rows), :] = dv_ref[...]


def span_tables(extra):
    rows = extra.shape[1]
    first = lax.broadcasted_iota(jnp.int32, (rows, rows), 0)
    second = lax.broadcasted_iota(jnp.int32, (rows, rows), 1)
    lower = first >= second
    along = nn(extra, (first <= second).astype(jnp.float32).astype(jnp.bfloat16))
    down = nt(lower.astype(jnp.float32).astype(jnp.bfloat16), extra)
    row = along[0:1] + along[1:2] + along[2:3]
    col = down[:, 0:1] + down[:, 1:2] + down[:, 2:3]
    finish = row[:, rows - 1 : rows]
    return row, col, finish, lower, first <= second


def gain_of(extra):
    wide = extra.astype(jnp.float32)
    return wide[3:4] + wide[4:5] + wide[5:6]


def lin_parts(x_ref, slot, span, rows):
    q, k, v = (
        x_ref[span, pl.ds((slot * 3 + place) * rows, rows), :] for place in range(3)
    )
    return q, k, v, x_ref[span, pl.ds(6 * rows + slot * PAD, PAD), :]


def lin_local_kernel(half, rows, *refs):
    steps, (x_ref, out_ref, states_ref, give_ref) = refs[:half], refs[half:]
    me = place_in(half)
    for step, ref in enumerate(steps):
        x_ref[jnp.bitwise_xor(me, step)] = ref[...]
    width = x_ref.shape[2]
    for slot in range(2):
        state = jnp.zeros((width, width), jnp.float32)
        for span in range(half):
            q, k, v, extra = lin_parts(x_ref, slot, span, rows)
            row, col, finish, lower, _ = span_tables(extra)
            within = jnp.exp(jnp.where(lower, col - row, -1e30))
            pair = (nt(q, k) * within).astype(jnp.bfloat16)
            out = nn(pair, v)
            if span > 0:
                low_state = state.astype(jnp.bfloat16)
                states_ref[slot, span] = low_state
                out = out + jnp.exp(col) * nn(q, low_state)
            else:
                states_ref[slot, span] = jnp.zeros((width, width), jnp.bfloat16)
            out_ref[slot, span] = out
            decayed = (k.astype(jnp.float32) * jnp.exp(finish - col)).astype(jnp.bfloat16)
            state = jnp.exp(finish) * state + tn(decayed, v)
        give_ref[1 - slot] = state.astype(jnp.bfloat16)


def lin_sums_kernel(half, rows, x_ref, own_ref, far_ref, local_ref, given_ref, cot_ref, out_ref, sums_ref):
    before = [jnp.zeros((1, 1), jnp.float32)] * 2
    for span in range(half):
        at = pl.ds(span * rows, rows)
        inner, squares = None, None
        for slot, part_ref in enumerate((own_ref, far_ref)):
            q, _, _, extra = lin_parts(x_ref, slot, span, rows)
            _, col, finish, _, _ = span_tables(extra)
            out = local_ref[slot, span] + jnp.exp(before[slot] + col) * nn(q, given_ref[slot])
            before[slot] = before[slot] + finish
            out_ref[slot, span] = out
            scaled = gain_of(extra) * part_ref[at, :].astype(jnp.float32)
            cot_ref[slot, span] = scaled
            inner = scaled * out if slot == 0 else inner + scaled * out
            squares = out * out if slot == 0 else squares + out * out
        sums_ref[pl.ds(span, 1), :] = jnp.sum(jnp.transpose(squares), axis=0, keepdims=True)
        sums_ref[pl.ds(half + span, 1), :] = jnp.sum(jnp.transpose(inner), axis=0, keepdims=True)


def lin_cot_kernel(half, rows, total_width, x_ref, cot_ref, out_ref, sums_ref, low_ref, state_ref):
    width = cot_ref.shape[3]
    mean = sums_ref[pl.ds(0, half), :] / total_width + epsilon
    root = jnp.sqrt(mean)
    inner = sums_ref[pl.ds(half, half), :] / (total_width * root * mean)
    scalars = jnp.transpose(jnp.concatenate([1.0 / root, inner], axis=0))
    for slot in range(2):
        state = jnp.zeros((width, width), jnp.float32)
        for span in reversed(range(half)):
            q, _, _, extra = lin_parts(x_ref, slot, span, rows)
            _, col, finish, _, _ = span_tables(extra)
            cotangent = (
                cot_ref[slot, span] * scalars[:, span : span + 1]
                - out_ref[slot, span] * scalars[:, half + span : half + span + 1]
            )
            low_cot = cotangent.astype(jnp.bfloat16)
            low_ref[slot, span] = low_cot
            decayed = (q.astype(jnp.float32) * jnp.exp(col)).astype(jnp.bfloat16)
            state = jnp.exp(finish) * state + tn(decayed, low_cot)
        state_ref[1 - slot] = state.astype(jnp.bfloat16)


def lin_own_kernel(half, rows, x_ref, low_ref, states_ref, given_ref, dq_ref, made_ref):
    width = low_ref.shape[3]
    for slot in range(2):
        before = [jnp.zeros((1, 1), jnp.float32)]
        for span in range(half):
            finish = span_tables(lin_parts(x_ref, slot, span, rows)[3])[2]
            before.append(before[-1] + finish)
        given = given_ref[slot].astype(jnp.float32)
        state = jnp.zeros((width, width), jnp.float32)
        for span in reversed(range(half)):
            q, k, v, extra = lin_parts(x_ref, slot, span, rows)
            row, col, finish, lower, upper = span_tables(extra)
            within = jnp.exp(jnp.where(lower, col - row, -1e30))
            within_t = jnp.exp(jnp.where(upper, row - col, -1e30))
            low_cot = low_ref[slot, span]
            grad_pair = (nt(low_cot, v) * within).astype(jnp.bfloat16)
            grad_pair_t = (nt(v, low_cot) * within_t).astype(jnp.bfloat16)
            pair_t = (nt(k, q) * within_t).astype(jnp.bfloat16)
            leading = jnp.exp(col)
            trailing = jnp.exp(finish - col)
            low_state = state.astype(jnp.bfloat16)
            carried = states_ref[slot, span].astype(jnp.float32) + jnp.exp(before[span]) * given
            dq = nn(grad_pair, k) + leading * nt(low_cot, carried.astype(jnp.bfloat16))
            dq_ref[slot, span] = dq.astype(jnp.bfloat16)
            made_ref[slot, 0, span] = nn(grad_pair_t, q) + trailing * nt(v, low_state)
            made_ref[slot, 1, span] = nn(pair_t, low_cot) + trailing * nn(k, low_state)
            decayed = (q.astype(jnp.float32) * leading).astype(jnp.bfloat16)
            state = jnp.exp(finish) * state + tn(decayed, low_cot)


def lin_finish_kernel(half, rows, x_ref, dq_ref, made_ref, state_ref, *refs):
    outs, packed = refs[:half], refs[half]
    for slot in range(2):
        state = state_ref[slot]
        after = jnp.zeros((1, 1), jnp.float32)
        for span in reversed(range(half)):
            _, k, v, extra = lin_parts(x_ref, slot, span, rows)
            _, col, finish, _, _ = span_tables(extra)
            trailing = jnp.exp(after + finish - col)
            after = after + finish
            dk = made_ref[slot, 0, span] + trailing * nt(v, state)
            dv = made_ref[slot, 1, span] + trailing * nn(k, state)
            for place, made in enumerate((dq_ref[slot, span], dk, dv)):
                packed[span, pl.ds((slot * 3 + place) * rows, rows), :] = made.astype(
                    jnp.bfloat16
                )
    for step, out in enumerate(outs):
        out[...] = packed[jnp.bitwise_xor(place_in(half), step)]


def call(name, kernel, out_shape, scratch, cost, *args):
    with jax.named_scope(name):
        return pl.pallas_call(
            kernel,
            out_shape=out_shape,
            scratch_shapes=scratch,
            name=name,
            compiler_params=pltpu.CompilerParams(vmem_limit_bytes=VMEM_BYTES[name.startswith("pack_soft")]),
            cost_estimate=pl.CostEstimate(flops=cost, bytes_accessed=1024, transcendentals=0),
        )(*args)


def by_halves(lin_q, lin_k, lin_v, lin_decay, norm_gain, soft_q, soft_k, soft_v, out_grad):
    rows, heads, width = lin_q.shape
    spans = lax.axis_size("ctx")
    half = spans // 2
    tokens = half * rows
    total_width = heads * lax.axis_size("head") * width
    low = lambda *s: jax.ShapeDtypeStruct(s, jnp.bfloat16)
    full = lambda *s: jax.ShapeDtypeStruct(s, jnp.float32)
    held = lambda *s: pltpu.VMEM(s, jnp.float32)
    bind = functools.partial
    tiles, wide = spans // GROUP, GROUP * rows
    after = lax.optimization_barrier

    def moved(x, pairs):
        return lax.ppermute(x, "ctx", pairs)

    def exchanged(parts):
        return [parts[0]] + [
            moved(parts[step], [(i, i ^ step) for i in range(spans)]) for step in range(1, half)
        ]

    both = [(i, i ^ half) for i in range(spans)]
    up = [(i, i + half) for i in range(half)]
    down = [(i + half, i) for i in range(half)]
    turned = held(rows * heads, width)
    mine = (low(rows, heads, width),) * 3
    soft_sent = call(
        "pack_soft", bind(pack_soft_kernel, half), low(spans, 4 * rows, width), [turned], 11960000000,
        soft_q, soft_k, soft_v, out_grad,
    )
    x = lax.all_to_all(soft_sent, "ctx", 0, 0, tiled=True)
    lin_sent = call(
        "pack_lin", bind(pack_lin_kernel, half), (low(6 * rows + 2 * PAD, width),) * half,
        [turned] * 3 + [held(6 * heads, width)], 5980000000,
        lin_q, lin_k, lin_v, lin_decay, norm_gain,
    )
    lin_got = exchanged(lin_sent)
    lines, dv, own, give = call(
        "soft_forward", bind(soft_forward_kernel, half),
        (full(8, spans * rows), low(spans, rows, width), full(tokens, width), low(tokens, width)),
        [held(tiles, wide, wide), held(tiles, wide, width)], COST, x,
    )
    far = moved(give, both)
    lin_got[0], own = after((lin_got[0], own))
    lin_x, local_out, states, state = call(
        "lin_local", bind(lin_local_kernel, half, rows),
        (
            low(half, 6 * rows + 2 * PAD, width),
            full(2, half, rows, width),
            low(2, half, width, width),
            low(2, width, width),
        ),
        [], 13340000000, *lin_got,
    )
    state = moved(state, up)
    soft_made = call(
        "soft_backward", soft_backward_kernel, low(spans, 3 * rows, width),
        [held(tiles, wide, width)], 16560000000, x, lines, dv,
    )
    far, soft_made = after((far, soft_made))
    cot, layer_out, sums = call(
        "lin_sums", bind(lin_sums_kernel, half, rows),
        (full(2, half, rows, width),) * 2 + (full(2 * half, rows),), [], COST,
        lin_x, own, far, local_out, state,
    )
    soft_made, sums = after((soft_made, sums))
    soft_back = lax.all_to_all(soft_made, "ctx", 0, 0, tiled=True)
    for axis, reach in (("head", lax.axis_size("head")), ("ctx", half)):
        count = lax.axis_size(axis)
        sums = after(sums)
        sums = sums + sum(
            lax.ppermute(sums, axis, [(i, i ^ step) for i in range(count)])
            for step in range(1, reach)
        )
    low_cot, late_state = call(
        "lin_cot", bind(lin_cot_kernel, half, rows, total_width),
        (low(2, half, rows, width), low(2, width, width)), [], COST,
        lin_x, cot, layer_out, sums,
    )
    late_state = moved(late_state, down)
    lin_dq, lin_made = call(
        "lin_own", bind(lin_own_kernel, half, rows),
        (low(2, half, rows, width), full(2, 2, half, rows, width)), [], COST,
        lin_x, low_cot, states, state,
    )
    lin_made = call(
        "lin_finish", bind(lin_finish_kernel, half, rows), (low(6 * rows, width),) * half,
        [pltpu.VMEM((half, 6 * rows, width), jnp.bfloat16)], COST,
        lin_x, lin_dq, lin_made, late_state,
    )
    lin_back = exchanged(lin_made)
    soft_out = call(
        "unpack_soft", bind(unpack_soft_kernel, half), mine, [turned], COST, soft_back
    )
    lin_out = call("unpack_lin", bind(unpack_lin_kernel, half), mine, [turned], COST, *lin_back)
    return (*lin_out, *soft_out)


def layers(
    lin_q,
    lin_k,
    lin_v,
    lin_decay,
    norm_gain,
    soft_q,
    soft_k,
    soft_v,
    out_grad,
    block_lists,
    block_counts,
):
    spans = lax.axis_size("ctx")
    if (
        lin_q.shape[0] == BLK
        and spans - 1 <= NSEL
        and lin_q.shape[1] == spans
        and spans >= 4
        and spans & (spans - 1) == 0
    ):
        return by_halves(
            lin_q, lin_k, lin_v, lin_decay, norm_gain, soft_q, soft_k, soft_v, out_grad
        )
    return local(
        lin_q,
        lin_k,
        lin_v,
        lin_decay,
        norm_gain,
        soft_q,
        soft_k,
        soft_v,
        out_grad,
        block_lists,
        block_counts,
    )


def solution(mesh):
    in_specs = (
        P("ctx", "head", None),
        P("ctx", "head", None),
        P("ctx", "head", None),
        P("head", "ctx"),
        P("head", None),
        P("ctx", "head", None),
        P("ctx", "head", None),
        P("ctx", "head", None),
        P("ctx", "head", None),
        P("ctx", None),
        P("ctx"),
    )
    out_specs = (
        P("ctx", "head", None),
        P("ctx", "head", None),
        P("ctx", "head", None),
        P("ctx", "head", None),
        P("ctx", "head", None),
        P("ctx", "head", None),
    )
    return jax.shard_map(layers, mesh=mesh, in_specs=in_specs, out_specs=out_specs, check_vma=False)
```

profile of v0, /device:TPU:0, one launch (start us, length us, event | category | flops | bytes accessed | tf_op | source)
XLA Modules:
  0.0 91.5 jit_solution(8340665710655572158)
XLA Ops:
  0.6 2.6 %pack_soft.1 = bf16[8,512,128]{2,1,0:T(8,128)(2,1)} custom-call(bf16[128,8,128]{2,1,0:T(8,128)(2,1)} %refs_0_.3, bf16[128,8,128]{2,1,0:T(8,128)(2,1)} %refs_1_.3, bf16[128,8,128]{2,1,0:T(8,128)(2,1)} %refs_2_.3, bf16[128,8,128]{2,1,0:T(8,128)(2,1)} %refs_3_.3), custom_call_target="tpu_custom_call" | custom-call | flops 11960000512 | bytes 1024 | tf_op jit(solution)/shard_map/pack_soft/pack_soft/pallas_call | solution.py:586
  3.3 7.4 %all-to-all-start = ((bf16[8,512,128]{2,1,0:T(8,128)(2,1)}), bf16[8,512,128]{2,1,0:T(8,128)(2,1)S(1)}, u32[]{:S(2)}, u32[]{:S(2)}) async-start(bf16[8,512,128]{2,1,0:T(8,128)(2,1)} %pack_soft.1), calls=%async_computation | async-start | bytes 2097152 | tf_op jit(solution)/shard_map/all_to_all | solution.py:626
  11.1 2.1 %collective-permute-start = (bf16[800,128]{1,0:T(8,128)(2,1)S(1)}, bf16[800,128]{1,0:T(8,128)(2,1)S(1)}, u32[]{:S(2)}, u32[]{:S(2)}) collective-permute-start(bf16[800,128]{1,0:T(8,128)(2,1)S(1)} %get-tuple-element.44), channel_id=1, source_target_pairs={{0,4},{4,0},{8,12},{12,8},{16,20},{20,16},{24,28},{28,24},{1,5},{5... | collective-permute-start | bytes 614408 | tf_op jit(solution)/shard_map/ppermute | solution.py:610
  13.2 1.5 %collective-permute-start.1 = (bf16[800,128]{1,0:T(8,128)(2,1)S(1)}, bf16[800,128]{1,0:T(8,128)(2,1)S(1)}, u32[]{:S(2)}, u32[]{:S(2)}) collective-permute-start(bf16[800,128]{1,0:T(8,128)(2,1)S(1)} %get-tuple-element.45), channel_id=1, source_target_pairs={{0,8},{4,12},{8,0},{12,4},{16,24},{20,28},{24,16},{28,20},{1,9},{5... | collective-permute-start | bytes 614408 | tf_op jit(solution)/shard_map/ppermute | solution.py:610
  14.8 21.8 %all-to-all-done.x_ref = bf16[8,512,128]{2,1,0:T(8,128)(2,1)S(1)} async-done(((bf16[8,512,128]{2,1,0:T(8,128)(2,1)}), bf16[8,512,128]{2,1,0:T(8,128)(2,1)S(1)}, u32[]{:S(2)}, u32[]{:S(2)}) %all-to-all-start) | async-done | bytes 1048608 | tf_op jit(solution)/shard_map/all_to_all | solution.py:626
  36.6 2.2 %soft_forward.1 = (f32[8,1024]{1,0:T(8,128)S(1)}, bf16[8,128,128]{2,1,0:T(8,128)(2,1)S(1)}, f32[512,128]{1,0:T(8,128)S(1)}, bf16[512,128]{1,0:T(8,128)(2,1)S(1)}) custom-call(bf16[8,512,128]{2,1,0:T(8,128)(2,1)S(1)} %all-to-all-done.x_ref), custom_call_target="tpu_custom_call" | custom-call | flops 1024 | bytes 1024 | tf_op jit(solution)/shard_map/soft_forward/soft_forward/pallas_call | solution.py:586
  39.6 3.0 %lin_local.1 = (bf16[4,800,128]{2,1,0:T(8,128)(2,1)S(1)}, f32[2,4,128,128]{3,2,1,0:T(8,128)S(1)}, bf16[2,4,128,128]{3,2,1,0:T(8,128)(2,1)S(1)}, bf16[2,128,128]{2,1,0:T(8,128)(2,1)S(1)}) custom-call(bf16[800,128]{1,0:T(8,128)(2,1)S(1)} %get-tuple-element.43.refs_0_, bf16[800,128]{1,0:T(8,128)(2,1)S(1)} %collective-permute-done.refs_1_, ...), custom_call_target="tpu_custom_call" | custom-call | flops 13340000256 | bytes 1024 | tf_op jit(solution)/shard_map/lin_local/lin_local/pallas_call | solution.py:586
  42.6 4.3 %collective-permute-start.4 = (bf16[2,128,128]{2,1,0:T(8,128)(2,1)S(1)}, bf16[2,128,128]{2,1,0:T(8,128)(2,1)S(1)}, u32[]{:S(2)}, u32[]{:S(2)}) collective-permute-start(bf16[2,128,128]{2,1,0:T(8,128)(2,1)S(1)} %get-tuple-element.54), channel_id=1, source_target_pairs={{0,16},{4,20},{8,24},{12,28},{1,17},{5,21},{9,25},{13,29},{2,18},{... | collective-permute-start | bytes 196616 | tf_op jit(solution)/shard_map/ppermute | solution.py:610
  46.9 3.6 %soft_backward.1 = bf16[8,384,128]{2,1,0:T(8,128)(2,1)} custom-call(bf16[8,512,128]{2,1,0:T(8,128)(2,1)S(1)} %all-to-all-done.x_ref, f32[8,1024]{1,0:T(8,128)S(1)} %get-tuple-element.50.lines_ref, bf16[8,128,128]{2,1,0:T(8,128)(2,1)S(1)} %get-tuple-element.51.dv_ref), custom_call_target="tpu_custom_call" | custom-call | flops 16560000000 | bytes 1024 | tf_op jit(solution)/shard_map/soft_backward/soft_backward/pallas_call | solution.py:586
  50.4 1.2 %lin_sums.1 = (f32[2,4,128,128]{3,2,1,0:T(8,128)S(1)}, f32[2,4,128,128]{3,2,1,0:T(8,128)S(1)}, f32[8,128]{1,0:T(8,128)S(1)}) custom-call(bf16[4,800,128]{2,1,0:T(8,128)(2,1)S(1)} %get-tuple-element.47.x_ref, f32[512,128]{1,0:T(8,128)S(1)} %get-tuple-element.48.own_ref, bf16[512,128]{1,0:T(8,128)(2,1)S(1)} %collective-permute-done.3.far_ref, ...), custom_call_target="tpu_custom_call" | custom-call | flops 1024 | bytes 1024 | tf_op jit(solution)/shard_map/lin_sums/lin_sums/pallas_call | solution.py:586
  51.6 3.6 %all-to-all-start.1 = ((bf16[8,384,128]{2,1,0:T(8,128)(2,1)}), bf16[8,384,128]{2,1,0:T(8,128)(2,1)S(1)}, u32[]{:S(2)}, u32[]{:S(2)}) async-start(bf16[8,384,128]{2,1,0:T(8,128)(2,1)} %soft_backward.1), calls=%async_computation.1 | async-start | bytes 1572864 | tf_op jit(solution)/shard_map/all_to_all | solution.py:662
  55.3 1.6 %collective-permute-start.6 = (f32[8,128]{1,0:T(8,128)S(1)}, f32[8,128]{1,0:T(8,128)S(1)}, u32[]{:S(2)}, u32[]{:S(2)}) collective-permute-start(f32[8,128]{1,0:T(8,128)S(1)} %get-tuple-element.59), channel_id=1, source_target_pairs={{0,2},{1,3},{2,0},{3,1},{4,6},{5,7},{6,4},{7,5},{8,10},{9,11},{10,... | collective-permute-start | bytes 12296 | tf_op jit(solution)/shard_map/ppermute | solution.py:667
  57.1 1.2 %collective-permute-done.7 = f32[8,128]{1,0:T(8,128)S(1)} collective-permute-done((f32[8,128]{1,0:T(8,128)S(1)}, f32[8,128]{1,0:T(8,128)S(1)}, u32[]{:S(2)}, u32[]{:S(2)}) %collective-permute-start.7) | collective-permute-done | bytes 4128 | tf_op jit(solution)/shard_map/ppermute | solution.py:667
  59.0 2.9 %collective-permute-start.10 = (f32[8,128]{1,0:T(8,128)S(1)}, f32[8,128]{1,0:T(8,128)S(1)}, u32[]{:S(2)}, u32[]{:S(2)}) collective-permute-start(f32[8,128]{1,0:T(8,128)S(1)} %add_add_fusion.1), channel_id=1, source_target_pairs={{0,12},{4,8},{8,4},{12,0},{16,28},{20,24},{24,20},{28,16},{1,13},{... | collective-permute-start | bytes 12296 | tf_op jit(solution)/shard_map/ppermute | solution.py:667
  62.5 4.9 %collective-permute-done.10 = f32[8,128]{1,0:T(8,128)S(1)} collective-permute-done((f32[8,128]{1,0:T(8,128)S(1)}, f32[8,128]{1,0:T(8,128)S(1)}, u32[]{:S(2)}, u32[]{:S(2)}) %collective-permute-start.10) | collective-permute-done | bytes 4128 | tf_op jit(solution)/shard_map/ppermute | solution.py:667
  67.4 1.5 %lin_cot.1 = (bf16[2,4,128,128]{3,2,1,0:T(8,128)(2,1)S(1)}, bf16[2,128,128]{2,1,0:T(8,128)(2,1)S(1)}) custom-call(bf16[4,800,128]{2,1,0:T(8,128)(2,1)S(1)} %get-tuple-element.47.x_ref, f32[2,4,128,128]{3,2,1,0:T(8,128)S(1)} %get-tuple-element.55.cot_ref, f32[2,4,128,128]{3,2,1,0:T(8,128)S(1)} %get-tuple-element.56.out_ref, f32[8,128]{1,0:T(8,128)S(1)} %add_add_fusion.sums_ref), custom_call_target="tpu_custom_call" | custom-call | flops 1024 | bytes 1024 | tf_op jit(solution)/shard_map/lin_cot/lin_cot/pallas_call | solution.py:586
  69.0 1.5 %collective-permute-start.11 = (bf16[2,128,128]{2,1,0:T(8,128)(2,1)S(1)}, bf16[2,128,128]{2,1,0:T(8,128)(2,1)S(1)}, u32[]{:S(2)}, u32[]{:S(2)}) collective-permute-start(bf16[2,128,128]{2,1,0:T(8,128)(2,1)S(1)} %get-tuple-element.64), channel_id=1, source_target_pairs={{16,0},{20,4},{24,8},{28,12},{17,1},{21,5},{25,9},{29,13},{18,2},{... | collective-permute-start | bytes 196616 | tf_op jit(solution)/shard_map/ppermute | solution.py:610
  70.4 3.3 %lin_own.1 = (bf16[2,4,128,128]{3,2,1,0:T(8,128)(2,1)S(1)}, f32[2,2,4,128,128]{4,3,2,1,0:T(8,128)S(1)}) custom-call(bf16[4,800,128]{2,1,0:T(8,128)(2,1)S(1)} %get-tuple-element.47.x_ref, bf16[2,4,128,128]{3,2,1,0:T(8,128)(2,1)S(1)} %get-tuple-element.60.low_ref, bf16[2,4,128,128]{3,2,1,0:T(8,128)(2,1)S(1)} %get-tuple-element.61.states_ref, ...), custom_call_target="tpu_custom_call" | custom-call | flops 1024 | bytes 1024 | tf_op jit(solution)/shard_map/lin_own/lin_own/pallas_call | solution.py:586
  73.7 4.2 %collective-permute-done.11.state_ref = bf16[2,128,128]{2,1,0:T(8,128)(2,1)S(1)} collective-permute-done((bf16[2,128,128]{2,1,0:T(8,128)(2,1)S(1)}, bf16[2,128,128]{2,1,0:T(8,128)(2,1)S(1)}, u32[]{:S(2)}, u32[]{:S(2)}) %collective-permute-start.11) | collective-permute-done | bytes 65568 | tf_op jit(solution)/shard_map/ppermute | solution.py:610
  79.6 1.7 %collective-permute-start.13 = (bf16[768,128]{1,0:T(8,128)(2,1)S(1)}, bf16[768,128]{1,0:T(8,128)(2,1)S(1)}, u32[]{:S(2)}, u32[]{:S(2)}) collective-permute-start(bf16[768,128]{1,0:T(8,128)(2,1)S(1)} %get-tuple-element.67), channel_id=1, source_target_pairs={{0,8},{4,12},{8,0},{12,4},{16,24},{20,28},{24,16},{28,20},{1,9},{5... | collective-permute-start | bytes 589832 | tf_op jit(solution)/shard_map/ppermute | solution.py:610
  81.2 1.2 %collective-permute-start.14 = (bf16[768,128]{1,0:T(8,128)(2,1)S(1)}, bf16[768,128]{1,0:T(8,128)(2,1)S(1)}, u32[]{:S(2)}, u32[]{:S(2)}) collective-permute-start(bf16[768,128]{1,0:T(8,128)(2,1)S(1)} %get-tuple-element.68), channel_id=1, source_target_pairs={{0,12},{4,8},{8,4},{12,0},{16,28},{20,24},{24,20},{28,16},{1,13},{... | collective-permute-start | bytes 589832 | tf_op jit(solution)/shard_map/ppermute | solution.py:610
  82.4 4.3 %collective-permute-done.12.refs_1_ = bf16[768,128]{1,0:T(8,128)(2,1)S(1)} collective-permute-done((bf16[768,128]{1,0:T(8,128)(2,1)S(1)}, bf16[768,128]{1,0:T(8,128)(2,1)S(1)}, u32[]{:S(2)}, u32[]{:S(2)}) %collective-permute-start.12) | collective-permute-done | bytes 196640 | tf_op jit(solution)/shard_map/ppermute | solution.py:610
  86.8 2.2 %collective-permute-done.14.refs_3_ = bf16[768,128]{1,0:T(8,128)(2,1)S(1)} collective-permute-done((bf16[768,128]{1,0:T(8,128)(2,1)S(1)}, bf16[768,128]{1,0:T(8,128)(2,1)S(1)}, u32[]{:S(2)}, u32[]{:S(2)}) %collective-permute-start.14) | collective-permute-done | bytes 196640 | tf_op jit(solution)/shard_map/ppermute | solution.py:610
  89.0 1.3 %unpack_lin.1 = (bf16[128,8,128]{2,1,0:T(8,128)(2,1)}, bf16[128,8,128]{2,1,0:T(8,128)(2,1)}, bf16[128,8,128]{2,1,0:T(8,128)(2,1)}) custom-call(bf16[768,128]{1,0:T(8,128)(2,1)S(1)} %get-tuple-element.65.refs_0_, bf16[768,128]{1,0:T(8,128)(2,1)S(1)} %collective-permute-done.12.refs_1_, bf16[768,128]{1,0:T(8,128)(2,1)S(1)} %collective-permute-done.13.refs_2_, ...), custom_call_target="tpu_custom_call" | custom-call | flops 1024 | bytes 1024 | tf_op jit(solution)/shard_map/unpack_lin/unpack_lin/pallas_call | solution.py:586
  (33 shorter events, 5.8 us)
Async XLA Ops:
  3.3 7.5 %copy-start = (bf16[128,8,128]{2,1,0:T(8,128)(2,1)S(1)}, bf16[128,8,128]{2,1,0:T(8,128)(2,1)}, u32[]{:S(2)}) copy-start(bf16[128,8,128]{2,1,0:T(8,128)(2,1)} %refs_0_.2) | copy-start | bytes 786436
  3.3 7.5 %copy-start.1 = (bf16[128,8,128]{2,1,0:T(8,128)(2,1)S(1)}, bf16[128,8,128]{2,1,0:T(8,128)(2,1)}, u32[]{:S(2)}) copy-start(bf16[128,8,128]{2,1,0:T(8,128)(2,1)} %refs_1_.2) | copy-start | bytes 786436
  3.3 7.5 %copy-start.2 = (bf16[128,8,128]{2,1,0:T(8,128)(2,1)S(1)}, bf16[128,8,128]{2,1,0:T(8,128)(2,1)}, u32[]{:S(2)}) copy-start(bf16[128,8,128]{2,1,0:T(8,128)(2,1)} %refs_2_.2) | copy-start | bytes 786436
  3.3 7.5 %copy-start.3 = (f32[8,128]{1,0:T(8,128)S(1)}, f32[8,128]{1,0:T(8,128)}, u32[]{:S(2)}) copy-start(f32[8,128]{1,0:T(8,128)} %refs_3_.2) | copy-start | bytes 12292
  3.3 7.5 %copy-start.4 = (f32[8,128]{1,0:T(8,128)S(1)}, f32[8,128]{1,0:T(8,128)}, u32[]{:S(2)}) copy-start(f32[8,128]{1,0:T(8,128)} %refs_4_.1) | copy-start | bytes 12292
  3.3 33.3 %all-to-all-start = ((bf16[8,512,128]{2,1,0:T(8,128)(2,1)}), bf16[8,512,128]{2,1,0:T(8,128)(2,1)S(1)}, u32[]{:S(2)}, u32[]{:S(2)}) async-start(bf16[8,512,128]{2,1,0:T(8,128)(2,1)} %pack_soft.1), calls=%async_computation | async-start | bytes 2097152 | tf_op jit(solution)/shard_map/all_to_all | solution.py:626
  11.1 27.8 %collective-permute-start = (bf16[800,128]{1,0:T(8,128)(2,1)S(1)}, bf16[800,128]{1,0:T(8,128)(2,1)S(1)}, u32[]{:S(2)}, u32[]{:S(2)}) collective-permute-start(bf16[800,128]{1,0:T(8,128)(2,1)S(1)} %get-tuple-element.44), channel_id=1, source_target_pairs={{0,4},{4,0},{8,12},{12,8},{16,20},{20,16},{24,28},{28,24},{1,5},{5... | collective-permute-start | bytes 614408 | tf_op jit(solution)/shard_map/ppermute | solution.py:610
  13.2 25.7 %collective-permute-start.1 = (bf16[800,128]{1,0:T(8,128)(2,1)S(1)}, bf16[800,128]{1,0:T(8,128)(2,1)S(1)}, u32[]{:S(2)}, u32[]{:S(2)}) collective-permute-start(bf16[800,128]{1,0:T(8,128)(2,1)S(1)} %get-tuple-element.45), channel_id=1, source_target_pairs={{0,8},{4,12},{8,0},{12,4},{16,24},{20,28},{24,16},{28,20},{1,9},{5... | collective-permute-start | bytes 614408 | tf_op jit(solution)/shard_map/ppermute | solution.py:610
  14.7 24.9 %collective-permute-start.2 = (bf16[800,128]{1,0:T(8,128)(2,1)S(1)}, bf16[800,128]{1,0:T(8,128)(2,1)S(1)}, u32[]{:S(2)}, u32[]{:S(2)}) collective-permute-start(bf16[800,128]{1,0:T(8,128)(2,1)S(1)} %get-tuple-element.46), channel_id=1, source_target_pairs={{0,12},{4,8},{8,4},{12,0},{16,28},{20,24},{24,20},{28,16},{1,13},{... | collective-permute-start | bytes 614408 | tf_op jit(solution)/shard_map/ppermute | solution.py:610
  38.8 11.6 %collective-permute-start.3 = (bf16[512,128]{1,0:T(8,128)(2,1)S(1)}, bf16[512,128]{1,0:T(8,128)(2,1)S(1)}, u32[]{:S(2)}, u32[]{:S(2)}) collective-permute-start(bf16[512,128]{1,0:T(8,128)(2,1)S(1)} %get-tuple-element.49), channel_id=1, source_target_pairs={{0,16},{4,20},{8,24},{12,28},{16,0},{20,4},{24,8},{28,12},{1,17},{... | collective-permute-start | bytes 393224 | tf_op jit(solution)/shard_map/ppermute | solution.py:610
  42.6 7.9 %collective-permute-start.4 = (bf16[2,128,128]{2,1,0:T(8,128)(2,1)S(1)}, bf16[2,128,128]{2,1,0:T(8,128)(2,1)S(1)}, u32[]{:S(2)}, u32[]{:S(2)}) collective-permute-start(bf16[2,128,128]{2,1,0:T(8,128)(2,1)S(1)} %get-tuple-element.54), channel_id=1, source_target_pairs={{0,16},{4,20},{8,24},{12,28},{1,17},{5,21},{9,25},{13,29},{2,18},{... | collective-permute-start | bytes 196616 | tf_op jit(solution)/shard_map/ppermute | solution.py:610
  51.6 38.7 %all-to-all-start.1 = ((bf16[8,384,128]{2,1,0:T(8,128)(2,1)}), bf16[8,384,128]{2,1,0:T(8,128)(2,1)S(1)}, u32[]{:S(2)}, u32[]{:S(2)}) async-start(bf16[8,384,128]{2,1,0:T(8,128)(2,1)} %soft_backward.1), calls=%async_computation.1 | async-start | bytes 1572864 | tf_op jit(solution)/shard_map/all_to_all | solution.py:662
  55.2 3.1 %collective-permute-start.7 = (f32[8,128]{1,0:T(8,128)S(1)}, f32[8,128]{1,0:T(8,128)S(1)}, u32[]{:S(2)}, u32[]{:S(2)}) collective-permute-start(f32[8,128]{1,0:T(8,128)S(1)} %get-tuple-element.59), channel_id=1, source_target_pairs={{0,3},{1,2},{2,1},{3,0},{4,7},{5,6},{6,5},{7,4},{8,11},{9,10},{10,... | collective-permute-start | bytes 12296 | tf_op jit(solution)/shard_map/ppermute | solution.py:667
  55.3 3.7 %collective-permute-start.6 = (f32[8,128]{1,0:T(8,128)S(1)}, f32[8,128]{1,0:T(8,128)S(1)}, u32[]{:S(2)}, u32[]{:S(2)}) collective-permute-start(f32[8,128]{1,0:T(8,128)S(1)} %get-tuple-element.59), channel_id=1, source_target_pairs={{0,2},{1,3},{2,0},{3,1},{4,6},{5,7},{6,4},{7,5},{8,10},{9,11},{10,... | collective-permute-start | bytes 12296 | tf_op jit(solution)/shard_map/ppermute | solution.py:667
  56.8 2.1 %collective-permute-start.5 = (f32[8,128]{1,0:T(8,128)S(1)}, f32[8,128]{1,0:T(8,128)S(1)}, u32[]{:S(2)}, u32[]{:S(2)}) collective-permute-start(f32[8,128]{1,0:T(8,128)S(1)} %get-tuple-element.59), channel_id=1, source_target_pairs={{0,1},{1,0},{2,3},{3,2},{4,5},{5,4},{6,7},{7,6},{8,9},{9,8},{10,11... | collective-permute-start | bytes 12296 | tf_op jit(solution)/shard_map/ppermute | solution.py:667
  59.0 8.5 %collective-permute-start.10 = (f32[8,128]{1,0:T(8,128)S(1)}, f32[8,128]{1,0:T(8,128)S(1)}, u32[]{:S(2)}, u32[]{:S(2)}) collective-permute-start(f32[8,128]{1,0:T(8,128)S(1)} %add_add_fusion.1), channel_id=1, source_target_pairs={{0,12},{4,8},{8,4},{12,0},{16,28},{20,24},{24,20},{28,16},{1,13},{... | collective-permute-start | bytes 12296 | tf_op jit(solution)/shard_map/ppermute | solution.py:667
  61.8 5.6 %collective-permute-start.9 = (f32[8,128]{1,0:T(8,128)S(1)}, f32[8,128]{1,0:T(8,128)S(1)}, u32[]{:S(2)}, u32[]{:S(2)}) collective-permute-start(f32[8,128]{1,0:T(8,128)S(1)} %add_add_fusion.1), channel_id=1, source_target_pairs={{0,8},{4,12},{8,0},{12,4},{16,24},{20,28},{24,16},{28,20},{1,9},{5... | collective-permute-start | bytes 12296 | tf_op jit(solution)/shard_map/ppermute | solution.py:667
  62.4 5.0 %collective-permute-start.8 = (f32[8,128]{1,0:T(8,128)S(1)}, f32[8,128]{1,0:T(8,128)S(1)}, u32[]{:S(2)}, u32[]{:S(2)}) collective-permute-start(f32[8,128]{1,0:T(8,128)S(1)} %add_add_fusion.1), channel_id=1, source_target_pairs={{0,4},{4,0},{8,12},{12,8},{16,20},{20,16},{24,28},{28,24},{1,5},{5... | collective-permute-start | bytes 12296 | tf_op jit(solution)/shard_map/ppermute | solution.py:667
  69.0 9.0 %collective-permute-start.11 = (bf16[2,128,128]{2,1,0:T(8,128)(2,1)S(1)}, bf16[2,128,128]{2,1,0:T(8,128)(2,1)S(1)}, u32[]{:S(2)}, u32[]{:S(2)}) collective-permute-start(bf16[2,128,128]{2,1,0:T(8,128)(2,1)S(1)} %get-tuple-element.64), channel_id=1, source_target_pairs={{16,0},{20,4},{24,8},{28,12},{17,1},{21,5},{25,9},{29,13},{18,2},{... | collective-permute-start | bytes 196616 | tf_op jit(solution)/shard_map/ppermute | solution.py:610
  78.9 7.8 %collective-permute-start.12 = (bf16[768,128]{1,0:T(8,128)(2,1)S(1)}, bf16[768,128]{1,0:T(8,128)(2,1)S(1)}, u32[]{:S(2)}, u32[]{:S(2)}) collective-permute-start(bf16[768,128]{1,0:T(8,128)(2,1)S(1)} %get-tuple-element.66), channel_id=1, source_target_pairs={{0,4},{4,0},{8,12},{12,8},{16,20},{20,16},{24,28},{28,24},{1,5},{5... | collective-permute-start | bytes 589832 | tf_op jit(solution)/shard_map/ppermute | solution.py:610
  79.6 7.3 %collective-permute-start.13 = (bf16[768,128]{1,0:T(8,128)(2,1)S(1)}, bf16[768,128]{1,0:T(8,128)(2,1)S(1)}, u32[]{:S(2)}, u32[]{:S(2)}) collective-permute-start(bf16[768,128]{1,0:T(8,128)(2,1)S(1)} %get-tuple-element.67), channel_id=1, source_target_pairs={{0,8},{4,12},{8,0},{12,4},{16,24},{20,28},{24,16},{28,20},{1,9},{5... | collective-permute-start | bytes 589832 | tf_op jit(solution)/shard_map/ppermute | solution.py:610
  81.2 7.8 %collective-permute-start.14 = (bf16[768,128]{1,0:T(8,128)(2,1)S(1)}, bf16[768,128]{1,0:T(8,128)(2,1)S(1)}, u32[]{:S(2)}, u32[]{:S(2)}) collective-permute-start(bf16[768,128]{1,0:T(8,128)(2,1)S(1)} %get-tuple-element.68), channel_id=1, source_target_pairs={{0,12},{4,8},{8,4},{12,0},{16,28},{20,24},{24,20},{28,16},{1,13},{... | collective-permute-start | bytes 589832 | tf_op jit(solution)/shard_map/ppermute | solution.py:610
where the time goes:
time: 91.8 us; the launch traced here: 91.5 us
  waiting for transfers between devices  40 us (44%)
  starting transfers between devices  29.5 us (32%)
  Pallas kernels  21.1 us (23%)
    all_to_all x1, waiting for transfers between devices, by_halves(): x = lax.all_to_all(soft_sent, 'ctx', 0, 0, tiled=True)  21.8 us
    pallas_call x11, Pallas kernels, call(): pl.pallas_call(kernel, out_shape=out_shape, scratch_shapes=scratch, name=...  21.1 us
    ppermute x9, starting transfers between devices, moved(): return lax.ppermute(x, 'ctx', pairs)  13 us
    ppermute x9, waiting for transfers between devices, moved(): return lax.ppermute(x, 'ctx', pairs)  11.5 us
    all_to_all x1, starting transfers between devices, by_halves(): x = lax.all_to_all(soft_sent, 'ctx', 0, 0, tiled=True)  7.42 us
    ppermute x6, waiting for transfers between devices, by_halves(): lax.ppermute(sums, axis, [(i, i ^ step) for i in range(count)])  6.7 us
    ppermute x6, starting transfers between devices, by_halves(): lax.ppermute(sums, axis, [(i, i ^ step) for i in range(count)])  5.5 us
    all_to_all x1, starting transfers between devices, by_halves(): soft_back = lax.all_to_all(soft_made, 'ctx', 0, 0, tiled=True)  3.56 us
  transfers between devices with their start and end apart: 17, of which 9 were waited for; matrix products, arithmetic and copies ran while one was open for 0% of the time, Pallas kernels for 18%

commit v1 on v0

--- a/solution.py
+++ b/solution.py
@@ -284,14 +284,16 @@
 
 
 def pack_soft_kernel(half, *refs):
-    sources, sent, scratch = refs[:4], refs[4], refs[5]
+    sources, outs, scratches = refs[:4], refs[4 : 4 + 2 * half], refs[4 + 2 * half :]
     rows, heads, _ = sources[0].shape
-    for place, source in enumerate(sources):
+    me = lax.axis_index("ctx")
+    for source, scratch in zip(sources, scratches):
         spread(source, scratch)
-        for dest in range(2 * half):
-            sent[dest, pl.ds(place * rows, rows), :] = head_of(
-                scratch, soft_head(dest, half), heads
-            ).astype(jnp.bfloat16)
+    for step, out in enumerate(outs):
+        dest = jnp.bitwise_xor(me, step)
+        head = jnp.where(dest < half, 2 * dest, 2 * (dest - half) + 1)
+        for place, scratch in enumerate(scratches):
+            out[pl.ds(place * rows, rows), :] = head_of(scratch, head, heads).astype(jnp.bfloat16)
 
 
 def put_heads(half, outs, scratch, first, second, rows, heads):
@@ -373,7 +375,11 @@
     return jnp.where(key_at <= query_at, scores, -1e30)
 
 
-def soft_forward_kernel(half, x_ref, lines_ref, dv_ref, own_ref, give_ref, scr, total_scr):
+def soft_forward_kernel(half, *refs):
+    steps, refs = refs[: 2 * half], refs[2 * half :]
+    x_ref, lines_ref, dv_ref, own_ref, give_ref, scr, total_scr = refs
+    for step, ref in enumerate(steps):
+        x_ref[jnp.bitwise_xor(lax.axis_index("ctx"), step)] = ref[...]
     late = later(half)
     spans, rows, width = dv_ref.shape
     wide, scale = GROUP * rows, width**-0.5
@@ -491,7 +497,8 @@
 
 
 def lin_sums_kernel(half, rows, x_ref, own_ref, far_ref, local_ref, given_ref, cot_ref, out_ref, sums_ref):
-    before = [jnp.zeros((1, 1), jnp.float32)] * 2
+    late = later(half)
+    before = [jnp.where(late, jnp.zeros((1, 1), jnp.float32), -1e30)] * 2
     for span in range(half):
         at = pl.ds(span * rows, rows)
         inner, squares = None, None
@@ -538,7 +545,7 @@
         for span in range(half):
             finish = span_tables(lin_parts(x_ref, slot, span, rows)[3])[2]
             before.append(before[-1] + finish)
-        given = given_ref[slot].astype(jnp.float32)
+        given = jnp.where(later(half), given_ref[slot].astype(jnp.float32), 0.0)
         state = jnp.zeros((width, width), jnp.float32)
         for span in reversed(range(half)):
             q, k, v, extra = lin_parts(x_ref, slot, span, rows)
@@ -565,7 +572,7 @@
     outs, packed = refs[:half], refs[half]
     for slot in range(2):
         state = state_ref[slot]
-        after = jnp.zeros((1, 1), jnp.float32)
+        after = jnp.where(later(half), -1e30, jnp.zeros((1, 1), jnp.float32))
         for span in reversed(range(half)):
             _, k, v, extra = lin_parts(x_ref, slot, span, rows)
             _, col, finish, _, _ = span_tables(extra)
@@ -611,29 +618,33 @@
 
     def exchanged(parts):
         return [parts[0]] + [
-            moved(parts[step], [(i, i ^ step) for i in range(spans)]) for step in range(1, half)
+            moved(parts[step], [(i, i ^ step) for i in range(spans)]) for step in range(1, len(parts))
         ]
 
     both = [(i, i ^ half) for i in range(spans)]
-    up = [(i, i + half) for i in range(half)]
-    down = [(i + half, i) for i in range(half)]
     turned = held(rows * heads, width)
     mine = (low(rows, heads, width),) * 3
     soft_sent = call(
-        "pack_soft", bind(pack_soft_kernel, half), low(spans, 4 * rows, width), [turned], 11960000000,
+        "pack_soft", bind(pack_soft_kernel, half), (low(4 * rows, width),) * spans, [turned] * 4, 11960000000,
         soft_q, soft_k, soft_v, out_grad,
     )
-    x = lax.all_to_all(soft_sent, "ctx", 0, 0, tiled=True)
+    soft_got = exchanged(soft_sent)
     lin_sent = call(
         "pack_lin", bind(pack_lin_kernel, half), (low(6 * rows + 2 * PAD, width),) * half,
         [turned] * 3 + [held(6 * heads, width)], 5980000000,
         lin_q, lin_k, lin_v, lin_decay, norm_gain,
     )
     lin_got = exchanged(lin_sent)
-    lines, dv, own, give = call(
+    x, lines, dv, own, give = call(
         "soft_forward", bind(soft_forward_kernel, half),
-        (full(8, spans * rows), low(spans, rows, width), full(tokens, width), low(tokens, width)),
-        [held(tiles, wide, wide), held(tiles, wide, width)], COST, x,
+        (
+            low(spans, 4 * rows, width),
+            full(8, spans * rows),
+            low(spans, rows, width),
+            full(tokens, width),
+            low(tokens, width),
+        ),
+        [held(tiles, wide, wide), held(tiles, wide, width)], COST, *soft_got,
     )
     far = moved(give, both)
     lin_got[0], own = after((lin_got[0], own))
@@ -647,7 +658,7 @@
         ),
         [], 13340000000, *lin_got,
     )
-    state = moved(state, up)
+    state = moved(state, both)
     soft_made = call(
         "soft_backward", soft_backward_kernel, low(spans, 3 * rows, width),
         [held(tiles, wide, width)], 16560000000, x, lines, dv,
@@ -672,7 +683,7 @@
         (low(2, half, rows, width), low(2, width, width)), [], COST,
         lin_x, cot, layer_out, sums,
     )
-    late_state = moved(late_state, down)
+    late_state = moved(late_state, both)
     lin_dq, lin_made = call(
         "lin_own", bind(lin_own_kernel, half, rows),
         (low(2, half, rows, width), full(2, 2, half, rows, width)), [], COST,
@@ -685,8 +696,10 @@
     )
     lin_back = exchanged(lin_made)
     soft_out = call(
-        "unpack_soft", bind(unpack_soft_kernel, half), mine, [turned], COST, soft_back
-    )
+        "unpack_soft", bind(unpack_soft_kernel, half), mine, [turned], 4600000000, soft_back
+    )
+    soft_out = list(soft_out)
+    lin_back[0], soft_out[0] = after((lin_back[0], soft_out[0]))
     lin_out = call("unpack_lin", bind(unpack_lin_kernel, half), mine, [turned], COST, *lin_back)
     return (*lin_out, *soft_out)
 

time: 91.8 us -> 88 us (0.959)
  waiting for transfers between devices: 40 us -> 26.9 us
  starting transfers between devices: 29.5 us -> 38.7 us
    all_to_all x1 -> x0, waiting for transfers between devices: 21.8 us -> none  [by_halves(): x = lax.all_to_all(soft_sent, 'ctx', 0, 0, tiled=True)]
    ppermute x9 -> x16, starting transfers between devices: 13 us -> 29.5 us  [moved(): return lax.ppermute(x, 'ctx', pairs)]
    ppermute x9 -> x16, waiting for transfers between devices: 11.5 us -> 20.2 us  [moved(): return lax.ppermute(x, 'ctx', pairs)]
    all_to_all x1 -> x0, starting transfers between devices: 7.42 us -> none  [by_halves(): x = lax.all_to_all(soft_sent, 'ctx', 0, 0, tiled=True)]
  transfers between devices with their start and end apart: 17 -> 23, of which waited for: 9 -> 10; matrix products, arithmetic and copies ran while one was open for 0% -> 0% of each run, Pallas kernels for 18% -> 18%
where the time goes in v1:
time: 88 us; the launch traced here: 87.8 us
  starting transfers between devices  38.7 us (44%)
  waiting for transfers between devices  26.9 us (31%)
  Pallas kernels  21.3 us (24%)
    ppermute x16, starting transfers between devices, moved(): return lax.ppermute(x, 'ctx', pairs)  29.5 us
    pallas_call x11, Pallas kernels, call(): pl.pallas_call(kernel, out_shape=out_shape, scratch_shapes=scratch, name=...  21.3 us
    ppermute x16, waiting for transfers between devices, moved(): return lax.ppermute(x, 'ctx', pairs)  20.2 us
    ppermute x6, waiting for transfers between devices, by_halves(): lax.ppermute(sums, axis, [(i, i ^ step) for i in range(count)])  6.71 us
    ppermute x6, starting transfers between devices, by_halves(): lax.ppermute(sums, axis, [(i, i ^ step) for i in range(count)])  5.47 us
    all_to_all x1, starting transfers between devices, by_halves(): soft_back = lax.all_to_all(soft_made, 'ctx', 0, 0, tiled=True)  3.74 us
  transfers between devices with their start and end apart: 23, of which 10 were waited for; matrix products, arithmetic and copies ran while one was open for 0% of the time, Pallas kernels for 18%

profile of v1, /device:TPU:0, one launch (start us, length us, event | category | flops | bytes accessed | tf_op | source)
XLA Modules:
  0.0 87.8 jit_solution(211076547789886366)
XLA Ops:
  0.7 2.7 %pack_soft.1 = (bf16[512,128]{1,0:T(8,128)(2,1)}, bf16[512,128]{1,0:T(8,128)(2,1)}, bf16[512,128]{1,0:T(8,128)(2,1)}, bf16[512,128]{1,0:T(8,128)(2,1)}, bf16[512...) custom-call(bf16[128,8,128]{2,1,0:T(8,128)(2,1)} %refs_0_.3, ...), custom_call_target="tpu_custom_call" | custom-call | flops 11960000512 | bytes 1024 | tf_op jit(solution)/shard_map/pack_soft/pack_soft/pallas_call | solution.py:593
  3.4 3.0 %collective-permute-start = (bf16[512,128]{1,0:T(8,128)(2,1)}, bf16[512,128]{1,0:T(8,128)(2,1)S(1)}, u32[]{:S(2)}, u32[]{:S(2)}) collective-permute-start(bf16[512,128]{1,0:T(8,128)(2,1)} %get-tuple-element.54), channel_id=1, source_target_pairs={{0,4},{4,0},{8,12},{12,8},{16,20},{20,16},{24,28},{28,24},{1,5},{5... | collective-permute-start | bytes 393224 | tf_op jit(solution)/shard_map/ppermute | solution.py:617
  6.4 1.6 %collective-permute-start.1 = (bf16[512,128]{1,0:T(8,128)(2,1)}, bf16[512,128]{1,0:T(8,128)(2,1)S(1)}, u32[]{:S(2)}, u32[]{:S(2)}) collective-permute-start(bf16[512,128]{1,0:T(8,128)(2,1)} %get-tuple-element.55), channel_id=1, source_target_pairs={{0,8},{4,12},{8,0},{12,4},{16,24},{20,28},{24,16},{28,20},{1,9},{5... | collective-permute-start | bytes 393224 | tf_op jit(solution)/shard_map/ppermute | solution.py:617
  8.0 3.0 %collective-permute-start.3 = (bf16[512,128]{1,0:T(8,128)(2,1)}, bf16[512,128]{1,0:T(8,128)(2,1)S(1)}, u32[]{:S(2)}, u32[]{:S(2)}) collective-permute-start(bf16[512,128]{1,0:T(8,128)(2,1)} %get-tuple-element.57), channel_id=1, source_target_pairs={{0,16},{4,20},{8,24},{12,28},{16,0},{20,4},{24,8},{28,12},{1,17},{... | collective-permute-start | bytes 393224 | tf_op jit(solution)/shard_map/ppermute | solution.py:617
  11.0 1.3 %collective-permute-start.4 = (bf16[512,128]{1,0:T(8,128)(2,1)}, bf16[512,128]{1,0:T(8,128)(2,1)S(1)}, u32[]{:S(2)}, u32[]{:S(2)}) collective-permute-start(bf16[512,128]{1,0:T(8,128)(2,1)} %get-tuple-element.58), channel_id=1, source_target_pairs={{0,20},{4,16},{8,28},{12,24},{16,4},{20,0},{24,12},{28,8},{1,21},{... | collective-permute-start | bytes 393224 | tf_op jit(solution)/shard_map/ppermute | solution.py:617
  13.0 4.9 %collective-permute-done.1.refs_2_ = bf16[512,128]{1,0:T(8,128)(2,1)S(1)} collective-permute-done((bf16[512,128]{1,0:T(8,128)(2,1)}, bf16[512,128]{1,0:T(8,128)(2,1)S(1)}, u32[]{:S(2)}, u32[]{:S(2)}) %collective-permute-start.1) | collective-permute-done | bytes 131104 | tf_op jit(solution)/shard_map/ppermute | solution.py:617
  18.9 5.4 %collective-permute-start.5 = (bf16[512,128]{1,0:T(8,128)(2,1)S(1)}, bf16[512,128]{1,0:T(8,128)(2,1)S(1)}, u32[]{:S(2)}, u32[]{:S(2)}) collective-permute-start(bf16[512,128]{1,0:T(8,128)(2,1)S(1)} %copy-done.7), channel_id=1, source_target_pairs={{0,24},{4,28},{8,16},{12,20},{16,8},{20,12},{24,0},{28,4},{1,25},{... | collective-permute-start | bytes 393224 | tf_op jit(solution)/shard_map/ppermute | solution.py:617
  25.0 3.1 %collective-permute-start.6 = (bf16[512,128]{1,0:T(8,128)(2,1)S(1)}, bf16[512,128]{1,0:T(8,128)(2,1)S(1)}, u32[]{:S(2)}, u32[]{:S(2)}) collective-permute-start(bf16[512,128]{1,0:T(8,128)(2,1)S(1)} %copy-done.6), channel_id=1, source_target_pairs={{0,28},{4,24},{8,20},{12,16},{16,12},{20,8},{24,4},{28,0},{1,29},{... | collective-permute-start | bytes 393224 | tf_op jit(solution)/shard_map/ppermute | solution.py:617
  28.1 7.3 %collective-permute-done.5.refs_6_ = bf16[512,128]{1,0:T(8,128)(2,1)S(1)} collective-permute-done((bf16[512,128]{1,0:T(8,128)(2,1)S(1)}, bf16[512,128]{1,0:T(8,128)(2,1)S(1)}, u32[]{:S(2)}, u32[]{:S(2)}) %collective-permute-start.5) | collective-permute-done | bytes 131104 | tf_op jit(solution)/shard_map/ppermute | solution.py:617
  35.4 1.5 %collective-permute-done.6.refs_7_ = bf16[512,128]{1,0:T(8,128)(2,1)S(1)} collective-permute-done((bf16[512,128]{1,0:T(8,128)(2,1)S(1)}, bf16[512,128]{1,0:T(8,128)(2,1)S(1)}, u32[]{:S(2)}, u32[]{:S(2)}) %collective-permute-start.6) | collective-permute-done | bytes 131104 | tf_op jit(solution)/shard_map/ppermute | solution.py:617
  36.9 2.3 %soft_forward.1 = (bf16[8,512,128]{2,1,0:T(8,128)(2,1)S(1)}, f32[8,1024]{1,0:T(8,128)S(1)}, bf16[8,128,128]{2,1,0:T(8,128)(2,1)S(1)}, f32[512,128]{1,0:T(8,128)S(1)}, bf16[512,128]{1,0:T(8,128)(2,1)S(1)}) custom-call(bf16[512,128]{1,0:T(8,128)(2,1)S(1)} %copy-done, bf16[512,128]{1,0:T(8,128)(2,1)S(1)} %collective-permute-done.refs_1_, ...), custom_call_target="tpu_custom_call" | custom-call | flops 1024 | bytes 1024 | tf_op jit(solution)/shard_map/soft_forward/soft_forward/pallas_call | solution.py:593
  39.4 3.0 %lin_local.1 = (bf16[4,800,128]{2,1,0:T(8,128)(2,1)S(1)}, f32[2,4,128,128]{3,2,1,0:T(8,128)S(1)}, bf16[2,4,128,128]{3,2,1,0:T(8,128)(2,1)S(1)}, bf16[2,128,128]{2,1,0:T(8,128)(2,1)S(1)}) custom-call(bf16[800,128]{1,0:T(8,128)(2,1)S(1)} %get-tuple-element.62.refs_0_, bf16[800,128]{1,0:T(8,128)(2,1)S(1)} %collective-permute-done.7.refs_1_, ...), custom_call_target="tpu_custom_call" | custom-call | flops 13340000256 | bytes 1024 | tf_op jit(solution)/shard_map/lin_local/lin_local/pallas_call | solution.py:593
  42.3 3.0 %collective-permute-start.11 = (bf16[2,128,128]{2,1,0:T(8,128)(2,1)S(1)}, bf16[2,128,128]{2,1,0:T(8,128)(2,1)S(1)}, u32[]{:S(2)}, u32[]{:S(2)}) collective-permute-start(bf16[2,128,128]{2,1,0:T(8,128)(2,1)S(1)} %get-tuple-element.74), channel_id=1, source_target_pairs={{0,16},{4,20},{8,24},{12,28},{16,0},{20,4},{24,8},{28,12},{1,17},{... | collective-permute-start | bytes 196616 | tf_op jit(solution)/shard_map/ppermute | solution.py:617
  45.3 3.6 %soft_backward.1 = bf16[8,384,128]{2,1,0:T(8,128)(2,1)} custom-call(bf16[8,512,128]{2,1,0:T(8,128)(2,1)S(1)} %get-tuple-element.69.x_ref, f32[8,1024]{1,0:T(8,128)S(1)} %get-tuple-element.70.lines_ref, bf16[8,128,128]{2,1,0:T(8,128)(2,1)S(1)} %get-tuple-element.71.dv_ref), custom_call_target="tpu_custom_call" | custom-call | flops 16560000000 | bytes 1024 | tf_op jit(solution)/shard_map/soft_backward/soft_backward/pallas_call | solution.py:593
  50.0 3.7 %all-to-all-start = ((bf16[8,384,128]{2,1,0:T(8,128)(2,1)}), bf16[8,384,128]{2,1,0:T(8,128)(2,1)S(1)}, u32[]{:S(2)}, u32[]{:S(2)}) async-start(bf16[8,384,128]{2,1,0:T(8,128)(2,1)} %soft_backward.1), calls=%async_computation | async-start | bytes 1572864 | tf_op jit(solution)/shard_map/all_to_all | solution.py:673
  53.9 1.6 %collective-permute-start.13 = (f32[8,128]{1,0:T(8,128)S(1)}, f32[8,128]{1,0:T(8,128)S(1)}, u32[]{:S(2)}, u32[]{:S(2)}) collective-permute-start(f32[8,128]{1,0:T(8,128)S(1)} %get-tuple-element.79), channel_id=1, source_target_pairs={{0,2},{1,3},{2,0},{3,1},{4,6},{5,7},{6,4},{7,5},{8,10},{9,11},{10,... | collective-permute-start | bytes 12296 | tf_op jit(solution)/shard_map/ppermute | solution.py:678
  57.6 2.8 %collective-permute-start.17 = (f32[8,128]{1,0:T(8,128)S(1)}, f32[8,128]{1,0:T(8,128)S(1)}, u32[]{:S(2)}, u32[]{:S(2)}) collective-permute-start(f32[8,128]{1,0:T(8,128)S(1)} %add_add_fusion.1), channel_id=1, source_target_pairs={{0,12},{4,8},{8,4},{12,0},{16,28},{20,24},{24,20},{28,16},{1,13},{... | collective-permute-start | bytes 12296 | tf_op jit(solution)/shard_map/ppermute | solution.py:678
  61.1 4.9 %collective-permute-done.17 = f32[8,128]{1,0:T(8,128)S(1)} collective-permute-done((f32[8,128]{1,0:T(8,128)S(1)}, f32[8,128]{1,0:T(8,128)S(1)}, u32[]{:S(2)}, u32[]{:S(2)}) %collective-permute-start.17) | collective-permute-done | bytes 4128 | tf_op jit(solution)/shard_map/ppermute | solution.py:678
  66.0 1.5 %lin_cot.1 = (bf16[2,4,128,128]{3,2,1,0:T(8,128)(2,1)S(1)}, bf16[2,128,128]{2,1,0:T(8,128)(2,1)S(1)}) custom-call(bf16[4,800,128]{2,1,0:T(8,128)(2,1)S(1)} %get-tuple-element.66.x_ref, f32[2,4,128,128]{3,2,1,0:T(8,128)S(1)} %get-tuple-element.75.cot_ref, f32[2,4,128,128]{3,2,1,0:T(8,128)S(1)} %get-tuple-element.76.out_ref, f32[8,128]{1,0:T(8,128)S(1)} %add_add_fusion.sums_ref), custom_call_target="tpu_custom_call" | custom-call | flops 1024 | bytes 1024 | tf_op jit(solution)/shard_map/lin_cot/lin_cot/pallas_call | solution.py:593
  67.5 5.3 %collective-permute-start.18 = (bf16[2,128,128]{2,1,0:T(8,128)(2,1)S(1)}, bf16[2,128,128]{2,1,0:T(8,128)(2,1)S(1)}, u32[]{:S(2)}, u32[]{:S(2)}) collective-permute-start(bf16[2,128,128]{2,1,0:T(8,128)(2,1)S(1)} %get-tuple-element.84), channel_id=1, source_target_pairs={{0,16},{4,20},{8,24},{12,28},{16,0},{20,4},{24,8},{28,12},{1,17},{... | collective-permute-start | bytes 196616 | tf_op jit(solution)/shard_map/ppermute | solution.py:617
  72.8 3.3 %lin_own.1 = (bf16[2,4,128,128]{3,2,1,0:T(8,128)(2,1)S(1)}, f32[2,2,4,128,128]{4,3,2,1,0:T(8,128)S(1)}) custom-call(bf16[4,800,128]{2,1,0:T(8,128)(2,1)S(1)} %get-tuple-element.66.x_ref, bf16[2,4,128,128]{3,2,1,0:T(8,128)(2,1)S(1)} %get-tuple-element.80.low_ref, bf16[2,4,128,128]{3,2,1,0:T(8,128)(2,1)S(1)} %get-tuple-element.81.states_ref, ...), custom_call_target="tpu_custom_call" | custom-call | flops 1024 | bytes 1024 | tf_op jit(solution)/shard_map/lin_own/lin_own/pallas_call | solution.py:593
  78.0 2.7 %collective-permute-start.21 = (bf16[768,128]{1,0:T(8,128)(2,1)S(1)}, bf16[768,128]{1,0:T(8,128)(2,1)S(1)}, u32[]{:S(2)}, u32[]{:S(2)}) collective-permute-start(bf16[768,128]{1,0:T(8,128)(2,1)S(1)} %get-tuple-element.91), channel_id=1, source_target_pairs={{0,12},{4,8},{8,4},{12,0},{16,28},{20,24},{24,20},{28,16},{1,13},{... | collective-permute-start | bytes 589832 | tf_op jit(solution)/shard_map/ppermute | solution.py:617
  81.7 2.7 %collective-permute-done.19.refs_1_ = bf16[768,128]{1,0:T(8,128)(2,1)S(1)} collective-permute-done((bf16[768,128]{1,0:T(8,128)(2,1)S(1)}, bf16[768,128]{1,0:T(8,128)(2,1)S(1)}, u32[]{:S(2)}, u32[]{:S(2)}) %collective-permute-start.19) | collective-permute-done | bytes 196640 | tf_op jit(solution)/shard_map/ppermute | solution.py:617
  84.5 2.1 %collective-permute-done.21.refs_3_ = bf16[768,128]{1,0:T(8,128)(2,1)S(1)} collective-permute-done((bf16[768,128]{1,0:T(8,128)(2,1)S(1)}, bf16[768,128]{1,0:T(8,128)(2,1)S(1)}, u32[]{:S(2)}, u32[]{:S(2)}) %collective-permute-start.21) | collective-permute-done | bytes 196640 | tf_op jit(solution)/shard_map/ppermute | solution.py:617
  (51 shorter events, 10.9 us)
Async XLA Ops:
  3.4 9.3 %collective-permute-start = (bf16[512,128]{1,0:T(8,128)(2,1)}, bf16[512,128]{1,0:T(8,128)(2,1)S(1)}, u32[]{:S(2)}, u32[]{:S(2)}) collective-permute-start(bf16[512,128]{1,0:T(8,128)(2,1)} %get-tuple-element.54), channel_id=1, source_target_pairs={{0,4},{4,0},{8,12},{12,8},{16,20},{20,16},{24,28},{28,24},{1,5},{5... | collective-permute-start | bytes 393224 | tf_op jit(solution)/shard_map/ppermute | solution.py:617
  6.4 11.5 %collective-permute-start.1 = (bf16[512,128]{1,0:T(8,128)(2,1)}, bf16[512,128]{1,0:T(8,128)(2,1)S(1)}, u32[]{:S(2)}, u32[]{:S(2)}) collective-permute-start(bf16[512,128]{1,0:T(8,128)(2,1)} %get-tuple-element.55), channel_id=1, source_target_pairs={{0,8},{4,12},{8,0},{12,4},{16,24},{20,28},{24,16},{28,20},{1,9},{5... | collective-permute-start | bytes 393224 | tf_op jit(solution)/shard_map/ppermute | solution.py:617
  8.0 10.8 %collective-permute-start.2 = (bf16[512,128]{1,0:T(8,128)(2,1)}, bf16[512,128]{1,0:T(8,128)(2,1)S(1)}, u32[]{:S(2)}, u32[]{:S(2)}) collective-permute-start(bf16[512,128]{1,0:T(8,128)(2,1)} %get-tuple-element.56), channel_id=1, source_target_pairs={{0,12},{4,8},{8,4},{12,0},{16,28},{20,24},{24,20},{28,16},{1,13},{... | collective-permute-start | bytes 393224 | tf_op jit(solution)/shard_map/ppermute | solution.py:617
  8.0 10.8 %collective-permute-start.3 = (bf16[512,128]{1,0:T(8,128)(2,1)}, bf16[512,128]{1,0:T(8,128)(2,1)S(1)}, u32[]{:S(2)}, u32[]{:S(2)}) collective-permute-start(bf16[512,128]{1,0:T(8,128)(2,1)} %get-tuple-element.57), channel_id=1, source_target_pairs={{0,16},{4,20},{8,24},{12,28},{16,0},{20,4},{24,8},{28,12},{1,17},{... | collective-permute-start | bytes 393224 | tf_op jit(solution)/shard_map/ppermute | solution.py:617
  11.0 25.9 %copy-start = (bf16[512,128]{1,0:T(8,128)(2,1)S(1)}, bf16[512,128]{1,0:T(8,128)(2,1)}, u32[]{:S(2)}) copy-start(bf16[512,128]{1,0:T(8,128)(2,1)} %get-tuple-element.53.refs_0_) | copy-start | bytes 393220
  11.0 14.0 %collective-permute-start.4 = (bf16[512,128]{1,0:T(8,128)(2,1)}, bf16[512,128]{1,0:T(8,128)(2,1)S(1)}, u32[]{:S(2)}, u32[]{:S(2)}) collective-permute-start(bf16[512,128]{1,0:T(8,128)(2,1)} %get-tuple-element.58), channel_id=1, source_target_pairs={{0,20},{4,16},{8,28},{12,24},{16,4},{20,0},{24,12},{28,8},{1,21},{... | collective-permute-start | bytes 393224 | tf_op jit(solution)/shard_map/ppermute | solution.py:617
  12.7 26.6 %collective-permute-start.7 = (bf16[800,128]{1,0:T(8,128)(2,1)S(1)}, bf16[800,128]{1,0:T(8,128)(2,1)S(1)}, u32[]{:S(2)}, u32[]{:S(2)}) collective-permute-start(bf16[800,128]{1,0:T(8,128)(2,1)S(1)} %get-tuple-element.63), channel_id=1, source_target_pairs={{0,4},{4,0},{8,12},{12,8},{16,20},{20,16},{24,28},{28,24},{1,5},{5... | collective-permute-start | bytes 614408 | tf_op jit(solution)/shard_map/ppermute | solution.py:617
  17.9 21.4 %collective-permute-start.8 = (bf16[800,128]{1,0:T(8,128)(2,1)S(1)}, bf16[800,128]{1,0:T(8,128)(2,1)S(1)}, u32[]{:S(2)}, u32[]{:S(2)}) collective-permute-start(bf16[800,128]{1,0:T(8,128)(2,1)S(1)} %get-tuple-element.64), channel_id=1, source_target_pairs={{0,8},{4,12},{8,0},{12,4},{16,24},{20,28},{24,16},{28,20},{1,9},{5... | collective-permute-start | bytes 614408 | tf_op jit(solution)/shard_map/ppermute | solution.py:617
  18.9 20.5 %collective-permute-start.9 = (bf16[800,128]{1,0:T(8,128)(2,1)S(1)}, bf16[800,128]{1,0:T(8,128)(2,1)S(1)}, u32[]{:S(2)}, u32[]{:S(2)}) collective-permute-start(bf16[800,128]{1,0:T(8,128)(2,1)S(1)} %get-tuple-element.65), channel_id=1, source_target_pairs={{0,12},{4,8},{8,4},{12,0},{16,28},{20,24},{24,20},{28,16},{1,13},{... | collective-permute-start | bytes 614408 | tf_op jit(solution)/shard_map/ppermute | solution.py:617
  18.9 16.6 %collective-permute-start.5 = (bf16[512,128]{1,0:T(8,128)(2,1)S(1)}, bf16[512,128]{1,0:T(8,128)(2,1)S(1)}, u32[]{:S(2)}, u32[]{:S(2)}) collective-permute-start(bf16[512,128]{1,0:T(8,128)(2,1)S(1)} %copy-done.7), channel_id=1, source_target_pairs={{0,24},{4,28},{8,16},{12,20},{16,8},{20,12},{24,0},{28,4},{1,25},{... | collective-permute-start | bytes 393224 | tf_op jit(solution)/shard_map/ppermute | solution.py:617
  25.0 11.9 %collective-permute-start.6 = (bf16[512,128]{1,0:T(8,128)(2,1)S(1)}, bf16[512,128]{1,0:T(8,128)(2,1)S(1)}, u32[]{:S(2)}, u32[]{:S(2)}) collective-permute-start(bf16[512,128]{1,0:T(8,128)(2,1)S(1)} %copy-done.6), channel_id=1, source_target_pairs={{0,28},{4,24},{8,20},{12,16},{16,12},{20,8},{24,4},{28,0},{1,29},{... | collective-permute-start | bytes 393224 | tf_op jit(solution)/shard_map/ppermute | solution.py:617
  39.3 9.6 %collective-permute-start.10 = (bf16[512,128]{1,0:T(8,128)(2,1)S(1)}, bf16[512,128]{1,0:T(8,128)(2,1)S(1)}, u32[]{:S(2)}, u32[]{:S(2)}) collective-permute-start(bf16[512,128]{1,0:T(8,128)(2,1)S(1)} %get-tuple-element.68), channel_id=1, source_target_pairs={{0,16},{4,20},{8,24},{12,28},{16,0},{20,4},{24,8},{28,12},{1,17},{... | collective-permute-start | bytes 393224 | tf_op jit(solution)/shard_map/ppermute | solution.py:617
  42.3 6.5 %collective-permute-start.11 = (bf16[2,128,128]{2,1,0:T(8,128)(2,1)S(1)}, bf16[2,128,128]{2,1,0:T(8,128)(2,1)S(1)}, u32[]{:S(2)}, u32[]{:S(2)}) collective-permute-start(bf16[2,128,128]{2,1,0:T(8,128)(2,1)S(1)} %get-tuple-element.74), channel_id=1, source_target_pairs={{0,16},{4,20},{8,24},{12,28},{16,0},{20,4},{24,8},{28,12},{1,17},{... | collective-permute-start | bytes 196616 | tf_op jit(solution)/shard_map/ppermute | solution.py:617
  50.0 30.6 %all-to-all-start = ((bf16[8,384,128]{2,1,0:T(8,128)(2,1)}), bf16[8,384,128]{2,1,0:T(8,128)(2,1)S(1)}, u32[]{:S(2)}, u32[]{:S(2)}) async-start(bf16[8,384,128]{2,1,0:T(8,128)(2,1)} %soft_backward.1), calls=%async_computation | async-start | bytes 1572864 | tf_op jit(solution)/shard_map/all_to_all | solution.py:673
  53.8 3.1 %collective-permute-start.14 = (f32[8,128]{1,0:T(8,128)S(1)}, f32[8,128]{1,0:T(8,128)S(1)}, u32[]{:S(2)}, u32[]{:S(2)}) collective-permute-start(f32[8,128]{1,0:T(8,128)S(1)} %get-tuple-element.79), channel_id=1, source_target_pairs={{0,3},{1,2},{2,1},{3,0},{4,7},{5,6},{6,5},{7,4},{8,11},{9,10},{10,... | collective-permute-start | bytes 12296 | tf_op jit(solution)/shard_map/ppermute | solution.py:678
  53.9 3.7 %collective-permute-start.13 = (f32[8,128]{1,0:T(8,128)S(1)}, f32[8,128]{1,0:T(8,128)S(1)}, u32[]{:S(2)}, u32[]{:S(2)}) collective-permute-start(f32[8,128]{1,0:T(8,128)S(1)} %get-tuple-element.79), channel_id=1, source_target_pairs={{0,2},{1,3},{2,0},{3,1},{4,6},{5,7},{6,4},{7,5},{8,10},{9,11},{10,... | collective-permute-start | bytes 12296 | tf_op jit(solution)/shard_map/ppermute | solution.py:678
  55.4 2.1 %collective-permute-start.12 = (f32[8,128]{1,0:T(8,128)S(1)}, f32[8,128]{1,0:T(8,128)S(1)}, u32[]{:S(2)}, u32[]{:S(2)}) collective-permute-start(f32[8,128]{1,0:T(8,128)S(1)} %get-tuple-element.79), channel_id=1, source_target_pairs={{0,1},{1,0},{2,3},{3,2},{4,5},{5,4},{6,7},{7,6},{8,9},{9,8},{10,11... | collective-permute-start | bytes 12296 | tf_op jit(solution)/shard_map/ppermute | solution.py:678
  57.6 8.4 %collective-permute-start.17 = (f32[8,128]{1,0:T(8,128)S(1)}, f32[8,128]{1,0:T(8,128)S(1)}, u32[]{:S(2)}, u32[]{:S(2)}) collective-permute-start(f32[8,128]{1,0:T(8,128)S(1)} %add_add_fusion.1), channel_id=1, source_target_pairs={{0,12},{4,8},{8,4},{12,0},{16,28},{20,24},{24,20},{28,16},{1,13},{... | collective-permute-start | bytes 12296 | tf_op jit(solution)/shard_map/ppermute | solution.py:678
  60.4 5.6 %collective-permute-start.16 = (f32[8,128]{1,0:T(8,128)S(1)}, f32[8,128]{1,0:T(8,128)S(1)}, u32[]{:S(2)}, u32[]{:S(2)}) collective-permute-start(f32[8,128]{1,0:T(8,128)S(1)} %add_add_fusion.1), channel_id=1, source_target_pairs={{0,8},{4,12},{8,0},{12,4},{16,24},{20,28},{24,16},{28,20},{1,9},{5... | collective-permute-start | bytes 12296 | tf_op jit(solution)/shard_map/ppermute | solution.py:678
  60.9 5.1 %collective-permute-start.15 = (f32[8,128]{1,0:T(8,128)S(1)}, f32[8,128]{1,0:T(8,128)S(1)}, u32[]{:S(2)}, u32[]{:S(2)}) collective-permute-start(f32[8,128]{1,0:T(8,128)S(1)} %add_add_fusion.1), channel_id=1, source_target_pairs={{0,4},{4,0},{8,12},{12,8},{16,20},{20,16},{24,28},{28,24},{1,5},{5... | collective-permute-start | bytes 12296 | tf_op jit(solution)/shard_map/ppermute | solution.py:678
  67.5 8.6 %collective-permute-start.18 = (bf16[2,128,128]{2,1,0:T(8,128)(2,1)S(1)}, bf16[2,128,128]{2,1,0:T(8,128)(2,1)S(1)}, u32[]{:S(2)}, u32[]{:S(2)}) collective-permute-start(bf16[2,128,128]{2,1,0:T(8,128)(2,1)S(1)} %get-tuple-element.84), channel_id=1, source_target_pairs={{0,16},{4,20},{8,24},{12,28},{16,0},{20,4},{24,8},{28,12},{1,17},{... | collective-permute-start | bytes 196616 | tf_op jit(solution)/shard_map/ppermute | solution.py:617
  77.1 7.4 %collective-permute-start.19 = (bf16[768,128]{1,0:T(8,128)(2,1)S(1)}, bf16[768,128]{1,0:T(8,128)(2,1)S(1)}, u32[]{:S(2)}, u32[]{:S(2)}) collective-permute-start(bf16[768,128]{1,0:T(8,128)(2,1)S(1)} %get-tuple-element.89), channel_id=1, source_target_pairs={{0,4},{4,0},{8,12},{12,8},{16,20},{20,16},{24,28},{28,24},{1,5},{5... | collective-permute-start | bytes 589832 | tf_op jit(solution)/shard_map/ppermute | solution.py:617
  77.9 6.5 %collective-permute-start.20 = (bf16[768,128]{1,0:T(8,128)(2,1)S(1)}, bf16[768,128]{1,0:T(8,128)(2,1)S(1)}, u32[]{:S(2)}, u32[]{:S(2)}) collective-permute-start(bf16[768,128]{1,0:T(8,128)(2,1)S(1)} %get-tuple-element.90), channel_id=1, source_target_pairs={{0,8},{4,12},{8,0},{12,4},{16,24},{20,28},{24,16},{28,20},{1,9},{5... | collective-permute-start | bytes 589832 | tf_op jit(solution)/shard_map/ppermute | solution.py:617
  78.0 8.6 %collective-permute-start.21 = (bf16[768,128]{1,0:T(8,128)(2,1)S(1)}, bf16[768,128]{1,0:T(8,128)(2,1)S(1)}, u32[]{:S(2)}, u32[]{:S(2)}) collective-permute-start(bf16[768,128]{1,0:T(8,128)(2,1)S(1)} %get-tuple-element.91), channel_id=1, source_target_pairs={{0,12},{4,8},{8,4},{12,0},{16,28},{20,24},{24,20},{28,16},{1,13},{... | collective-permute-start | bytes 589832 | tf_op jit(solution)/shard_map/ppermute | solution.py:617
  (7 other events, 74.7 us)

commit v2 on v0

--- a/solution.py
+++ b/solution.py
@@ -279,21 +279,6 @@
     return scratch[pl.ds(head, scratch.shape[0] // heads, stride=heads), :]
 
 
-def soft_head(place, half):
-    return 2 * place if place < half else 2 * (place - half) + 1
-
-
-def pack_soft_kernel(half, *refs):
-    sources, sent, scratch = refs[:4], refs[4], refs[5]
-    rows, heads, _ = sources[0].shape
-    for place, source in enumerate(sources):
-        spread(source, scratch)
-        for dest in range(2 * half):
-            sent[dest, pl.ds(place * rows, rows), :] = head_of(
-                scratch, soft_head(dest, half), heads
-            ).astype(jnp.bfloat16)
-
-
 def put_heads(half, outs, scratch, first, second, rows, heads):
     late, me = later(half), place_in(half)
     for step, out in enumerate(outs):
@@ -301,6 +286,14 @@
         even, odd = head_of(scratch, head, heads), head_of(scratch, head + 1, heads)
         out[pl.ds(first * rows, rows), :] = jnp.where(late, odd, even).astype(jnp.bfloat16)
         out[pl.ds(second * rows, rows), :] = jnp.where(late, even, odd).astype(jnp.bfloat16)
+
+
+def pack_soft_kernel(half, *refs):
+    sources, outs, scratches = refs[:4], refs[4 : 4 + half], refs[4 + half :]
+    rows, heads, _ = sources[0].shape
+    for place, (source, scratch) in enumerate(zip(sources, scratches)):
+        spread(source, scratch)
+        put_heads(half, outs, scratch, place, 4 + place, rows, heads)
 
 
 def pack_lin_kernel(half, *refs):
@@ -328,18 +321,7 @@
         out[pl.ds(6 * rows + PAD, PAD), :] = jnp.where(late, even, odd).astype(jnp.bfloat16)
 
 
-def unpack_soft_kernel(half, packed, *refs):
-    outs, scratch = refs[:-1], refs[-1]
-    rows, heads, width = outs[0].shape
-    for place, out in enumerate(outs):
-        for source in range(2 * half):
-            scratch[pl.ds(soft_head(source, half), rows, stride=heads), :] = packed[
-                source, pl.ds(place * rows, rows), :
-            ].astype(jnp.float32)
-        out[...] = scratch[...].reshape(rows, heads, width).astype(jnp.bfloat16)
-
-
-def unpack_lin_kernel(half, *refs):
+def unpack_kernel(half, *refs):
     steps, outs, scratch = refs[:half], refs[half:-1], refs[-1]
     late, me = later(half), place_in(half)
     rows, heads, width = outs[0].shape
@@ -353,103 +335,312 @@
         out[...] = scratch[...].reshape(rows, heads, width).astype(jnp.bfloat16)
 
 
-def soft_part(x_ref, place):
-    rows, width = x_ref.shape[1] // 4, x_ref.shape[2]
-
-    def take(tile):
-        return x_ref[pl.ds(tile * GROUP, GROUP), pl.ds(place * rows, rows), :].reshape(
-            GROUP * rows, width
+def soft_gather_kernel(half, *refs):
+    steps, x_ref, give_ref = refs[:half], refs[half], refs[half + 1]
+    late, me = later(half), place_in(half)
+    rows = x_ref.shape[1] // 8
+    for step, ref in enumerate(steps):
+        source = jnp.bitwise_xor(me, step)
+        x_ref[source] = ref[...]
+        give_ref[source] = jnp.where(
+            late, ref[pl.ds(0, rows), :], ref[pl.ds(rows, rows), :]
         )
 
-    return take
-
-
-def tile_scores(k, q, i, j):
+
+def soft_blocks(half, x_ref, recv_ref):
+    late = later(half)
+    rows = x_ref.shape[1] // 8
+    width = x_ref.shape[2]
+
+    def own(slot, place):
+        def take(tile):
+            return x_ref[
+                pl.ds(tile * GROUP, GROUP), pl.ds((slot * 4 + place) * rows, rows), :
+            ].reshape(GROUP * rows, width)
+
+        return take
+
+    def other(place):
+        def take(tile):
+            return recv_ref[place][pl.ds(tile * GROUP, GROUP)].reshape(GROUP * rows, width)
+
+        return take
+
+    def either(if_late, if_early):
+        return lambda tile: jnp.where(late, if_late(tile), if_early(tile))
+
+    zero = (own(0, 0), own(0, 1), own(0, 2), own(0, 3), True)
+    same = (own(1, 0), own(1, 1), own(1, 2), own(1, 3), True)
+    rect = (
+        either(own(1, 0), other(0)),
+        either(other(0), own(1, 1)),
+        either(other(1), own(1, 2)),
+        either(own(1, 3), other(1)),
+        False,
+    )
+    return zero, same, rect
+
+
+def tile_scores(block, i, j, wide):
+    q, k, _, _, causal = block
     scores = nt(k(i), q(j))
-    if i < j:
+    if not causal or i < j:
         return scores
-    key_at = lax.broadcasted_iota(jnp.int32, scores.shape, 0)
-    query_at = lax.broadcasted_iota(jnp.int32, scores.shape, 1)
+    key_at = lax.broadcasted_iota(jnp.int32, (wide, wide), 0)
+    query_at = lax.broadcasted_iota(jnp.int32, (wide, wide), 1)
     return jnp.where(key_at <= query_at, scores, -1e30)
 
 
-def soft_forward_kernel(half, x_ref, lines_ref, dv_ref, own_ref, give_ref, scr, total_scr):
-    late = later(half)
-    spans, rows, width = dv_ref.shape
-    wide, scale = GROUP * rows, width**-0.5
-    q, k, v, g = (soft_part(x_ref, place) for place in range(4))
-    lines_ref[...] = jnp.zeros_like(lines_ref)
-    for j in range(spans // GROUP):
+def tiles_of(block, j, tiles):
+    return range(j + 1) if block[4] else range(tiles)
+
+
+def block_stats(block, scr, tiles, wide, scale):
+    tops, totals, dots = [], [], []
+    _, _, v, g, _ = block
+    for j in range(tiles):
         top = None
-        for i in range(j + 1):
-            scores = tile_scores(k, q, i, j)
-            scr[i] = scores
+        for i in tiles_of(block, j, tiles):
+            scores = tile_scores(block, i, j, wide)
+            scr[i, j] = scores
             here = jnp.max(scores, axis=0, keepdims=True)
             top = here if top is None else jnp.maximum(top, here)
         total = jnp.zeros_like(top)
+        out_t = None
+        for i in tiles_of(block, j, tiles):
+            weights = jnp.exp((scr[i, j] - top) * scale)
+            scr[i, j] = weights
+            total = total + jnp.sum(weights, axis=0, keepdims=True)
+            part = tn(v(i), weights.astype(jnp.bfloat16))
+            out_t = part if out_t is None else out_t + part
+        grads_t = jnp.transpose(g(j).astype(jnp.float32))
+        tops.append(top)
+        totals.append(total)
+        dots.append(jnp.sum(grads_t * out_t, axis=0, keepdims=True))
+    return tops, totals, dots
+
+
+def joined(mine, other, use, scale):
+    top, total, dot = mine
+    top_other, total_other, dot_other = other
+    top_other = jnp.where(use, top_other, top)
+    both = jnp.maximum(top, top_other)
+    here = jnp.exp((top - both) * scale)
+    there = jnp.where(use, jnp.exp((top_other - both) * scale), 0.0)
+    inverse = 1.0 / (total * here + total_other * there)
+    return here * inverse, (dot * here + dot_other * there) * inverse
+
+
+def block_grads(block, factors, deltas, scr, tiles, scale):
+    q, k, v, g, _ = block
+    dq, dk, dv = [], [None] * tiles, [None] * tiles
+    add = lambda total, part: part if total is None else total + part
+    for j in range(tiles):
+        dq_t = None
+        for i in tiles_of(block, j, tiles):
+            probs = scr[i, j] * factors[j]
+            dv[i] = add(dv[i], nn(probs.astype(jnp.bfloat16), g(j)))
+            grad_probs = nt(v(i), g(j))
+            grad_scores = (probs * (grad_probs - deltas[j])).astype(jnp.bfloat16)
+            dq_t = add(dq_t, tn(k(i), grad_scores))
+            dk[i] = add(dk[i], nn(grad_scores, q(j)))
+        dq.append(jnp.transpose(dq_t) * scale)
+    return dq, [x * scale for x in dk], dv
+
+
+def put_lines(ref, first, lines, wide):
+    for place, row in enumerate(lines):
+        for j, piece in enumerate(row):
+            ref[pl.ds(first + place, 1), pl.ds(j * wide, wide)] = piece
+
+
+def get_lines(ref, first, j, wide):
+    return [ref[pl.ds(first + place, 1), pl.ds(j * wide, wide)] for place in range(3)]
+
+
+def soft_shape(half, x_ref):
+    rows, width = x_ref.shape[1] // 8, x_ref.shape[2]
+    return half // GROUP, GROUP * rows, width**-0.5
+
+
+def soft_stats_kernel(half, x_ref, lines_ref, give_ref, scr):
+    late, rows = later(half), x_ref.shape[1] // 8
+    for span in range(half):
+        give_ref[span] = jnp.where(
+            late, x_ref[span, pl.ds(3 * rows, rows), :], x_ref[span, pl.ds(2 * rows, rows), :]
+        )
+    tiles, wide, scale = soft_shape(half, x_ref)
+    zero, same, _ = soft_blocks(half, x_ref, None)
+    lines_ref[...] = jnp.zeros_like(lines_ref)
+    put_lines(lines_ref, 0, block_stats(zero, scr, tiles, wide, scale), wide)
+    put_lines(lines_ref, 3, block_stats(same, scr, tiles, wide, scale), wide)
+
+
+def rect_joined(late, lines_ref, far_ref, lines, j, wide, scale):
+    near, far = get_lines(lines_ref, 3, j, wide), get_lines(far_ref, 0, j, wide)
+    other = [jnp.where(late, a, b) for a, b in zip(near, far)]
+    return joined([line[j] for line in lines], other, True, scale)
+
+
+def soft_first_kernel(half, x_ref, recv_ref, lines_ref, send_ref, rect_ref, scr):
+    late = later(half)
+    tiles, wide, scale = soft_shape(half, x_ref)
+    _, same, rect = soft_blocks(half, x_ref, (recv_ref, recv_ref))
+    grads = same[3]
+    tops, totals = [], []
+    rect_ref[...] = jnp.zeros_like(rect_ref)
+    dv = [None] * tiles
+    for j in range(tiles):
+        top = None
+        for i in range(tiles):
+            scores = tile_scores(rect, i, j, wide)
+            scr[i, j] = scores
+            here = jnp.max(scores, axis=0, keepdims=True)
+            top = here if top is None else jnp.maximum(top, here)
+        total = jnp.zeros_like(top)
+        for i in range(tiles):
+            weights = jnp.exp((scr[i, j] - top) * scale)
+            scr[i, j] = weights
+            total = total + jnp.sum(weights, axis=0, keepdims=True)
+        tops.append(top)
+        totals.append(total)
+        zeros = [jnp.zeros_like(top)] * tiles
+        factor, _ = rect_joined(
+            late, lines_ref, lines_ref, ([top] * tiles, [total] * tiles, zeros), j, wide, scale
+        )
+        for i in range(tiles):
+            part = nn((scr[i, j] * factor).astype(jnp.bfloat16), grads(j))
+            dv[i] = part if dv[i] is None else dv[i] + part
+    put_lines(rect_ref, 0, (tops, totals), wide)
+    for i in range(tiles):
+        send_ref[pl.ds(i * wide, wide), :] = dv[i].astype(jnp.bfloat16)
+
+    @pl.when(jnp.logical_not(late))
+    def _():
+        width = x_ref.shape[2]
+        for place, part in enumerate(triple(rect_ref[...])):
+            for piece in range(rect_ref.shape[1] // width):
+                send_ref[pl.ds((place * tiles * GROUP + piece) * PAD, PAD), :] = jnp.concatenate(
+                    [part[:, piece * width : (piece + 1) * width]] * (PAD // 8), axis=0
+                )
+
+
+def soft_rect_kernel(
+    half, x_ref, recv_ref, recv_two_ref, lines_ref, far_ref, made_ref, rect_ref, scr
+):
+    late = later(half)
+    tiles, wide, scale = soft_shape(half, x_ref)
+    _, _, rect = soft_blocks(half, x_ref, (recv_ref, recv_two_ref))
+    lines = block_stats(rect, scr, tiles, wide, scale)
+    rect_ref[...] = jnp.zeros_like(rect_ref)
+    put_lines(rect_ref, 0, lines, wide)
+    both = [rect_joined(late, lines_ref, far_ref, lines, j, wide, scale) for j in range(tiles)]
+    factors, deltas = zip(*both)
+    dq, dk, dv = block_grads(rect, factors, deltas, scr, tiles, scale)
+    for j in range(tiles):
+        at = pl.ds(j * wide, wide)
+        for place, made in enumerate((dq[j], dk[j], dv[j])):
+            made_ref[place, at, :] = made
+
+
+def sent_lines(ref, pieces, lines_ref):
+    width = ref.shape[1]
+    for piece in range(pieces):
+        parts = [
+            ref[pl.ds((place * pieces + piece) * PAD, PAD), :].astype(jnp.float32)[0:8]
+            for place in range(3)
+        ]
+        lines_ref[:, pl.ds(piece * width, width)] = parts[0] + parts[1] + parts[2]
+
+
+def causal_grads(half, slot, x_ref, lines_ref, far_ref, scr):
+    tiles, wide, scale = soft_shape(half, x_ref)
+    block = soft_blocks(half, x_ref, None)[slot]
+    factors, deltas = [], []
+    for j in range(tiles):
+        mine = get_lines(lines_ref, 3 * slot, j, wide)
+        factor, delta = joined(mine, get_lines(far_ref, 0, j, wide), later(half), scale)
+        factors.append(factor)
+        deltas.append(delta)
         for i in range(j + 1):
-            weights = jnp.exp((scr[i] - top) * scale)
-            scr[i] = weights
-            total = total + jnp.sum(weights, axis=0, keepdims=True)
-        inverse = 1.0 / total
-        out_t = None
+            scr[i, j] = jnp.exp((tile_scores(block, i, j, wide) - mine[0]) * scale)
+    return block_grads(block, factors, deltas, scr, tiles, scale)
+
+
+def soft_zero_kernel(half, x_ref, lines_ref, far_ref, made_ref, scr):
+    tiles, wide, _ = soft_shape(half, x_ref)
+    grads = causal_grads(half, 0, x_ref, lines_ref, far_ref, scr)
+    for j in range(tiles):
+        for place in range(3):
+            made_ref[place, pl.ds(j * wide, wide), :] = grads[place][j]
+
+
+def soft_value_kernel(half, x_ref, lines_ref, sent_ref, dv_ref, far_ref):
+    sent_lines(sent_ref, half, far_ref)
+    tiles, wide, scale = soft_shape(half, x_ref)
+    zero, _, _ = soft_blocks(half, x_ref, None)
+    dv = [None] * tiles
+    for j in range(tiles):
+        mine = get_lines(lines_ref, 0, j, wide)
+        factor, _ = joined(mine, get_lines(far_ref, 0, j, wide), later(half), scale)
         for i in range(j + 1):
-            low = (scr[i] * inverse).astype(jnp.bfloat16)
-            part = tn(v(i), low)
-            out_t = part if out_t is None else out_t + part
-            part = nn(low, g(j))
-            total_scr[i] = part if i == j else total_scr[i] + part
-        delta = jnp.sum(jnp.transpose(g(j).astype(jnp.float32)) * out_t, axis=0, keepdims=True)
-        for place, line in enumerate((top, inverse, delta)):
-            lines_ref[pl.ds(place, 1), pl.ds(j * wide, wide)] = line
-    for i in range(spans // GROUP):
-        dv_ref[pl.ds(i * GROUP, GROUP)] = (
-            total_scr[i].astype(jnp.bfloat16).reshape(GROUP, rows, width)
-        )
-        total_scr[i] = total_scr[i] + g(i).astype(jnp.float32)
-    tiles = half // GROUP
+            weights = jnp.exp((tile_scores(zero, i, j, wide) - mine[0]) * scale)
+            part = nn((weights * factor).astype(jnp.bfloat16), zero[3](j))
+            dv[i] = part if dv[i] is None else dv[i] + part
     for i in range(tiles):
-        early, after = total_scr[i], total_scr[tiles + i]
-        at = pl.ds(i * wide, wide)
-        own_ref[at, :] = jnp.where(late, after, early)
-        give_ref[at, :] = jnp.where(late, early, after).astype(jnp.bfloat16)
-
-
-def soft_backward_kernel(x_ref, lines_ref, dv_ref, packed, dk_scr):
-    spans, rows, width = dv_ref.shape
-    wide, scale = GROUP * rows, width**-0.5
-    q, k, v, g = (soft_part(x_ref, place) for place in range(4))
-    for j in range(spans // GROUP):
-        top, inverse, delta = (
-            lines_ref[pl.ds(place, 1), pl.ds(j * wide, wide)] for place in range(3)
-        )
-        dq_t = None
-        for i in range(j + 1):
-            probs = jnp.exp((tile_scores(k, q, i, j) - top) * scale) * inverse
-            grad_scores = (probs * (nt(v(i), g(j)) - delta)).astype(jnp.bfloat16)
-            part = tn(k(i), grad_scores)
-            dq_t = part if dq_t is None else dq_t + part
-            part = nn(grad_scores, q(j))
-            dk_scr[i] = part if i == j else dk_scr[i] + part
-        dq = (jnp.transpose(dq_t) * scale).astype(jnp.bfloat16)
-        packed[pl.ds(j * GROUP, GROUP), pl.ds(0, rows), :] = dq.reshape(GROUP, rows, width)
-    for i in range(spans // GROUP):
-        dk = (dk_scr[i] * scale).astype(jnp.bfloat16)
-        packed[pl.ds(i * GROUP, GROUP), pl.ds(rows, rows), :] = dk.reshape(GROUP, rows, width)
-    packed[:, pl.ds(2 * rows, rows), :] = dv_ref[...]
-
-
-def span_tables(extra):
-    rows = extra.shape[1]
+        dv_ref[pl.ds(i * wide, wide), :] = dv[i]
+
+
+def soft_same_kernel(half, x_ref, lines_ref, rect_lines_ref, rect_ref, packed, dv_ref, scr):
+    late = later(half)
+    tiles, wide, _ = soft_shape(half, x_ref)
+    rows = wide // GROUP
+    grads = causal_grads(half, 1, x_ref, lines_ref, rect_lines_ref, scr)
+    for j in range(tiles):
+        at = pl.ds(j * wide, wide)
+        for place in range(3):
+            added = rect_ref[place, at, :]
+            made = grads[place][j] + (
+                jnp.where(late, added, 0.0) if place == 0 else jnp.where(late, 0.0, added)
+            )
+            packed[pl.ds(j * GROUP, GROUP), pl.ds(place * rows, rows), :] = made.astype(
+                jnp.bfloat16
+            ).reshape(GROUP, rows, made.shape[1])
+            if place == 2:
+                dv_ref[at, :] = made
+
+
+def decay_lines(half, rows, x_ref):
+    firsts = [
+        x_ref[span, pl.ds(6 * rows + slot * PAD, PAD), :].astype(jnp.float32)
+        for slot in range(2)
+        for span in range(half)
+    ]
+    parts = [
+        jnp.concatenate([block[place : place + 1] for block in firsts], axis=0)
+        for place in range(3)
+    ]
     first = lax.broadcasted_iota(jnp.int32, (rows, rows), 0)
     second = lax.broadcasted_iota(jnp.int32, (rows, rows), 1)
-    lower = first >= second
-    along = nn(extra, (first <= second).astype(jnp.float32).astype(jnp.bfloat16))
-    down = nt(lower.astype(jnp.float32).astype(jnp.bfloat16), extra)
-    row = along[0:1] + along[1:2] + along[2:3]
-    col = down[:, 0:1] + down[:, 1:2] + down[:, 2:3]
-    finish = row[:, rows - 1 : rows]
-    return row, col, finish, lower, first <= second
+    ones = (first <= second).astype(jnp.float32).astype(jnp.bfloat16)
+    sums = nn(jnp.concatenate(parts, axis=0).astype(jnp.bfloat16), ones)
+    count = 2 * half
+    return sums[:count] + sums[count : 2 * count] + sums[2 * count :]
+
+
+def tables(lines):
+    count, rows = lines.shape
+    columns = jnp.transpose(lines)
+    return [
+        (lines[c : c + 1], columns[:, c : c + 1], lines[c : c + 1, rows - 1 : rows])
+        for c in range(count)
+    ]
+
+
+def triangle(rows):
+    first = lax.broadcasted_iota(jnp.int32, (rows, rows), 0)
+    second = lax.broadcasted_iota(jnp.int32, (rows, rows), 1)
+    return first >= second, first <= second
 
 
 def gain_of(extra):
@@ -465,43 +656,62 @@
 
 
 def lin_local_kernel(half, rows, *refs):
-    steps, (x_ref, out_ref, states_ref, give_ref) = refs[:half], refs[half:]
+    steps, (x_ref, lines_ref, out_ref, states_ref, give_ref) = refs[:half], refs[half + 1 :]
     me = place_in(half)
     for step, ref in enumerate(steps):
         x_ref[jnp.bitwise_xor(me, step)] = ref[...]
     width = x_ref.shape[2]
+    lines = decay_lines(half, rows, x_ref)
+    lines_ref[...] = lines
+    chunks = tables(lines)
+    lower, _ = triangle(rows)
     for slot in range(2):
-        state = jnp.zeros((width, width), jnp.float32)
+        state = None
         for span in range(half):
-            q, k, v, extra = lin_parts(x_ref, slot, span, rows)
-            row, col, finish, lower, _ = span_tables(extra)
-            within = jnp.exp(jnp.where(lower, col - row, -1e30))
-            pair = (nt(q, k) * within).astype(jnp.bfloat16)
-            out = nn(pair, v)
-            if span > 0:
-                low_state = state.astype(jnp.bfloat16)
-                states_ref[slot, span] = low_state
-                out = out + jnp.exp(col) * nn(q, low_state)
+            _, k, v, _ = lin_parts(x_ref, slot, span, rows)
+            _, col, finish = chunks[slot * half + span]
+            decayed = (k.astype(jnp.float32) * jnp.exp(finish - col)).astype(jnp.bfloat16)
+            if span:
+                states_ref[slot, span] = state.astype(jnp.bfloat16)
+                state = jnp.exp(finish) * state + tn(decayed, v)
             else:
                 states_ref[slot, span] = jnp.zeros((width, width), jnp.bfloat16)
+                state = tn(decayed, v)
+        give_ref[1 - slot] = state.astype(jnp.bfloat16)
+    for slot in range(2):
+        for span in range(half):
+            q, k, v, _ = lin_parts(x_ref, slot, span, rows)
+            row, col, _ = chunks[slot * half + span]
+            within = jnp.exp(jnp.where(lower, col - row, -1e30))
+            out = nn((nt(q, k) * within).astype(jnp.bfloat16), v)
+            if span:
+                out = out + jnp.exp(col) * nn(q, states_ref[slot, span])
             out_ref[slot, span] = out
-            decayed = (k.astype(jnp.float32) * jnp.exp(finish - col)).astype(jnp.bfloat16)
-            state = jnp.exp(finish) * state + tn(decayed, v)
-        give_ref[1 - slot] = state.astype(jnp.bfloat16)
-
-
-def lin_sums_kernel(half, rows, x_ref, own_ref, far_ref, local_ref, given_ref, cot_ref, out_ref, sums_ref):
-    before = [jnp.zeros((1, 1), jnp.float32)] * 2
+
+
+def lin_sums_kernel(
+    half, rows, x_ref, lines_ref, soft_ref, zero_ref, same_ref, dv_ref, local_ref, given_ref,
+    cot_ref, out_ref, sums_ref,
+):
+    late = later(half)
+    chunks = tables(lines_ref[...])
+    before = [jnp.where(late, jnp.zeros((1, 1), jnp.float32), -1e30)] * 2
     for span in range(half):
         at = pl.ds(span * rows, rows)
         inner, squares = None, None
-        for slot, part_ref in enumerate((own_ref, far_ref)):
+        for slot in range(2):
             q, _, _, extra = lin_parts(x_ref, slot, span, rows)
-            _, col, finish, _, _ = span_tables(extra)
+            _, col, finish = chunks[slot * half + span]
             out = local_ref[slot, span] + jnp.exp(before[slot] + col) * nn(q, given_ref[slot])
             before[slot] = before[slot] + finish
             out_ref[slot, span] = out
-            scaled = gain_of(extra) * part_ref[at, :].astype(jnp.float32)
+            cot = soft_ref[span, pl.ds((slot * 4 + 3) * rows, rows), :].astype(jnp.float32)
+            if slot == 0:
+                cot = cot + zero_ref[at, :]
+                cot = cot + jnp.where(late, 0.0, dv_ref[at, :].astype(jnp.float32))
+            else:
+                cot = cot + same_ref[at, :]
+            scaled = gain_of(extra) * cot
             cot_ref[slot, span] = scaled
             inner = scaled * out if slot == 0 else inner + scaled * out
             squares = out * out if slot == 0 else squares + out * out
@@ -509,40 +719,46 @@
         sums_ref[pl.ds(half + span, 1), :] = jnp.sum(jnp.transpose(inner), axis=0, keepdims=True)
 
 
-def lin_cot_kernel(half, rows, total_width, x_ref, cot_ref, out_ref, sums_ref, low_ref, state_ref):
-    width = cot_ref.shape[3]
+def lin_cot_kernel(
+    half, rows, total_width, x_ref, lines_ref, cot_ref, out_ref, sums_ref, low_ref, state_ref
+):
     mean = sums_ref[pl.ds(0, half), :] / total_width + epsilon
     root = jnp.sqrt(mean)
     inner = sums_ref[pl.ds(half, half), :] / (total_width * root * mean)
     scalars = jnp.transpose(jnp.concatenate([1.0 / root, inner], axis=0))
+    chunks = tables(lines_ref[...])
     for slot in range(2):
-        state = jnp.zeros((width, width), jnp.float32)
-        for span in reversed(range(half)):
-            q, _, _, extra = lin_parts(x_ref, slot, span, rows)
-            _, col, finish, _, _ = span_tables(extra)
+        before = jnp.zeros((1, 1), jnp.float32)
+        state = None
+        for span in range(half):
+            q, _, _, _ = lin_parts(x_ref, slot, span, rows)
+            _, col, finish = chunks[slot * half + span]
             cotangent = (
                 cot_ref[slot, span] * scalars[:, span : span + 1]
                 - out_ref[slot, span] * scalars[:, half + span : half + span + 1]
             )
             low_cot = cotangent.astype(jnp.bfloat16)
             low_ref[slot, span] = low_cot
-            decayed = (q.astype(jnp.float32) * jnp.exp(col)).astype(jnp.bfloat16)
-            state = jnp.exp(finish) * state + tn(decayed, low_cot)
+            decayed = (q.astype(jnp.float32) * jnp.exp(before + col)).astype(jnp.bfloat16)
+            before = before + finish
+            part = tn(decayed, low_cot)
+            state = part if state is None else state + part
         state_ref[1 - slot] = state.astype(jnp.bfloat16)
 
 
-def lin_own_kernel(half, rows, x_ref, low_ref, states_ref, given_ref, dq_ref, made_ref):
-    width = low_ref.shape[3]
+def lin_own_kernel(half, rows, x_ref, lines_ref, low_ref, states_ref, given_ref, dq_ref, made_ref):
+    chunks = tables(lines_ref[...])
+    lower, upper = triangle(rows)
+    late = later(half)
     for slot in range(2):
+        given = jnp.where(late, given_ref[slot].astype(jnp.float32), 0.0)
         before = [jnp.zeros((1, 1), jnp.float32)]
         for span in range(half):
-            finish = span_tables(lin_parts(x_ref, slot, span, rows)[3])[2]
-            before.append(before[-1] + finish)
-        given = given_ref[slot].astype(jnp.float32)
-        state = jnp.zeros((width, width), jnp.float32)
+            before.append(before[-1] + chunks[slot * half + span][2])
+        state = None
         for span in reversed(range(half)):
-            q, k, v, extra = lin_parts(x_ref, slot, span, rows)
-            row, col, finish, lower, upper = span_tables(extra)
+            q, k, v, _ = lin_parts(x_ref, slot, span, rows)
+            row, col, finish = chunks[slot * half + span]
             within = jnp.exp(jnp.where(lower, col - row, -1e30))
             within_t = jnp.exp(jnp.where(upper, row - col, -1e30))
             low_cot = low_ref[slot, span]
@@ -551,34 +767,66 @@
             pair_t = (nt(k, q) * within_t).astype(jnp.bfloat16)
             leading = jnp.exp(col)
             trailing = jnp.exp(finish - col)
-            low_state = state.astype(jnp.bfloat16)
             carried = states_ref[slot, span].astype(jnp.float32) + jnp.exp(before[span]) * given
             dq = nn(grad_pair, k) + leading * nt(low_cot, carried.astype(jnp.bfloat16))
+            dk = nn(grad_pair_t, q)
+            dv = nn(pair_t, low_cot)
+            decayed = (q.astype(jnp.float32) * leading).astype(jnp.bfloat16)
+            part = tn(decayed, low_cot)
+            if state is None:
+                state = part
+            else:
+                low_state = state.astype(jnp.bfloat16)
+                dk = dk + trailing * nt(v, low_state)
+                dv = dv + trailing * nn(k, low_state)
+                state = jnp.exp(finish) * state + part
             dq_ref[slot, span] = dq.astype(jnp.bfloat16)
-            made_ref[slot, 0, span] = nn(grad_pair_t, q) + trailing * nt(v, low_state)
-            made_ref[slot, 1, span] = nn(pair_t, low_cot) + trailing * nn(k, low_state)
-            decayed = (q.astype(jnp.float32) * leading).astype(jnp.bfloat16)
-            state = jnp.exp(finish) * state + tn(decayed, low_cot)
-
-
-def lin_finish_kernel(half, rows, x_ref, dq_ref, made_ref, state_ref, *refs):
+            made_ref[slot, 0, span] = dk
+            made_ref[slot, 1, span] = dv
+
+
+def lin_finish_kernel(half, rows, x_ref, lines_ref, dq_ref, made_ref, state_ref, *refs):
     outs, packed = refs[:half], refs[half]
+    chunks = tables(lines_ref[...])
+    me = place_in(half)
     for slot in range(2):
         state = state_ref[slot]
-        after = jnp.zeros((1, 1), jnp.float32)
+        after = jnp.where(later(half), -1e30, jnp.zeros((1, 1), jnp.float32))
         for span in reversed(range(half)):
-            _, k, v, extra = lin_parts(x_ref, slot, span, rows)
-            _, col, finish, _, _ = span_tables(extra)
+            _, k, v, _ = lin_parts(x_ref, slot, span, rows)
+            _, col, finish = chunks[slot * half + span]
             trailing = jnp.exp(after + finish - col)
             after = after + finish
             dk = made_ref[slot, 0, span] + trailing * nt(v, state)
             dv = made_ref[slot, 1, span] + trailing * nn(k, state)
-            for place, made in enumerate((dq_ref[slot, span], dk, dv)):
-                packed[span, pl.ds((slot * 3 + place) * rows, rows), :] = made.astype(
-                    jnp.bfloat16
-                )
+            packed[span, pl.ds(slot * 3 * rows, rows), :] = dq_ref[slot, span]
+            packed[span, pl.ds((slot * 3 + 1) * rows, rows), :] = dk.astype(jnp.bfloat16)
+            packed[span, pl.ds((slot * 3 + 2) * rows, rows), :] = dv.astype(jnp.bfloat16)
     for step, out in enumerate(outs):
-        out[...] = packed[jnp.bitwise_xor(place_in(half), step)]
+        out[...] = packed[jnp.bitwise_xor(me, step)]
+
+
+def pack_give_kernel(half, rect_ref, give_ref):
+    give_ref[...] = jnp.where(later(half), rect_ref[1], rect_ref[0]).astype(jnp.bfloat16)
+
+
+def pack_early_kernel(half, zero_ref, same_ref, dv_ref, given_ref, *outs):
+    late, me = later(half), place_in(half)
+    rows = same_ref.shape[1] // 3
+    for step, out in enumerate(outs):
+        span = jnp.bitwise_xor(me, step)
+        at = pl.ds(pl.multiple_of(span * rows, rows), rows)
+        given = given_ref[at, :].astype(jnp.float32)
+        added = (
+            jnp.where(late, given, 0.0),
+            jnp.where(late, 0.0, given),
+            jnp.where(late, 0.0, dv_ref[at, :].astype(jnp.float32)),
+        )
+        for place in range(3):
+            out[pl.ds(place * rows, rows), :] = (zero_ref[place, at, :] + added[place]).astype(
+                jnp.bfloat16
+            )
+        out[pl.ds(3 * rows, 3 * rows), :] = same_ref[span]
 
 
 def call(name, kernel, out_shape, scratch, cost, *args):
@@ -588,7 +836,7 @@
             out_shape=out_shape,
             scratch_shapes=scratch,
             name=name,
-            compiler_params=pltpu.CompilerParams(vmem_limit_bytes=VMEM_BYTES[name.startswith("pack_soft")]),
+            compiler_params=pltpu.CompilerParams(vmem_limit_bytes=VMEM_BYTES[name == "pack_soft"]),
             cost_estimate=pl.CostEstimate(flops=cost, bytes_accessed=1024, transcendentals=0),
         )(*args)
 
@@ -603,91 +851,116 @@
     full = lambda *s: jax.ShapeDtypeStruct(s, jnp.float32)
     held = lambda *s: pltpu.VMEM(s, jnp.float32)
     bind = functools.partial
-    tiles, wide = spans // GROUP, GROUP * rows
+    tiles, wide = half // GROUP, GROUP * rows
     after = lax.optimization_barrier
-
-    def moved(x, pairs):
-        return lax.ppermute(x, "ctx", pairs)
+    turned = held(rows * heads, width)
+    scores = held(tiles, tiles, wide, wide)
+    mine = (low(rows, heads, width),) * 3
+
+    def moved(x, step):
+        return lax.ppermute(x, "ctx", [(i, i ^ step) for i in range(spans)])
 
     def exchanged(parts):
-        return [parts[0]] + [
-            moved(parts[step], [(i, i ^ step) for i in range(spans)]) for step in range(1, half)
-        ]
-
-    both = [(i, i ^ half) for i in range(spans)]
-    up = [(i, i + half) for i in range(half)]
-    down = [(i + half, i) for i in range(half)]
-    turned = held(rows * heads, width)
-    mine = (low(rows, heads, width),) * 3
+        return [moved(part, step) if step else part for step, part in enumerate(parts)]
+
     soft_sent = call(
-        "pack_soft", bind(pack_soft_kernel, half), low(spans, 4 * rows, width), [turned], 11960000000,
-        soft_q, soft_k, soft_v, out_grad,
-    )
-    x = lax.all_to_all(soft_sent, "ctx", 0, 0, tiled=True)
+        "pack_soft", bind(pack_soft_kernel, half), (low(8 * rows, width),) * half, [turned] * 4,
+        11960000000, soft_q, soft_k, soft_v, out_grad,
+    )
+    soft_got = exchanged(soft_sent)
     lin_sent = call(
         "pack_lin", bind(pack_lin_kernel, half), (low(6 * rows + 2 * PAD, width),) * half,
         [turned] * 3 + [held(6 * heads, width)], 5980000000,
         lin_q, lin_k, lin_v, lin_decay, norm_gain,
     )
     lin_got = exchanged(lin_sent)
-    lines, dv, own, give = call(
-        "soft_forward", bind(soft_forward_kernel, half),
-        (full(8, spans * rows), low(spans, rows, width), full(tokens, width), low(tokens, width)),
-        [held(tiles, wide, wide), held(tiles, wide, width)], COST, x,
-    )
-    far = moved(give, both)
-    lin_got[0], own = after((lin_got[0], own))
-    lin_x, local_out, states, state = call(
+    x, give = call(
+        "soft_gather", bind(soft_gather_kernel, half),
+        (low(half, 8 * rows, width), low(half, rows, width)), [], COST, *soft_got,
+    )
+    recv = moved(give, half)
+    lines, give = call(
+        "soft_stats", bind(soft_stats_kernel, half), (full(8, tokens), low(half, rows, width)),
+        [scores], 5520000000, x,
+    )
+    recv_two = moved(give, half)
+    far_lines = moved(lines, half)
+    dv_give, first_lines = call(
+        "soft_first", bind(soft_first_kernel, half), (low(tokens, width), full(8, tokens)),
+        [scores], 13800000000, x, recv, lines,
+    )
+    dv_given = moved(dv_give, half)
+    lin_x, lin_lines, local_out, states, state = call(
         "lin_local", bind(lin_local_kernel, half, rows),
         (
             low(half, 6 * rows + 2 * PAD, width),
+            full(2 * half, rows),
             full(2, half, rows, width),
             low(2, half, width, width),
             low(2, width, width),
         ),
-        [], 13340000000, *lin_got,
-    )
-    state = moved(state, up)
-    soft_made = call(
-        "soft_backward", soft_backward_kernel, low(spans, 3 * rows, width),
-        [held(tiles, wide, width)], 16560000000, x, lines, dv,
-    )
-    far, soft_made = after((far, soft_made))
+        [], 7360000000, *lin_got, first_lines,
+    )
+    state = moved(state, half)
+    rect, rect_lines = call(
+        "soft_rect", bind(soft_rect_kernel, half), (full(3, tokens, width), full(8, tokens)),
+        [scores], 9200000000, x, recv, recv_two, lines, far_lines,
+    )
+    far_rect = moved(rect_lines, half)
+    same, same_dv = call(
+        "soft_same", bind(soft_same_kernel, half),
+        (low(half, 3 * rows, width), full(tokens, width)), [scores], 4370000000,
+        x, lines, rect_lines, rect,
+    )
+    zero_dv = call(
+        "soft_value", bind(soft_value_kernel, half), full(tokens, width), [held(8, tokens)], COST,
+        x, lines, dv_given,
+    )
     cot, layer_out, sums = call(
         "lin_sums", bind(lin_sums_kernel, half, rows),
         (full(2, half, rows, width),) * 2 + (full(2 * half, rows),), [], COST,
-        lin_x, own, far, local_out, state,
-    )
-    soft_made, sums = after((soft_made, sums))
-    soft_back = lax.all_to_all(soft_made, "ctx", 0, 0, tiled=True)
-    for axis, reach in (("head", lax.axis_size("head")), ("ctx", half)):
+        lin_x, lin_lines, x, zero_dv, same_dv, dv_given, local_out, state,
+    )
+    zero = call(
+        "soft_zero", bind(soft_zero_kernel, half), full(3, tokens, width), [scores], 3680000000,
+        x, lines, far_rect,
+    )
+    rect_then, sums = after((rect, sums))
+    give = call("pack_give", bind(pack_give_kernel, half), low(tokens, width), [], 9200000000, rect_then)
+    given = moved(give, half)
+    steps = [("ctx", 1 << bit) for bit in range((half - 1).bit_length())]
+    steps += [("head", 1 << bit) for bit in reversed(range((lax.axis_size("head") - 1).bit_length()))]
+    for place, (axis, step) in enumerate(steps):
+        sums = after(sums)
+        if place == 3:
+            given, sums = after((given, sums))
         count = lax.axis_size(axis)
-        sums = after(sums)
-        sums = sums + sum(
-            lax.ppermute(sums, axis, [(i, i ^ step) for i in range(count)])
-            for step in range(1, reach)
-        )
+        sums = sums + lax.ppermute(sums, axis, [(i, i ^ step) for i in range(count)])
+    early = call(
+        "pack_early", bind(pack_early_kernel, half), (low(6 * rows, width),) * half, [], 9200000000,
+        zero, same, dv_given, given,
+    )
+    early = exchanged(early)
     low_cot, late_state = call(
         "lin_cot", bind(lin_cot_kernel, half, rows, total_width),
         (low(2, half, rows, width), low(2, width, width)), [], COST,
-        lin_x, cot, layer_out, sums,
-    )
-    late_state = moved(late_state, down)
+        lin_x, lin_lines, cot, layer_out, sums,
+    )
+    late_state = moved(late_state, half)
     lin_dq, lin_made = call(
         "lin_own", bind(lin_own_kernel, half, rows),
         (low(2, half, rows, width), full(2, 2, half, rows, width)), [], COST,
-        lin_x, low_cot, states, state,
+        lin_x, lin_lines, low_cot, states, state,
     )
     lin_made = call(
         "lin_finish", bind(lin_finish_kernel, half, rows), (low(6 * rows, width),) * half,
         [pltpu.VMEM((half, 6 * rows, width), jnp.bfloat16)], COST,
-        lin_x, lin_dq, lin_made, late_state,
+        lin_x, lin_lines, lin_dq, lin_made, late_state,
     )
     lin_back = exchanged(lin_made)
-    soft_out = call(
-        "unpack_soft", bind(unpack_soft_kernel, half), mine, [turned], COST, soft_back
-    )
-    lin_out = call("unpack_lin", bind(unpack_lin_kernel, half), mine, [turned], COST, *lin_back)
+    soft_out = list(call("unpack_soft", bind(unpack_kernel, half), mine, [turned], 5060000000, *early))
+    lin_back[0], soft_out[0] = after((lin_back[0], soft_out[0]))
+    lin_out = call("unpack_lin", bind(unpack_kernel, half), mine, [turned], COST, *lin_back)
     return (*lin_out, *soft_out)
 
 

time: 91.8 us -> 85 us (0.926)
  waiting for transfers between devices: 40 us -> 30.6 us
  starting transfers between devices: 29.5 us -> 34.7 us
  Pallas kernels: 21.1 us -> 18.6 us
    all_to_all x2 -> x0, waiting for transfers between devices: 21.8 us -> none  [the longest x1 21.8 us: by_halves(): x = lax.all_to_all(soft_sent, 'ctx', 0, 0, tiled=True)]
    ppermute x9 -> x20, starting transfers between devices: 13 us -> 30.1 us  [moved(): return lax.ppermute(x, 'ctx', [(i, i ^ step) for i in range(spans)])]
    ppermute x9 -> x20, waiting for transfers between devices: 11.5 us -> 25.1 us  [moved(): return lax.ppermute(x, 'ctx', [(i, i ^ step) for i in range(spans)])]
    all_to_all x2 -> x0, starting transfers between devices: 11 us -> none  [the longest x1 7.42 us: by_halves(): x = lax.all_to_all(soft_sent, 'ctx', 0, 0, tiled=True)]
    pallas_call x11 -> x18, Pallas kernels: 21.1 us -> 18.6 us  [call(): pl.pallas_call(kernel, out_shape=out_shape, scratch_shapes=scratch, name=...]
    ppermute x6 -> x4, waiting for transfers between devices: 6.7 us -> 5.56 us  [by_halves(): lax.ppermute(sums, axis, [(i, i ^ step) for i in range(count)])]
    ppermute x6 -> x4, starting transfers between devices: 5.5 us -> 4.64 us  [by_halves(): lax.ppermute(sums, axis, [(i, i ^ step) for i in range(count)])]
  transfers between devices with their start and end apart: 17 -> 24, of which waited for: 9 -> 14; matrix products, arithmetic and copies ran while one was open for 0% -> 0% of each run, Pallas kernels for 18% -> 16%
where the time goes in v2:
time: 85 us; the launch traced here: 84.8 us
  starting transfers between devices  34.7 us (41%)
  waiting for transfers between devices  30.6 us (36%)
  Pallas kernels  18.6 us (22%)
  between operations  0.85 us (1%)
    ppermute x20, starting transfers between devices, moved(): return lax.ppermute(x, 'ctx', [(i, i ^ step) for i in range(spans)])  30.1 us
    ppermute x20, waiting for transfers between devices, moved(): return lax.ppermute(x, 'ctx', [(i, i ^ step) for i in range(spans)])  25.1 us
    pallas_call x18, Pallas kernels, call(): pl.pallas_call(kernel, out_shape=out_shape, scratch_shapes=scratch, name=...  18.6 us
    ppermute x4, waiting for transfers between devices, by_halves(): lax.ppermute(sums, axis, [(i, i ^ step) for i in range(count)])  5.56 us
    ppermute x4, starting transfers between devices, by_halves(): lax.ppermute(sums, axis, [(i, i ^ step) for i in range(count)])  4.64 us
  transfers between devices with their start and end apart: 24, of which 14 were waited for; matrix products, arithmetic and copies ran while one was open for 0% of the time, Pallas kernels for 16%

profile of v2, /device:TPU:0, one launch (start us, length us, event | category | flops | bytes accessed | tf_op | source)
XLA Modules:
  0.0 84.8 jit_solution(1201281905576359759)
XLA Ops:
  0.7 2.6 %pack_soft.1 = (bf16[1024,128]{1,0:T(8,128)(2,1)}, bf16[1024,128]{1,0:T(8,128)(2,1)}, bf16[1024,128]{1,0:T(8,128)(2,1)}, bf16[1024,128]{1,0:T(8,128)(2,1)}) custom-call(bf16[128,8,128]{2,1,0:T(8,128)(2,1)} %refs_0_.3, bf16[128,8,128]{2,1,0:T(8,128)(2,1)} %refs_1_.3, bf16[128,8,128]{2,1,0:T(8,128)(2,1)} %refs_2_.3, bf16[128,8,128]{2,1,0:T(8,128)(2,1)} %refs_3_.3), custom_call_target="tpu_custom_call" | custom-call | flops 11960000512 | bytes 1024 | tf_op jit(solution)/shard_map/pack_soft/pack_soft/pallas_call | solution.py:834
  3.2 3.0 %collective-permute-start.3 = (bf16[1024,128]{1,0:T(8,128)(2,1)}, bf16[1024,128]{1,0:T(8,128)(2,1)S(1)}, u32[]{:S(2)}, u32[]{:S(2)}) collective-permute-start(bf16[1024,128]{1,0:T(8,128)(2,1)} %get-tuple-element.61), channel_id=1, source_target_pairs={{0,4},{4,0},{8,12},{12,8},{16,20},{20,16},{24,28},{28,24},{1,5},{5... | collective-permute-start | bytes 786440 | tf_op jit(solution)/shard_map/ppermute | solution.py:861
  6.2 1.6 %collective-permute-start.4 = (bf16[1024,128]{1,0:T(8,128)(2,1)}, bf16[1024,128]{1,0:T(8,128)(2,1)S(1)}, u32[]{:S(2)}, u32[]{:S(2)}) collective-permute-start(bf16[1024,128]{1,0:T(8,128)(2,1)} %get-tuple-element.62), channel_id=1, source_target_pairs={{0,8},{4,12},{8,0},{12,4},{16,24},{20,28},{24,16},{28,20},{1,9},{5... | collective-permute-start | bytes 786440 | tf_op jit(solution)/shard_map/ppermute | solution.py:861
  8.2 2.0 %collective-permute-start = (bf16[800,128]{1,0:T(8,128)(2,1)S(1)}, bf16[800,128]{1,0:T(8,128)(2,1)S(1)}, u32[]{:S(2)}, u32[]{:S(2)}) collective-permute-start(bf16[800,128]{1,0:T(8,128)(2,1)S(1)} %get-tuple-element.57), channel_id=1, source_target_pairs={{0,4},{4,0},{8,12},{12,8},{16,20},{20,16},{24,28},{28,24},{1,5},{5... | collective-permute-start | bytes 614408 | tf_op jit(solution)/shard_map/ppermute | solution.py:861
  10.2 1.6 %collective-permute-start.1 = (bf16[800,128]{1,0:T(8,128)(2,1)S(1)}, bf16[800,128]{1,0:T(8,128)(2,1)S(1)}, u32[]{:S(2)}, u32[]{:S(2)}) collective-permute-start(bf16[800,128]{1,0:T(8,128)(2,1)S(1)} %get-tuple-element.58), channel_id=1, source_target_pairs={{0,8},{4,12},{8,0},{12,4},{16,24},{20,28},{24,16},{28,20},{1,9},{5... | collective-permute-start | bytes 614408 | tf_op jit(solution)/shard_map/ppermute | solution.py:861
  11.8 2.5 %collective-permute-done.3.refs_1_ = bf16[1024,128]{1,0:T(8,128)(2,1)S(1)} collective-permute-done((bf16[1024,128]{1,0:T(8,128)(2,1)}, bf16[1024,128]{1,0:T(8,128)(2,1)S(1)}, u32[]{:S(2)}, u32[]{:S(2)}) %collective-permute-start.3) | collective-permute-done | bytes 262176 | tf_op jit(solution)/shard_map/ppermute | solution.py:861
  14.3 3.8 %collective-permute-start.2 = (bf16[800,128]{1,0:T(8,128)(2,1)S(1)}, bf16[800,128]{1,0:T(8,128)(2,1)S(1)}, u32[]{:S(2)}, u32[]{:S(2)}) collective-permute-start(bf16[800,128]{1,0:T(8,128)(2,1)S(1)} %get-tuple-element.59), channel_id=1, source_target_pairs={{0,12},{4,8},{8,4},{12,0},{16,28},{20,24},{24,20},{28,16},{1,13},{... | collective-permute-start | bytes 614408 | tf_op jit(solution)/shard_map/ppermute | solution.py:861
  18.1 2.7 %collective-permute-done.5.refs_3_ = bf16[1024,128]{1,0:T(8,128)(2,1)S(1)} collective-permute-done((bf16[1024,128]{1,0:T(8,128)(2,1)}, bf16[1024,128]{1,0:T(8,128)(2,1)S(1)}, u32[]{:S(2)}, u32[]{:S(2)}) %collective-permute-start.5) | collective-permute-done | bytes 262176 | tf_op jit(solution)/shard_map/ppermute | solution.py:861
  20.9 3.1 %collective-permute-start.6 = (bf16[4,128,128]{2,1,0:T(8,128)(2,1)S(1)}, bf16[4,128,128]{2,1,0:T(8,128)(2,1)S(1)}, u32[]{:S(2)}, u32[]{:S(2)}) collective-permute-start(bf16[4,128,128]{2,1,0:T(8,128)(2,1)S(1)} %get-tuple-element.65), channel_id=1, source_target_pairs={{0,16},{4,20},{8,24},{12,28},{16,0},{20,4},{24,8},{28,12},{1,17},{... | collective-permute-start | bytes 393224 | tf_op jit(solution)/shard_map/ppermute | solution.py:861
  25.3 6.7 %collective-permute-done.6.recv_ref = bf16[4,128,128]{2,1,0:T(8,128)(2,1)S(1)} collective-permute-done((bf16[4,128,128]{2,1,0:T(8,128)(2,1)S(1)}, bf16[4,128,128]{2,1,0:T(8,128)(2,1)S(1)}, u32[]{:S(2)}, u32[]{:S(2)}) %collective-permute-start.6) | collective-permute-done | bytes 131104 | tf_op jit(solution)/shard_map/ppermute | solution.py:861
  32.0 3.4 %collective-permute-start.9 = (f32[8,512]{1,0:T(8,128)S(1)}, f32[8,512]{1,0:T(8,128)S(1)}, u32[]{:S(2)}, u32[]{:S(2)}) collective-permute-start(f32[8,512]{1,0:T(8,128)S(1)} %get-tuple-element.66.lines_ref), channel_id=1, source_target_pairs={{0,16},{4,20},{8,24},{12,28},{16,0},{20,4},{24,8},{28,12},{1,17},{... | collective-permute-start | bytes 49160 | tf_op jit(solution)/shard_map/ppermute | solution.py:861
  36.5 1.6 %lin_local.1 = (bf16[4,800,128]{2,1,0:T(8,128)(2,1)S(1)}, f32[8,128]{1,0:T(8,128)S(1)}, f32[2,4,128,128]{3,2,1,0:T(8,128)S(1)}, bf16[2,4,128,128]{3,2,1,0:T(8,128)(2,1)S(1)}, bf16[2,128,128]{2,1,0:T(8,128)(2,1)S(1)}) custom-call(bf16[800,128]{1,0:T(8,128)(2,1)S(1)} %get-tuple-element.56.refs_0_, bf16[800,128]{1,0:T(8,128)(2,1)S(1)} %collective-permute-done.refs_1_, ...), custom_call_target="tpu_custom_call" | custom-call | flops 7360000000 | bytes 1024 | tf_op jit(solution)/shard_map/lin_local/lin_local/pallas_call | solution.py:834
  38.1 3.0 %collective-permute-start.10 = (bf16[2,128,128]{2,1,0:T(8,128)(2,1)S(1)}, bf16[2,128,128]{2,1,0:T(8,128)(2,1)S(1)}, u32[]{:S(2)}, u32[]{:S(2)}) collective-permute-start(bf16[2,128,128]{2,1,0:T(8,128)(2,1)S(1)} %get-tuple-element.76), channel_id=1, source_target_pairs={{0,16},{4,20},{8,24},{12,28},{16,0},{20,4},{24,8},{28,12},{1,17},{... | collective-permute-start | bytes 196616 | tf_op jit(solution)/shard_map/ppermute | solution.py:861
  41.0 1.8 %soft_rect.1 = (f32[3,512,128]{2,1,0:T(8,128)S(1)}, f32[8,512]{1,0:T(8,128)S(1)}) custom-call(bf16[4,1024,128]{2,1,0:T(8,128)(2,1)S(1)} %get-tuple-element.64.x_ref.soft_ref, bf16[4,128,128]{2,1,0:T(8,128)(2,1)S(1)} %collective-permute-done.6.recv_ref, bf16[4,128,128]{2,1,0:T(8,128)(2,1)S(1)} %collective-permute-done.8.recv_two_ref, ...), custom_call_target="tpu_custom_call" | custom-call | flops 9200000000 | bytes 1024 | tf_op jit(solution)/shard_map/soft_rect/soft_rect/pallas_call | solution.py:834
  45.8 1.8 %collective-permute-start.12 = (f32[8,128]{1,0:T(8,128)S(1)}, f32[8,128]{1,0:T(8,128)S(1)}, u32[]{:S(2)}, u32[]{:S(2)}) collective-permute-start(f32[8,128]{1,0:T(8,128)S(1)} %get-tuple-element.81), channel_id=1, source_target_pairs={{0,4},{4,0},{8,12},{12,8},{16,20},{20,16},{24,28},{28,24},{1,5},{5... | collective-permute-start | bytes 12296 | tf_op jit(solution)/shard_map/ppermute | solution.py:938
  47.8 1.7 %collective-permute-done.12 = f32[8,128]{1,0:T(8,128)S(1)} collective-permute-done((f32[8,128]{1,0:T(8,128)S(1)}, f32[8,128]{1,0:T(8,128)S(1)}, u32[]{:S(2)}, u32[]{:S(2)}) %collective-permute-start.12) | collective-permute-done | bytes 4128 | tf_op jit(solution)/shard_map/ppermute | solution.py:938
  53.5 1.5 %collective-permute-start.14 = (f32[8,128]{1,0:T(8,128)S(1)}, f32[8,128]{1,0:T(8,128)S(1)}, u32[]{:S(2)}, u32[]{:S(2)}) collective-permute-start(f32[8,128]{1,0:T(8,128)S(1)} %add.13), channel_id=1, source_target_pairs={{0,2},{1,3},{2,0},{3,1},{4,6},{5,7},{6,4},{7,5},{8,10},{9,11},{10,... | collective-permute-start | bytes 12296 | tf_op jit(solution)/shard_map/ppermute | solution.py:938
  59.6 2.4 %collective-permute-start.20 = (bf16[768,128]{1,0:T(8,128)(2,1)S(1)}, bf16[768,128]{1,0:T(8,128)(2,1)S(1)}, u32[]{:S(2)}, u32[]{:S(2)}) collective-permute-start(bf16[768,128]{1,0:T(8,128)(2,1)S(1)} %get-tuple-element.94), channel_id=1, source_target_pairs={{0,12},{4,8},{8,4},{12,0},{16,28},{20,24},{24,20},{28,16},{1,13},{... | collective-permute-start | bytes 589832 | tf_op jit(solution)/shard_map/ppermute | solution.py:861
  64.5 1.9 %lin_own.1 = (bf16[2,4,128,128]{3,2,1,0:T(8,128)(2,1)S(1)}, f32[2,2,4,128,128]{4,3,2,1,0:T(8,128)S(1)}) custom-call(bf16[4,800,128]{2,1,0:T(8,128)(2,1)S(1)} %get-tuple-element.68.x_ref, f32[8,128]{1,0:T(8,128)S(1)} %get-tuple-element.69.lines_ref, bf16[2,4,128,128]{3,2,1,0:T(8,128)(2,1)S(1)} %get-tuple-element.83.low_ref, ...), custom_call_target="tpu_custom_call" | custom-call | flops 1024 | bytes 1024 | tf_op jit(solution)/shard_map/lin_own/lin_own/pallas_call | solution.py:834
  66.4 4.0 %collective-permute-done.16.state_ref = bf16[2,128,128]{2,1,0:T(8,128)(2,1)S(1)} collective-permute-done((bf16[2,128,128]{2,1,0:T(8,128)(2,1)S(1)}, bf16[2,128,128]{2,1,0:T(8,128)(2,1)S(1)}, u32[]{:S(2)}, u32[]{:S(2)}) %collective-permute-start.16) | collective-permute-done | bytes 65568 | tf_op jit(solution)/shard_map/ppermute | solution.py:861
  72.3 2.5 %collective-permute-start.23 = (bf16[768,128]{1,0:T(8,128)(2,1)S(1)}, bf16[768,128]{1,0:T(8,128)(2,1)S(1)}, u32[]{:S(2)}, u32[]{:S(2)}) collective-permute-start(bf16[768,128]{1,0:T(8,128)(2,1)S(1)} %get-tuple-element.99), channel_id=1, source_target_pairs={{0,12},{4,8},{8,4},{12,0},{16,28},{20,24},{24,20},{28,16},{1,13},{... | collective-permute-start | bytes 589832 | tf_op jit(solution)/shard_map/ppermute | solution.py:861
  76.1 2.1 %collective-permute-done.21.refs_1_ = bf16[768,128]{1,0:T(8,128)(2,1)S(1)} collective-permute-done((bf16[768,128]{1,0:T(8,128)(2,1)S(1)}, bf16[768,128]{1,0:T(8,128)(2,1)S(1)}, u32[]{:S(2)}, u32[]{:S(2)}) %collective-permute-start.21) | collective-permute-done | bytes 196640 | tf_op jit(solution)/shard_map/ppermute | solution.py:861
  78.2 1.9 %collective-permute-done.22.refs_2_ = bf16[768,128]{1,0:T(8,128)(2,1)S(1)} collective-permute-done((bf16[768,128]{1,0:T(8,128)(2,1)S(1)}, bf16[768,128]{1,0:T(8,128)(2,1)S(1)}, u32[]{:S(2)}, u32[]{:S(2)}) %collective-permute-start.22) | collective-permute-done | bytes 196640 | tf_op jit(solution)/shard_map/ppermute | solution.py:861
  80.1 3.4 %collective-permute-done.23.refs_3_ = bf16[768,128]{1,0:T(8,128)(2,1)S(1)} collective-permute-done((bf16[768,128]{1,0:T(8,128)(2,1)S(1)}, bf16[768,128]{1,0:T(8,128)(2,1)S(1)}, u32[]{:S(2)}, u32[]{:S(2)}) %collective-permute-start.23) | collective-permute-done | bytes 196640 | tf_op jit(solution)/shard_map/ppermute | solution.py:861
  (58 shorter events, 21.6 us)
Async XLA Ops:
  3.2 11.0 %collective-permute-start.3 = (bf16[1024,128]{1,0:T(8,128)(2,1)}, bf16[1024,128]{1,0:T(8,128)(2,1)S(1)}, u32[]{:S(2)}, u32[]{:S(2)}) collective-permute-start(bf16[1024,128]{1,0:T(8,128)(2,1)} %get-tuple-element.61), channel_id=1, source_target_pairs={{0,4},{4,0},{8,12},{12,8},{16,20},{20,16},{24,28},{28,24},{1,5},{5... | collective-permute-start | bytes 786440 | tf_op jit(solution)/shard_map/ppermute | solution.py:861
  6.2 11.8 %collective-permute-start.4 = (bf16[1024,128]{1,0:T(8,128)(2,1)}, bf16[1024,128]{1,0:T(8,128)(2,1)S(1)}, u32[]{:S(2)}, u32[]{:S(2)}) collective-permute-start(bf16[1024,128]{1,0:T(8,128)(2,1)} %get-tuple-element.62), channel_id=1, source_target_pairs={{0,8},{4,12},{8,0},{12,4},{16,24},{20,28},{24,16},{28,20},{1,9},{5... | collective-permute-start | bytes 786440 | tf_op jit(solution)/shard_map/ppermute | solution.py:861
  7.8 13.0 %collective-permute-start.5 = (bf16[1024,128]{1,0:T(8,128)(2,1)}, bf16[1024,128]{1,0:T(8,128)(2,1)S(1)}, u32[]{:S(2)}, u32[]{:S(2)}) collective-permute-start(bf16[1024,128]{1,0:T(8,128)(2,1)} %get-tuple-element.63), channel_id=1, source_target_pairs={{0,12},{4,8},{8,4},{12,0},{16,28},{20,24},{24,20},{28,16},{1,13},{... | collective-permute-start | bytes 786440 | tf_op jit(solution)/shard_map/ppermute | solution.py:861
  8.2 28.2 %collective-permute-start = (bf16[800,128]{1,0:T(8,128)(2,1)S(1)}, bf16[800,128]{1,0:T(8,128)(2,1)S(1)}, u32[]{:S(2)}, u32[]{:S(2)}) collective-permute-start(bf16[800,128]{1,0:T(8,128)(2,1)S(1)} %get-tuple-element.57), channel_id=1, source_target_pairs={{0,4},{4,0},{8,12},{12,8},{16,20},{20,16},{24,28},{28,24},{1,5},{5... | collective-permute-start | bytes 614408 | tf_op jit(solution)/shard_map/ppermute | solution.py:861
  10.2 26.3 %collective-permute-start.1 = (bf16[800,128]{1,0:T(8,128)(2,1)S(1)}, bf16[800,128]{1,0:T(8,128)(2,1)S(1)}, u32[]{:S(2)}, u32[]{:S(2)}) collective-permute-start(bf16[800,128]{1,0:T(8,128)(2,1)S(1)} %get-tuple-element.58), channel_id=1, source_target_pairs={{0,8},{4,12},{8,0},{12,4},{16,24},{20,28},{24,16},{28,20},{1,9},{5... | collective-permute-start | bytes 614408 | tf_op jit(solution)/shard_map/ppermute | solution.py:861
  14.3 22.2 %collective-permute-start.2 = (bf16[800,128]{1,0:T(8,128)(2,1)S(1)}, bf16[800,128]{1,0:T(8,128)(2,1)S(1)}, u32[]{:S(2)}, u32[]{:S(2)}) collective-permute-start(bf16[800,128]{1,0:T(8,128)(2,1)S(1)} %get-tuple-element.59), channel_id=1, source_target_pairs={{0,12},{4,8},{8,4},{12,0},{16,28},{20,24},{24,20},{28,16},{1,13},{... | collective-permute-start | bytes 614408 | tf_op jit(solution)/shard_map/ppermute | solution.py:861
  20.9 11.1 %collective-permute-start.6 = (bf16[4,128,128]{2,1,0:T(8,128)(2,1)S(1)}, bf16[4,128,128]{2,1,0:T(8,128)(2,1)S(1)}, u32[]{:S(2)}, u32[]{:S(2)}) collective-permute-start(bf16[4,128,128]{2,1,0:T(8,128)(2,1)S(1)} %get-tuple-element.65), channel_id=1, source_target_pairs={{0,16},{4,20},{8,24},{12,28},{16,0},{20,4},{24,8},{28,12},{1,17},{... | collective-permute-start | bytes 393224 | tf_op jit(solution)/shard_map/ppermute | solution.py:861
  25.2 15.8 %collective-permute-start.8 = (bf16[4,128,128]{2,1,0:T(8,128)(2,1)S(1)}, bf16[4,128,128]{2,1,0:T(8,128)(2,1)S(1)}, u32[]{:S(2)}, u32[]{:S(2)}) collective-permute-start(bf16[4,128,128]{2,1,0:T(8,128)(2,1)S(1)} %get-tuple-element.71), channel_id=1, source_target_pairs={{0,16},{4,20},{8,24},{12,28},{16,0},{20,4},{24,8},{28,12},{1,17},{... | collective-permute-start | bytes 393224 | tf_op jit(solution)/shard_map/ppermute | solution.py:861
  32.0 9.0 %collective-permute-start.9 = (f32[8,512]{1,0:T(8,128)S(1)}, f32[8,512]{1,0:T(8,128)S(1)}, u32[]{:S(2)}, u32[]{:S(2)}) collective-permute-start(f32[8,512]{1,0:T(8,128)S(1)} %get-tuple-element.66.lines_ref), channel_id=1, source_target_pairs={{0,16},{4,20},{8,24},{12,28},{16,0},{20,4},{24,8},{28,12},{1,17},{... | collective-permute-start | bytes 49160 | tf_op jit(solution)/shard_map/ppermute | solution.py:861
  36.4 7.8 %collective-permute-start.7 = (bf16[512,128]{1,0:T(8,128)(2,1)S(1)}, bf16[512,128]{1,0:T(8,128)(2,1)S(1)}, u32[]{:S(2)}, u32[]{:S(2)}) collective-permute-start(bf16[512,128]{1,0:T(8,128)(2,1)S(1)} %get-tuple-element.70), channel_id=1, source_target_pairs={{0,16},{4,20},{8,24},{12,28},{16,0},{20,4},{24,8},{28,12},{1,17},{... | collective-permute-start | bytes 393224 | tf_op jit(solution)/shard_map/ppermute | solution.py:861
  38.1 6.9 %collective-permute-start.10 = (bf16[2,128,128]{2,1,0:T(8,128)(2,1)S(1)}, bf16[2,128,128]{2,1,0:T(8,128)(2,1)S(1)}, u32[]{:S(2)}, u32[]{:S(2)}) collective-permute-start(bf16[2,128,128]{2,1,0:T(8,128)(2,1)S(1)} %get-tuple-element.76), channel_id=1, source_target_pairs={{0,16},{4,20},{8,24},{12,28},{16,0},{20,4},{24,8},{28,12},{1,17},{... | collective-permute-start | bytes 196616 | tf_op jit(solution)/shard_map/ppermute | solution.py:861
  45.8 3.7 %collective-permute-start.12 = (f32[8,128]{1,0:T(8,128)S(1)}, f32[8,128]{1,0:T(8,128)S(1)}, u32[]{:S(2)}, u32[]{:S(2)}) collective-permute-start(f32[8,128]{1,0:T(8,128)S(1)} %get-tuple-element.81), channel_id=1, source_target_pairs={{0,4},{4,0},{8,12},{12,8},{16,20},{20,16},{24,28},{28,24},{1,5},{5... | collective-permute-start | bytes 12296 | tf_op jit(solution)/shard_map/ppermute | solution.py:938
  47.6 7.4 %collective-permute-start.17 = (f32[8,512]{1,0:T(8,128)S(1)}, f32[8,512]{1,0:T(8,128)S(1)}, u32[]{:S(2)}, u32[]{:S(2)}) collective-permute-start(f32[8,512]{1,0:T(8,128)S(1)} %get-tuple-element.72.rect_lines_ref), channel_id=1, source_target_pairs={{0,16},{4,20},{8,24},{12,28},{16,0},{20,4},{24,8},{28,12},{1,17},{... | collective-permute-start | bytes 49160 | tf_op jit(solution)/shard_map/ppermute | solution.py:861
  49.5 4.0 %collective-permute-start.13 = (f32[8,128]{1,0:T(8,128)S(1)}, f32[8,128]{1,0:T(8,128)S(1)}, u32[]{:S(2)}, u32[]{:S(2)}) collective-permute-start(f32[8,128]{1,0:T(8,128)S(1)} %add.12), channel_id=1, source_target_pairs={{0,8},{4,12},{8,0},{12,4},{16,24},{20,28},{24,16},{28,20},{1,9},{5... | collective-permute-start | bytes 12296 | tf_op jit(solution)/shard_map/ppermute | solution.py:938
  50.9 7.4 %collective-permute-start.11 = (bf16[512,128]{1,0:T(8,128)(2,1)S(1)}, bf16[512,128]{1,0:T(8,128)(2,1)S(1)}, u32[]{:S(2)}, u32[]{:S(2)}) collective-permute-start(bf16[512,128]{1,0:T(8,128)(2,1)S(1)} %pack_give.1), channel_id=1, source_target_pairs={{0,16},{4,20},{8,24},{12,28},{16,0},{20,4},{24,8},{28,12},{1,17},{... | collective-permute-start | bytes 393224 | tf_op jit(solution)/shard_map/ppermute | solution.py:861
  53.5 3.6 %collective-permute-start.14 = (f32[8,128]{1,0:T(8,128)S(1)}, f32[8,128]{1,0:T(8,128)S(1)}, u32[]{:S(2)}, u32[]{:S(2)}) collective-permute-start(f32[8,128]{1,0:T(8,128)S(1)} %add.13), channel_id=1, source_target_pairs={{0,2},{1,3},{2,0},{3,1},{4,6},{5,7},{6,4},{7,5},{8,10},{9,11},{10,... | collective-permute-start | bytes 12296 | tf_op jit(solution)/shard_map/ppermute | solution.py:938
  58.4 13.9 %collective-permute-start.18 = (bf16[768,128]{1,0:T(8,128)(2,1)S(1)}, bf16[768,128]{1,0:T(8,128)(2,1)S(1)}, u32[]{:S(2)}, u32[]{:S(2)}) collective-permute-start(bf16[768,128]{1,0:T(8,128)(2,1)S(1)} %get-tuple-element.92), channel_id=1, source_target_pairs={{0,4},{4,0},{8,12},{12,8},{16,20},{20,16},{24,28},{28,24},{1,5},{5... | collective-permute-start | bytes 589832 | tf_op jit(solution)/shard_map/ppermute | solution.py:861
  58.9 15.9 %collective-permute-start.19 = (bf16[768,128]{1,0:T(8,128)(2,1)S(1)}, bf16[768,128]{1,0:T(8,128)(2,1)S(1)}, u32[]{:S(2)}, u32[]{:S(2)}) collective-permute-start(bf16[768,128]{1,0:T(8,128)(2,1)S(1)} %get-tuple-element.93), channel_id=1, source_target_pairs={{0,8},{4,12},{8,0},{12,4},{16,24},{20,28},{24,16},{28,20},{1,9},{5... | collective-permute-start | bytes 589832 | tf_op jit(solution)/shard_map/ppermute | solution.py:861
  59.6 15.2 %collective-permute-start.20 = (bf16[768,128]{1,0:T(8,128)(2,1)S(1)}, bf16[768,128]{1,0:T(8,128)(2,1)S(1)}, u32[]{:S(2)}, u32[]{:S(2)}) collective-permute-start(bf16[768,128]{1,0:T(8,128)(2,1)S(1)} %get-tuple-element.94), channel_id=1, source_target_pairs={{0,12},{4,8},{8,4},{12,0},{16,28},{20,24},{24,20},{28,16},{1,13},{... | collective-permute-start | bytes 589832 | tf_op jit(solution)/shard_map/ppermute | solution.py:861
  62.0 1.2 %collective-permute-start.15 = (f32[8,128]{1,0:T(8,128)S(1)}, f32[8,128]{1,0:T(8,128)S(1)}, u32[]{:S(2)}, u32[]{:S(2)}) collective-permute-start(f32[8,128]{1,0:T(8,128)S(1)} %add.14), channel_id=1, source_target_pairs={{0,1},{1,0},{2,3},{3,2},{4,5},{5,4},{6,7},{7,6},{8,9},{9,8},{10,11... | collective-permute-start | bytes 12296 | tf_op jit(solution)/shard_map/ppermute | solution.py:938
  64.4 6.0 %collective-permute-start.16 = (bf16[2,128,128]{2,1,0:T(8,128)(2,1)S(1)}, bf16[2,128,128]{2,1,0:T(8,128)(2,1)S(1)}, u32[]{:S(2)}, u32[]{:S(2)}) collective-permute-start(bf16[2,128,128]{2,1,0:T(8,128)(2,1)S(1)} %get-tuple-element.87), channel_id=1, source_target_pairs={{0,16},{4,20},{8,24},{12,28},{16,0},{20,4},{24,8},{28,12},{1,17},{... | collective-permute-start | bytes 196616 | tf_op jit(solution)/shard_map/ppermute | solution.py:861
  71.3 7.0 %collective-permute-start.21 = (bf16[768,128]{1,0:T(8,128)(2,1)S(1)}, bf16[768,128]{1,0:T(8,128)(2,1)S(1)}, u32[]{:S(2)}, u32[]{:S(2)}) collective-permute-start(bf16[768,128]{1,0:T(8,128)(2,1)S(1)} %get-tuple-element.97), channel_id=1, source_target_pairs={{0,4},{4,0},{8,12},{12,8},{16,20},{20,16},{24,28},{28,24},{1,5},{5... | collective-permute-start | bytes 589832 | tf_op jit(solution)/shard_map/ppermute | solution.py:861
  72.3 7.8 %collective-permute-start.22 = (bf16[768,128]{1,0:T(8,128)(2,1)S(1)}, bf16[768,128]{1,0:T(8,128)(2,1)S(1)}, u32[]{:S(2)}, u32[]{:S(2)}) collective-permute-start(bf16[768,128]{1,0:T(8,128)(2,1)S(1)} %get-tuple-element.98), channel_id=1, source_target_pairs={{0,8},{4,12},{8,0},{12,4},{16,24},{20,28},{24,16},{28,20},{1,9},{5... | collective-permute-start | bytes 589832 | tf_op jit(solution)/shard_map/ppermute | solution.py:861
  72.3 11.2 %collective-permute-start.23 = (bf16[768,128]{1,0:T(8,128)(2,1)S(1)}, bf16[768,128]{1,0:T(8,128)(2,1)S(1)}, u32[]{:S(2)}, u32[]{:S(2)}) collective-permute-start(bf16[768,128]{1,0:T(8,128)(2,1)S(1)} %get-tuple-element.99), channel_id=1, source_target_pairs={{0,12},{4,8},{8,4},{12,0},{16,28},{20,24},{24,20},{28,16},{1,13},{... | collective-permute-start | bytes 589832 | tf_op jit(solution)/shard_map/ppermute | solution.py:861
  (6 other events, 46.2 us)

commit v3 on v2

--- a/solution.py
+++ b/solution.py
@@ -482,7 +482,7 @@
     return joined([line[j] for line in lines], other, True, scale)
 
 
-def soft_first_kernel(half, x_ref, recv_ref, lines_ref, send_ref, rect_ref, scr):
+def soft_first_kernel(half, x_ref, recv_ref, lines_ref, far_ref, send_ref, rect_ref, scr):
     late = later(half)
     tiles, wide, scale = soft_shape(half, x_ref)
     _, same, rect = soft_blocks(half, x_ref, (recv_ref, recv_ref))
@@ -506,7 +506,7 @@
         totals.append(total)
         zeros = [jnp.zeros_like(top)] * tiles
         factor, _ = rect_joined(
-            late, lines_ref, lines_ref, ([top] * tiles, [total] * tiles, zeros), j, wide, scale
+            late, lines_ref, far_ref, ([top] * tiles, [total] * tiles, zeros), j, wide, scale
         )
         for i in range(tiles):
             part = nn((scr[i, j] * factor).astype(jnp.bfloat16), grads(j))
@@ -656,7 +656,7 @@
 
 
 def lin_local_kernel(half, rows, *refs):
-    steps, (x_ref, lines_ref, out_ref, states_ref, give_ref) = refs[:half], refs[half + 1 :]
+    steps, (x_ref, lines_ref, out_ref, states_ref, give_ref) = refs[:half], refs[half:]
     me = place_in(half)
     for step, ref in enumerate(steps):
         x_ref[jnp.bitwise_xor(me, step)] = ref[...]
@@ -829,16 +829,27 @@
         out[pl.ds(3 * rows, 3 * rows), :] = same_ref[span]
 
 
-def call(name, kernel, out_shape, scratch, cost, *args):
+def call(name, kernel, out_shape, scratch, cost, *args, waits=()):
+    count = len(args)
+    places = {}
+    if waits:
+        places["in_specs"] = [pl.BlockSpec(memory_space=pltpu.VMEM)] * count + [
+            pl.BlockSpec(memory_space=pl.ANY)
+        ] * len(waits)
+
+    def body(*refs):
+        kernel(*refs[:count], *refs[count + len(waits) :])
+
     with jax.named_scope(name):
         return pl.pallas_call(
-            kernel,
+            body,
             out_shape=out_shape,
             scratch_shapes=scratch,
             name=name,
             compiler_params=pltpu.CompilerParams(vmem_limit_bytes=VMEM_BYTES[name == "pack_soft"]),
             cost_estimate=pl.CostEstimate(flops=cost, bytes_accessed=1024, transcendentals=0),
-        )(*args)
+            **places,
+        )(*args, *waits)
 
 
 def by_halves(lin_q, lin_k, lin_v, lin_decay, norm_gain, soft_q, soft_k, soft_v, out_grad):
@@ -887,7 +898,7 @@
     far_lines = moved(lines, half)
     dv_give, first_lines = call(
         "soft_first", bind(soft_first_kernel, half), (low(tokens, width), full(8, tokens)),
-        [scores], 13800000000, x, recv, lines,
+        [scores], 13800000000, x, recv, lines, far_lines, waits=lin_got[1:3],
     )
     dv_given = moved(dv_give, half)
     lin_x, lin_lines, local_out, states, state = call(
@@ -899,7 +910,7 @@
             low(2, half, width, width),
             low(2, width, width),
         ),
-        [], 7360000000, *lin_got, first_lines,
+        [], 7360000000, *lin_got, waits=(first_lines,),
     )
     state = moved(state, half)
     rect, rect_lines = call(

time: 85 us -> 84 us (0.988)
    ppermute x4, starting transfers between devices: 4.64 us -> 2.5 us  [by_halves(): lax.ppermute(sums, axis, [(i, i ^ step) for i in range(count)])]
    ppermute x20, starting transfers between devices: 30.1 us -> 31.5 us  [moved(): return lax.ppermute(x, 'ctx', [(i, i ^ step) for i in range(spans)])]
where the time goes in v3:
time: 84 us; the launch traced here: 83.9 us
  starting transfers between devices  34 us (40%)
  waiting for transfers between devices  30.4 us (36%)
  Pallas kernels  18.6 us (22%)
    ppermute x20, starting transfers between devices, moved(): return lax.ppermute(x, 'ctx', [(i, i ^ step) for i in range(spans)])  31.5 us
    ppermute x20, waiting for transfers between devices, moved(): return lax.ppermute(x, 'ctx', [(i, i ^ step) for i in range(spans)])  24.5 us
    pallas_call x18, Pallas kernels, call(): pl.pallas_call(body, out_shape=out_shape, scratch_shapes=scratch, name=na...  18.6 us
    ppermute x4, waiting for transfers between devices, by_halves(): lax.ppermute(sums, axis, [(i, i ^ step) for i in range(count)])  5.96 us
    ppermute x4, starting transfers between devices, by_halves(): lax.ppermute(sums, axis, [(i, i ^ step) for i in range(count)])  2.5 us
  transfers between devices with their start and end apart: 24, of which 14 were waited for; matrix products, arithmetic and copies ran while one was open for 0% of the time, Pallas kernels for 16%

profile of v3, /device:TPU:0, one launch (start us, length us, event | category | flops | bytes accessed | tf_op | source)
XLA Modules:
  0.0 83.9 jit_solution(17183965160344298920)
XLA Ops:
  0.7 2.6 %pack_soft.1 = (bf16[1024,128]{1,0:T(8,128)(2,1)}, bf16[1024,128]{1,0:T(8,128)(2,1)}, bf16[1024,128]{1,0:T(8,128)(2,1)}, bf16[1024,128]{1,0:T(8,128)(2,1)}) custom-call(bf16[128,8,128]{2,1,0:T(8,128)(2,1)} %refs_0_.3, bf16[128,8,128]{2,1,0:T(8,128)(2,1)} %refs_1_.3, bf16[128,8,128]{2,1,0:T(8,128)(2,1)} %refs_2_.3, bf16[128,8,128]{2,1,0:T(8,128)(2,1)} %refs_3_.3), custom_call_target="tpu_custom_call" | custom-call | flops 11960000512 | bytes 1024 | tf_op jit(solution)/shard_map/pack_soft/pack_soft/pallas_call | solution.py:844
  3.2 3.0 %collective-permute-start.3 = (bf16[1024,128]{1,0:T(8,128)(2,1)}, bf16[1024,128]{1,0:T(8,128)(2,1)S(1)}, u32[]{:S(2)}, u32[]{:S(2)}) collective-permute-start(bf16[1024,128]{1,0:T(8,128)(2,1)} %get-tuple-element.61), channel_id=1, source_target_pairs={{0,4},{4,0},{8,12},{12,8},{16,20},{20,16},{24,28},{28,24},{1,5},{5... | collective-permute-start | bytes 786440 | tf_op jit(solution)/shard_map/ppermute | solution.py:872
  6.2 1.6 %collective-permute-start.4 = (bf16[1024,128]{1,0:T(8,128)(2,1)}, bf16[1024,128]{1,0:T(8,128)(2,1)S(1)}, u32[]{:S(2)}, u32[]{:S(2)}) collective-permute-start(bf16[1024,128]{1,0:T(8,128)(2,1)} %get-tuple-element.62), channel_id=1, source_target_pairs={{0,8},{4,12},{8,0},{12,4},{16,24},{20,28},{24,16},{28,20},{1,9},{5... | collective-permute-start | bytes 786440 | tf_op jit(solution)/shard_map/ppermute | solution.py:872
  8.2 2.0 %collective-permute-start = (bf16[800,128]{1,0:T(8,128)(2,1)S(1)}, bf16[800,128]{1,0:T(8,128)(2,1)S(1)}, u32[]{:S(2)}, u32[]{:S(2)}) collective-permute-start(bf16[800,128]{1,0:T(8,128)(2,1)S(1)} %get-tuple-element.57), channel_id=1, source_target_pairs={{0,4},{4,0},{8,12},{12,8},{16,20},{20,16},{24,28},{28,24},{1,5},{5... | collective-permute-start | bytes 614408 | tf_op jit(solution)/shard_map/ppermute | solution.py:872
  10.2 1.6 %collective-permute-start.1 = (bf16[800,128]{1,0:T(8,128)(2,1)S(1)}, bf16[800,128]{1,0:T(8,128)(2,1)S(1)}, u32[]{:S(2)}, u32[]{:S(2)}) collective-permute-start(bf16[800,128]{1,0:T(8,128)(2,1)S(1)} %get-tuple-element.58), channel_id=1, source_target_pairs={{0,8},{4,12},{8,0},{12,4},{16,24},{20,28},{24,16},{28,20},{1,9},{5... | collective-permute-start | bytes 614408 | tf_op jit(solution)/shard_map/ppermute | solution.py:872
  11.8 2.5 %collective-permute-done.3.refs_1_ = bf16[1024,128]{1,0:T(8,128)(2,1)S(1)} collective-permute-done((bf16[1024,128]{1,0:T(8,128)(2,1)}, bf16[1024,128]{1,0:T(8,128)(2,1)S(1)}, u32[]{:S(2)}, u32[]{:S(2)}) %collective-permute-start.3) | collective-permute-done | bytes 262176 | tf_op jit(solution)/shard_map/ppermute | solution.py:872
  15.7 5.1 %collective-permute-done.5.refs_3_ = bf16[1024,128]{1,0:T(8,128)(2,1)S(1)} collective-permute-done((bf16[1024,128]{1,0:T(8,128)(2,1)}, bf16[1024,128]{1,0:T(8,128)(2,1)S(1)}, u32[]{:S(2)}, u32[]{:S(2)}) %collective-permute-start.5) | collective-permute-done | bytes 262176 | tf_op jit(solution)/shard_map/ppermute | solution.py:872
  20.9 3.1 %collective-permute-start.6 = (bf16[4,128,128]{2,1,0:T(8,128)(2,1)S(1)}, bf16[4,128,128]{2,1,0:T(8,128)(2,1)S(1)}, u32[]{:S(2)}, u32[]{:S(2)}) collective-permute-start(bf16[4,128,128]{2,1,0:T(8,128)(2,1)S(1)} %get-tuple-element.65), channel_id=1, source_target_pairs={{0,16},{4,20},{8,24},{12,28},{16,0},{20,4},{24,8},{28,12},{1,17},{... | collective-permute-start | bytes 393224 | tf_op jit(solution)/shard_map/ppermute | solution.py:872
  25.3 2.9 %collective-permute-start.2 = (bf16[800,128]{1,0:T(8,128)(2,1)S(1)}, bf16[800,128]{1,0:T(8,128)(2,1)S(1)}, u32[]{:S(2)}, u32[]{:S(2)}) collective-permute-start(bf16[800,128]{1,0:T(8,128)(2,1)S(1)} %get-tuple-element.59), channel_id=1, source_target_pairs={{0,12},{4,8},{8,4},{12,0},{16,28},{20,24},{24,20},{28,16},{1,13},{... | collective-permute-start | bytes 614408 | tf_op jit(solution)/shard_map/ppermute | solution.py:872
  28.2 2.6 %collective-permute-start.9 = (bf16[4,128,128]{2,1,0:T(8,128)(2,1)S(1)}, bf16[4,128,128]{2,1,0:T(8,128)(2,1)S(1)}, u32[]{:S(2)}, u32[]{:S(2)}) collective-permute-start(bf16[4,128,128]{2,1,0:T(8,128)(2,1)S(1)} %get-tuple-element.71), channel_id=1, source_target_pairs={{0,16},{4,20},{8,24},{12,28},{16,0},{20,4},{24,8},{28,12},{1,17},{... | collective-permute-start | bytes 393224 | tf_op jit(solution)/shard_map/ppermute | solution.py:872
  32.7 1.6 %collective-permute-done.2.refs_3_ = bf16[800,128]{1,0:T(8,128)(2,1)S(1)} collective-permute-done((bf16[800,128]{1,0:T(8,128)(2,1)S(1)}, bf16[800,128]{1,0:T(8,128)(2,1)S(1)}, u32[]{:S(2)}, u32[]{:S(2)}) %collective-permute-start.2) | collective-permute-done | bytes 204832 | tf_op jit(solution)/shard_map/ppermute | solution.py:872
  34.3 1.6 %lin_local.1 = (bf16[4,800,128]{2,1,0:T(8,128)(2,1)S(1)}, f32[8,128]{1,0:T(8,128)S(1)}, f32[2,4,128,128]{3,2,1,0:T(8,128)S(1)}, bf16[2,4,128,128]{3,2,1,0:T(8,128)(2,1)S(1)}, bf16[2,128,128]{2,1,0:T(8,128)(2,1)S(1)}) custom-call(bf16[800,128]{1,0:T(8,128)(2,1)S(1)} %get-tuple-element.56.refs_0_, bf16[800,128]{1,0:T(8,128)(2,1)S(1)} %collective-permute-done.refs_4_.refs_1_, ...), custom_call_target="tpu_custom_call" | custom-call | flops 7360000000 | bytes 1024 | tf_op jit(solution)/shard_map/lin_local/lin_local/pallas_call | solution.py:844
  35.8 2.9 %collective-permute-start.10 = (bf16[2,128,128]{2,1,0:T(8,128)(2,1)S(1)}, bf16[2,128,128]{2,1,0:T(8,128)(2,1)S(1)}, u32[]{:S(2)}, u32[]{:S(2)}) collective-permute-start(bf16[2,128,128]{2,1,0:T(8,128)(2,1)S(1)} %get-tuple-element.76), channel_id=1, source_target_pairs={{0,16},{4,20},{8,24},{12,28},{16,0},{20,4},{24,8},{28,12},{1,17},{... | collective-permute-start | bytes 196616 | tf_op jit(solution)/shard_map/ppermute | solution.py:872
  38.7 2.3 %collective-permute-done.9.refs_2_ = bf16[4,128,128]{2,1,0:T(8,128)(2,1)S(1)} collective-permute-done((bf16[4,128,128]{2,1,0:T(8,128)(2,1)S(1)}, bf16[4,128,128]{2,1,0:T(8,128)(2,1)S(1)}, u32[]{:S(2)}, u32[]{:S(2)}) %collective-permute-start.9) | collective-permute-done | bytes 131104 | tf_op jit(solution)/shard_map/ppermute | solution.py:872
  41.0 1.8 %soft_rect.1 = (f32[3,512,128]{2,1,0:T(8,128)S(1)}, f32[8,512]{1,0:T(8,128)S(1)}) custom-call(bf16[4,1024,128]{2,1,0:T(8,128)(2,1)S(1)} %get-tuple-element.64.refs_0_.refs_2_, bf16[4,128,128]{2,1,0:T(8,128)(2,1)S(1)} %collective-permute-done.6.refs_1_, bf16[4,128,128]{2,1,0:T(8,128)(2,1)S(1)} %collective-permute-done.9.refs_2_, ...), custom_call_target="tpu_custom_call" | custom-call | flops 9200000000 | bytes 1024 | tf_op jit(solution)/shard_map/soft_rect/soft_rect/pallas_call | solution.py:844
  46.5 2.4 %collective-permute-done.12 = f32[8,128]{1,0:T(8,128)S(1)} collective-permute-done((f32[8,128]{1,0:T(8,128)S(1)}, f32[8,128]{1,0:T(8,128)S(1)}, u32[]{:S(2)}, u32[]{:S(2)}) %collective-permute-start.12) | collective-permute-done | bytes 4128 | tf_op jit(solution)/shard_map/ppermute | solution.py:949
  49.8 2.1 %collective-permute-start.11 = (bf16[512,128]{1,0:T(8,128)(2,1)S(1)}, bf16[512,128]{1,0:T(8,128)(2,1)S(1)}, u32[]{:S(2)}, u32[]{:S(2)}) collective-permute-start(bf16[512,128]{1,0:T(8,128)(2,1)S(1)} %pack_give.1), channel_id=1, source_target_pairs={{0,16},{4,20},{8,24},{12,28},{16,0},{20,4},{24,8},{28,12},{1,17},{... | collective-permute-start | bytes 393224 | tf_op jit(solution)/shard_map/ppermute | solution.py:872
  58.9 1.9 %collective-permute-start.20 = (bf16[768,128]{1,0:T(8,128)(2,1)S(1)}, bf16[768,128]{1,0:T(8,128)(2,1)S(1)}, u32[]{:S(2)}, u32[]{:S(2)}) collective-permute-start(bf16[768,128]{1,0:T(8,128)(2,1)S(1)} %get-tuple-element.94), channel_id=1, source_target_pairs={{0,12},{4,8},{8,4},{12,0},{16,28},{20,24},{24,20},{28,16},{1,13},{... | collective-permute-start | bytes 589832 | tf_op jit(solution)/shard_map/ppermute | solution.py:872
  63.9 1.9 %lin_own.1 = (bf16[2,4,128,128]{3,2,1,0:T(8,128)(2,1)S(1)}, f32[2,2,4,128,128]{4,3,2,1,0:T(8,128)S(1)}) custom-call(bf16[4,800,128]{2,1,0:T(8,128)(2,1)S(1)} %get-tuple-element.68.refs_0_, f32[8,128]{1,0:T(8,128)S(1)} %get-tuple-element.69.refs_1_, bf16[2,4,128,128]{3,2,1,0:T(8,128)(2,1)S(1)} %get-tuple-element.83.refs_2_, ...), custom_call_target="tpu_custom_call" | custom-call | flops 1024 | bytes 1024 | tf_op jit(solution)/shard_map/lin_own/lin_own/pallas_call | solution.py:844
  65.8 3.7 %collective-permute-done.16.refs_4_ = bf16[2,128,128]{2,1,0:T(8,128)(2,1)S(1)} collective-permute-done((bf16[2,128,128]{2,1,0:T(8,128)(2,1)S(1)}, bf16[2,128,128]{2,1,0:T(8,128)(2,1)S(1)}, u32[]{:S(2)}, u32[]{:S(2)}) %collective-permute-start.16) | collective-permute-done | bytes 65568 | tf_op jit(solution)/shard_map/ppermute | solution.py:872
  71.7 2.3 %collective-permute-start.23 = (bf16[768,128]{1,0:T(8,128)(2,1)S(1)}, bf16[768,128]{1,0:T(8,128)(2,1)S(1)}, u32[]{:S(2)}, u32[]{:S(2)}) collective-permute-start(bf16[768,128]{1,0:T(8,128)(2,1)S(1)} %get-tuple-element.99), channel_id=1, source_target_pairs={{0,12},{4,8},{8,4},{12,0},{16,28},{20,24},{24,20},{28,16},{1,13},{... | collective-permute-start | bytes 589832 | tf_op jit(solution)/shard_map/ppermute | solution.py:872
  75.3 2.1 %collective-permute-done.21.refs_1_ = bf16[768,128]{1,0:T(8,128)(2,1)S(1)} collective-permute-done((bf16[768,128]{1,0:T(8,128)(2,1)S(1)}, bf16[768,128]{1,0:T(8,128)(2,1)S(1)}, u32[]{:S(2)}, u32[]{:S(2)}) %collective-permute-start.21) | collective-permute-done | bytes 196640 | tf_op jit(solution)/shard_map/ppermute | solution.py:872
  77.4 2.1 %collective-permute-done.22.refs_2_ = bf16[768,128]{1,0:T(8,128)(2,1)S(1)} collective-permute-done((bf16[768,128]{1,0:T(8,128)(2,1)S(1)}, bf16[768,128]{1,0:T(8,128)(2,1)S(1)}, u32[]{:S(2)}, u32[]{:S(2)}) %collective-permute-start.22) | collective-permute-done | bytes 196640 | tf_op jit(solution)/shard_map/ppermute | solution.py:872
  79.5 3.1 %collective-permute-done.23.refs_3_ = bf16[768,128]{1,0:T(8,128)(2,1)S(1)} collective-permute-done((bf16[768,128]{1,0:T(8,128)(2,1)S(1)}, bf16[768,128]{1,0:T(8,128)(2,1)S(1)}, u32[]{:S(2)}, u32[]{:S(2)}) %collective-permute-start.23) | collective-permute-done | bytes 196640 | tf_op jit(solution)/shard_map/ppermute | solution.py:872
  (58 shorter events, 24.4 us)
Async XLA Ops:
  3.2 11.0 %collective-permute-start.3 = (bf16[1024,128]{1,0:T(8,128)(2,1)}, bf16[1024,128]{1,0:T(8,128)(2,1)S(1)}, u32[]{:S(2)}, u32[]{:S(2)}) collective-permute-start(bf16[1024,128]{1,0:T(8,128)(2,1)} %get-tuple-element.61), channel_id=1, source_target_pairs={{0,4},{4,0},{8,12},{12,8},{16,20},{20,16},{24,28},{28,24},{1,5},{5... | collective-permute-start | bytes 786440 | tf_op jit(solution)/shard_map/ppermute | solution.py:872
  6.2 9.4 %collective-permute-start.4 = (bf16[1024,128]{1,0:T(8,128)(2,1)}, bf16[1024,128]{1,0:T(8,128)(2,1)S(1)}, u32[]{:S(2)}, u32[]{:S(2)}) collective-permute-start(bf16[1024,128]{1,0:T(8,128)(2,1)} %get-tuple-element.62), channel_id=1, source_target_pairs={{0,8},{4,12},{8,0},{12,4},{16,24},{20,28},{24,16},{28,20},{1,9},{5... | collective-permute-start | bytes 786440 | tf_op jit(solution)/shard_map/ppermute | solution.py:872
  7.8 13.0 %collective-permute-start.5 = (bf16[1024,128]{1,0:T(8,128)(2,1)}, bf16[1024,128]{1,0:T(8,128)(2,1)S(1)}, u32[]{:S(2)}, u32[]{:S(2)}) collective-permute-start(bf16[1024,128]{1,0:T(8,128)(2,1)} %get-tuple-element.63), channel_id=1, source_target_pairs={{0,12},{4,8},{8,4},{12,0},{16,28},{20,24},{24,20},{28,16},{1,13},{... | collective-permute-start | bytes 786440 | tf_op jit(solution)/shard_map/ppermute | solution.py:872
  8.2 20.0 %collective-permute-start = (bf16[800,128]{1,0:T(8,128)(2,1)S(1)}, bf16[800,128]{1,0:T(8,128)(2,1)S(1)}, u32[]{:S(2)}, u32[]{:S(2)}) collective-permute-start(bf16[800,128]{1,0:T(8,128)(2,1)S(1)} %get-tuple-element.57), channel_id=1, source_target_pairs={{0,4},{4,0},{8,12},{12,8},{16,20},{20,16},{24,28},{28,24},{1,5},{5... | collective-permute-start | bytes 614408 | tf_op jit(solution)/shard_map/ppermute | solution.py:872
  10.2 20.6 %collective-permute-start.1 = (bf16[800,128]{1,0:T(8,128)(2,1)S(1)}, bf16[800,128]{1,0:T(8,128)(2,1)S(1)}, u32[]{:S(2)}, u32[]{:S(2)}) collective-permute-start(bf16[800,128]{1,0:T(8,128)(2,1)S(1)} %get-tuple-element.58), channel_id=1, source_target_pairs={{0,8},{4,12},{8,0},{12,4},{16,24},{20,28},{24,16},{28,20},{1,9},{5... | collective-permute-start | bytes 614408 | tf_op jit(solution)/shard_map/ppermute | solution.py:872
  20.9 9.9 %collective-permute-start.6 = (bf16[4,128,128]{2,1,0:T(8,128)(2,1)S(1)}, bf16[4,128,128]{2,1,0:T(8,128)(2,1)S(1)}, u32[]{:S(2)}, u32[]{:S(2)}) collective-permute-start(bf16[4,128,128]{2,1,0:T(8,128)(2,1)S(1)} %get-tuple-element.65), channel_id=1, source_target_pairs={{0,16},{4,20},{8,24},{12,28},{16,0},{20,4},{24,8},{28,12},{1,17},{... | collective-permute-start | bytes 393224 | tf_op jit(solution)/shard_map/ppermute | solution.py:872
  25.2 5.5 %collective-permute-start.7 = (f32[8,512]{1,0:T(8,128)S(1)}, f32[8,512]{1,0:T(8,128)S(1)}, u32[]{:S(2)}, u32[]{:S(2)}) collective-permute-start(f32[8,512]{1,0:T(8,128)S(1)} %get-tuple-element.66.refs_2_.refs_1_.refs_3_), channel_id=1, source_target_pairs={{0,16},{4,20},{8,24},{12,28},{16,0},{20,4},{24,8},{28,12},{1,17},{... | collective-permute-start | bytes 49160 | tf_op jit(solution)/shard_map/ppermute | solution.py:872
  25.3 9.0 %collective-permute-start.2 = (bf16[800,128]{1,0:T(8,128)(2,1)S(1)}, bf16[800,128]{1,0:T(8,128)(2,1)S(1)}, u32[]{:S(2)}, u32[]{:S(2)}) collective-permute-start(bf16[800,128]{1,0:T(8,128)(2,1)S(1)} %get-tuple-element.59), channel_id=1, source_target_pairs={{0,12},{4,8},{8,4},{12,0},{16,28},{20,24},{24,20},{28,16},{1,13},{... | collective-permute-start | bytes 614408 | tf_op jit(solution)/shard_map/ppermute | solution.py:872
  28.2 12.8 %collective-permute-start.9 = (bf16[4,128,128]{2,1,0:T(8,128)(2,1)S(1)}, bf16[4,128,128]{2,1,0:T(8,128)(2,1)S(1)}, u32[]{:S(2)}, u32[]{:S(2)}) collective-permute-start(bf16[4,128,128]{2,1,0:T(8,128)(2,1)S(1)} %get-tuple-element.71), channel_id=1, source_target_pairs={{0,16},{4,20},{8,24},{12,28},{16,0},{20,4},{24,8},{28,12},{1,17},{... | collective-permute-start | bytes 393224 | tf_op jit(solution)/shard_map/ppermute | solution.py:872
  31.7 12.0 %collective-permute-start.8 = (bf16[512,128]{1,0:T(8,128)(2,1)S(1)}, bf16[512,128]{1,0:T(8,128)(2,1)S(1)}, u32[]{:S(2)}, u32[]{:S(2)}) collective-permute-start(bf16[512,128]{1,0:T(8,128)(2,1)S(1)} %get-tuple-element.70), channel_id=1, source_target_pairs={{0,16},{4,20},{8,24},{12,28},{16,0},{20,4},{24,8},{28,12},{1,17},{... | collective-permute-start | bytes 393224 | tf_op jit(solution)/shard_map/ppermute | solution.py:872
  35.8 8.5 %collective-permute-start.10 = (bf16[2,128,128]{2,1,0:T(8,128)(2,1)S(1)}, bf16[2,128,128]{2,1,0:T(8,128)(2,1)S(1)}, u32[]{:S(2)}, u32[]{:S(2)}) collective-permute-start(bf16[2,128,128]{2,1,0:T(8,128)(2,1)S(1)} %get-tuple-element.76), channel_id=1, source_target_pairs={{0,16},{4,20},{8,24},{12,28},{16,0},{20,4},{24,8},{28,12},{1,17},{... | collective-permute-start | bytes 196616 | tf_op jit(solution)/shard_map/ppermute | solution.py:872
  45.3 3.7 %collective-permute-start.12 = (f32[8,128]{1,0:T(8,128)S(1)}, f32[8,128]{1,0:T(8,128)S(1)}, u32[]{:S(2)}, u32[]{:S(2)}) collective-permute-start(f32[8,128]{1,0:T(8,128)S(1)} %get-tuple-element.81), channel_id=1, source_target_pairs={{0,4},{4,0},{8,12},{12,8},{16,20},{20,16},{24,28},{28,24},{1,5},{5... | collective-permute-start | bytes 12296 | tf_op jit(solution)/shard_map/ppermute | solution.py:949
  45.5 9.0 %collective-permute-start.17 = (f32[8,512]{1,0:T(8,128)S(1)}, f32[8,512]{1,0:T(8,128)S(1)}, u32[]{:S(2)}, u32[]{:S(2)}) collective-permute-start(f32[8,512]{1,0:T(8,128)S(1)} %get-tuple-element.72.refs_2_), channel_id=1, source_target_pairs={{0,16},{4,20},{8,24},{12,28},{16,0},{20,4},{24,8},{28,12},{1,17},{... | collective-permute-start | bytes 49160 | tf_op jit(solution)/shard_map/ppermute | solution.py:872
  49.0 4.0 %collective-permute-start.13 = (f32[8,128]{1,0:T(8,128)S(1)}, f32[8,128]{1,0:T(8,128)S(1)}, u32[]{:S(2)}, u32[]{:S(2)}) collective-permute-start(f32[8,128]{1,0:T(8,128)S(1)} %add.12), channel_id=1, source_target_pairs={{0,8},{4,12},{8,0},{12,4},{16,24},{20,28},{24,16},{28,20},{1,9},{5... | collective-permute-start | bytes 12296 | tf_op jit(solution)/shard_map/ppermute | solution.py:949
  49.8 7.3 %collective-permute-start.11 = (bf16[512,128]{1,0:T(8,128)(2,1)S(1)}, bf16[512,128]{1,0:T(8,128)(2,1)S(1)}, u32[]{:S(2)}, u32[]{:S(2)}) collective-permute-start(bf16[512,128]{1,0:T(8,128)(2,1)S(1)} %pack_give.1), channel_id=1, source_target_pairs={{0,16},{4,20},{8,24},{12,28},{16,0},{20,4},{24,8},{28,12},{1,17},{... | collective-permute-start | bytes 393224 | tf_op jit(solution)/shard_map/ppermute | solution.py:872
  53.0 3.6 %collective-permute-start.14 = (f32[8,128]{1,0:T(8,128)S(1)}, f32[8,128]{1,0:T(8,128)S(1)}, u32[]{:S(2)}, u32[]{:S(2)}) collective-permute-start(f32[8,128]{1,0:T(8,128)S(1)} %add.13), channel_id=1, source_target_pairs={{0,2},{1,3},{2,0},{3,1},{4,6},{5,7},{6,4},{7,5},{8,10},{9,11},{10,... | collective-permute-start | bytes 12296 | tf_op jit(solution)/shard_map/ppermute | solution.py:949
  57.3 14.4 %collective-permute-start.18 = (bf16[768,128]{1,0:T(8,128)(2,1)S(1)}, bf16[768,128]{1,0:T(8,128)(2,1)S(1)}, u32[]{:S(2)}, u32[]{:S(2)}) collective-permute-start(bf16[768,128]{1,0:T(8,128)(2,1)S(1)} %get-tuple-element.92), channel_id=1, source_target_pairs={{0,4},{4,0},{8,12},{12,8},{16,20},{20,16},{24,28},{28,24},{1,5},{5... | collective-permute-start | bytes 589832 | tf_op jit(solution)/shard_map/ppermute | solution.py:872
  58.5 15.5 %collective-permute-start.19 = (bf16[768,128]{1,0:T(8,128)(2,1)S(1)}, bf16[768,128]{1,0:T(8,128)(2,1)S(1)}, u32[]{:S(2)}, u32[]{:S(2)}) collective-permute-start(bf16[768,128]{1,0:T(8,128)(2,1)S(1)} %get-tuple-element.93), channel_id=1, source_target_pairs={{0,8},{4,12},{8,0},{12,4},{16,24},{20,28},{24,16},{28,20},{1,9},{5... | collective-permute-start | bytes 589832 | tf_op jit(solution)/shard_map/ppermute | solution.py:872
  58.9 15.1 %collective-permute-start.20 = (bf16[768,128]{1,0:T(8,128)(2,1)S(1)}, bf16[768,128]{1,0:T(8,128)(2,1)S(1)}, u32[]{:S(2)}, u32[]{:S(2)}) collective-permute-start(bf16[768,128]{1,0:T(8,128)(2,1)S(1)} %get-tuple-element.94), channel_id=1, source_target_pairs={{0,12},{4,8},{8,4},{12,0},{16,28},{20,24},{24,20},{28,16},{1,13},{... | collective-permute-start | bytes 589832 | tf_op jit(solution)/shard_map/ppermute | solution.py:872
  60.8 1.2 %collective-permute-start.15 = (f32[8,128]{1,0:T(8,128)S(1)}, f32[8,128]{1,0:T(8,128)S(1)}, u32[]{:S(2)}, u32[]{:S(2)}) collective-permute-start(f32[8,128]{1,0:T(8,128)S(1)} %add.14), channel_id=1, source_target_pairs={{0,1},{1,0},{2,3},{3,2},{4,5},{5,4},{6,7},{7,6},{8,9},{9,8},{10,11... | collective-permute-start | bytes 12296 | tf_op jit(solution)/shard_map/ppermute | solution.py:949
  63.2 6.3 %collective-permute-start.16 = (bf16[2,128,128]{2,1,0:T(8,128)(2,1)S(1)}, bf16[2,128,128]{2,1,0:T(8,128)(2,1)S(1)}, u32[]{:S(2)}, u32[]{:S(2)}) collective-permute-start(bf16[2,128,128]{2,1,0:T(8,128)(2,1)S(1)} %get-tuple-element.87), channel_id=1, source_target_pairs={{0,16},{4,20},{8,24},{12,28},{16,0},{20,4},{24,8},{28,12},{1,17},{... | collective-permute-start | bytes 196616 | tf_op jit(solution)/shard_map/ppermute | solution.py:872
  70.4 7.0 %collective-permute-start.21 = (bf16[768,128]{1,0:T(8,128)(2,1)S(1)}, bf16[768,128]{1,0:T(8,128)(2,1)S(1)}, u32[]{:S(2)}, u32[]{:S(2)}) collective-permute-start(bf16[768,128]{1,0:T(8,128)(2,1)S(1)} %get-tuple-element.97), channel_id=1, source_target_pairs={{0,4},{4,0},{8,12},{12,8},{16,20},{20,16},{24,28},{28,24},{1,5},{5... | collective-permute-start | bytes 589832 | tf_op jit(solution)/shard_map/ppermute | solution.py:872
  71.7 7.8 %collective-permute-start.22 = (bf16[768,128]{1,0:T(8,128)(2,1)S(1)}, bf16[768,128]{1,0:T(8,128)(2,1)S(1)}, u32[]{:S(2)}, u32[]{:S(2)}) collective-permute-start(bf16[768,128]{1,0:T(8,128)(2,1)S(1)} %get-tuple-element.98), channel_id=1, source_target_pairs={{0,8},{4,12},{8,0},{12,4},{16,24},{20,28},{24,16},{28,20},{1,9},{5... | collective-permute-start | bytes 589832 | tf_op jit(solution)/shard_map/ppermute | solution.py:872
  71.7 10.9 %collective-permute-start.23 = (bf16[768,128]{1,0:T(8,128)(2,1)S(1)}, bf16[768,128]{1,0:T(8,128)(2,1)S(1)}, u32[]{:S(2)}, u32[]{:S(2)}) collective-permute-start(bf16[768,128]{1,0:T(8,128)(2,1)S(1)} %get-tuple-element.99), channel_id=1, source_target_pairs={{0,12},{4,8},{8,4},{12,0},{16,28},{20,24},{24,20},{28,16},{1,13},{... | collective-permute-start | bytes 589832 | tf_op jit(solution)/shard_map/ppermute | solution.py:872
  (6 other events, 46.2 us)

commit v4 on v3

--- a/solution.py
+++ b/solution.py
@@ -322,7 +322,7 @@
 
 
 def unpack_kernel(half, *refs):
-    steps, outs, scratch = refs[:half], refs[half:-1], refs[-1]
+    steps, outs, scratch = refs[:half][::-1], refs[half:-1], refs[-1]
     late, me = later(half), place_in(half)
     rows, heads, width = outs[0].shape
     for place, out in enumerate(outs):
@@ -969,9 +969,9 @@
         lin_x, lin_lines, lin_dq, lin_made, late_state,
     )
     lin_back = exchanged(lin_made)
-    soft_out = list(call("unpack_soft", bind(unpack_kernel, half), mine, [turned], 5060000000, *early))
+    soft_out = list(call("unpack_soft", bind(unpack_kernel, half), mine, [turned], 5060000000, *early[::-1]))
     lin_back[0], soft_out[0] = after((lin_back[0], soft_out[0]))
-    lin_out = call("unpack_lin", bind(unpack_kernel, half), mine, [turned], COST, *lin_back)
+    lin_out = call("unpack_lin", bind(unpack_kernel, half), mine, [turned], COST, *lin_back[::-1])
     return (*lin_out, *soft_out)
 
 

time: 84 us -> 83.7 us (level)
  transfers between devices with their start and end apart: 24 -> 24, of which waited for: 14 -> 13; matrix products, arithmetic and copies ran while one was open for 0% -> 0% of each run, Pallas kernels for 16% -> 16%
where the time goes in v4:
time: 83.7 us; the launch traced here: 83.5 us
  starting transfers between devices  34.4 us (41%)
  waiting for transfers between devices  29.7 us (35%)
  Pallas kernels  18.6 us (22%)
    ppermute x20, starting transfers between devices, moved(): return lax.ppermute(x, 'ctx', [(i, i ^ step) for i in range(spans)])  31.9 us
    ppermute x20, waiting for transfers between devices, moved(): return lax.ppermute(x, 'ctx', [(i, i ^ step) for i in range(spans)])  23.7 us
    pallas_call x18, Pallas kernels, call(): pl.pallas_call(body, out_shape=out_shape, scratch_shapes=scratch, name=na...  18.6 us
    ppermute x4, waiting for transfers between devices, by_halves(): lax.ppermute(sums, axis, [(i, i ^ step) for i in range(count)])  5.96 us
    ppermute x4, starting transfers between devices, by_halves(): lax.ppermute(sums, axis, [(i, i ^ step) for i in range(count)])  2.5 us
  transfers between devices with their start and end apart: 24, of which 13 were waited for; matrix products, arithmetic and copies ran while one was open for 0% of the time, Pallas kernels for 16%

profile of v4, /device:TPU:0, one launch (start us, length us, event | category | flops | bytes accessed | tf_op | source)
XLA Modules:
  0.0 83.5 jit_solution(8435170153395681587)
XLA Ops:
  0.7 2.6 %pack_soft.1 = (bf16[1024,128]{1,0:T(8,128)(2,1)}, bf16[1024,128]{1,0:T(8,128)(2,1)}, bf16[1024,128]{1,0:T(8,128)(2,1)}, bf16[1024,128]{1,0:T(8,128)(2,1)}) custom-call(bf16[128,8,128]{2,1,0:T(8,128)(2,1)} %refs_0_.3, bf16[128,8,128]{2,1,0:T(8,128)(2,1)} %refs_1_.3, bf16[128,8,128]{2,1,0:T(8,128)(2,1)} %refs_2_.3, bf16[128,8,128]{2,1,0:T(8,128)(2,1)} %refs_3_.3), custom_call_target="tpu_custom_call" | custom-call | flops 11960000512 | bytes 1024 | tf_op jit(solution)/shard_map/pack_soft/pack_soft/pallas_call | solution.py:844
  3.2 3.0 %collective-permute-start.3 = (bf16[1024,128]{1,0:T(8,128)(2,1)}, bf16[1024,128]{1,0:T(8,128)(2,1)S(1)}, u32[]{:S(2)}, u32[]{:S(2)}) collective-permute-start(bf16[1024,128]{1,0:T(8,128)(2,1)} %get-tuple-element.61), channel_id=1, source_target_pairs={{0,4},{4,0},{8,12},{12,8},{16,20},{20,16},{24,28},{28,24},{1,5},{5... | collective-permute-start | bytes 786440 | tf_op jit(solution)/shard_map/ppermute | solution.py:872
  6.2 1.6 %collective-permute-start.4 = (bf16[1024,128]{1,0:T(8,128)(2,1)}, bf16[1024,128]{1,0:T(8,128)(2,1)S(1)}, u32[]{:S(2)}, u32[]{:S(2)}) collective-permute-start(bf16[1024,128]{1,0:T(8,128)(2,1)} %get-tuple-element.62), channel_id=1, source_target_pairs={{0,8},{4,12},{8,0},{12,4},{16,24},{20,28},{24,16},{28,20},{1,9},{5... | collective-permute-start | bytes 786440 | tf_op jit(solution)/shard_map/ppermute | solution.py:872
  8.2 2.0 %collective-permute-start = (bf16[800,128]{1,0:T(8,128)(2,1)S(1)}, bf16[800,128]{1,0:T(8,128)(2,1)S(1)}, u32[]{:S(2)}, u32[]{:S(2)}) collective-permute-start(bf16[800,128]{1,0:T(8,128)(2,1)S(1)} %get-tuple-element.57), channel_id=1, source_target_pairs={{0,4},{4,0},{8,12},{12,8},{16,20},{20,16},{24,28},{28,24},{1,5},{5... | collective-permute-start | bytes 614408 | tf_op jit(solution)/shard_map/ppermute | solution.py:872
  10.2 1.6 %collective-permute-start.1 = (bf16[800,128]{1,0:T(8,128)(2,1)S(1)}, bf16[800,128]{1,0:T(8,128)(2,1)S(1)}, u32[]{:S(2)}, u32[]{:S(2)}) collective-permute-start(bf16[800,128]{1,0:T(8,128)(2,1)S(1)} %get-tuple-element.58), channel_id=1, source_target_pairs={{0,8},{4,12},{8,0},{12,4},{16,24},{20,28},{24,16},{28,20},{1,9},{5... | collective-permute-start | bytes 614408 | tf_op jit(solution)/shard_map/ppermute | solution.py:872
  11.8 2.5 %collective-permute-done.3.refs_1_ = bf16[1024,128]{1,0:T(8,128)(2,1)S(1)} collective-permute-done((bf16[1024,128]{1,0:T(8,128)(2,1)}, bf16[1024,128]{1,0:T(8,128)(2,1)S(1)}, u32[]{:S(2)}, u32[]{:S(2)}) %collective-permute-start.3) | collective-permute-done | bytes 262176 | tf_op jit(solution)/shard_map/ppermute | solution.py:872
  15.7 5.1 %collective-permute-done.5.refs_3_ = bf16[1024,128]{1,0:T(8,128)(2,1)S(1)} collective-permute-done((bf16[1024,128]{1,0:T(8,128)(2,1)}, bf16[1024,128]{1,0:T(8,128)(2,1)S(1)}, u32[]{:S(2)}, u32[]{:S(2)}) %collective-permute-start.5) | collective-permute-done | bytes 262176 | tf_op jit(solution)/shard_map/ppermute | solution.py:872
  20.9 3.1 %collective-permute-start.6 = (bf16[4,128,128]{2,1,0:T(8,128)(2,1)S(1)}, bf16[4,128,128]{2,1,0:T(8,128)(2,1)S(1)}, u32[]{:S(2)}, u32[]{:S(2)}) collective-permute-start(bf16[4,128,128]{2,1,0:T(8,128)(2,1)S(1)} %get-tuple-element.65), channel_id=1, source_target_pairs={{0,16},{4,20},{8,24},{12,28},{16,0},{20,4},{24,8},{28,12},{1,17},{... | collective-permute-start | bytes 393224 | tf_op jit(solution)/shard_map/ppermute | solution.py:872
  25.3 2.9 %collective-permute-start.2 = (bf16[800,128]{1,0:T(8,128)(2,1)S(1)}, bf16[800,128]{1,0:T(8,128)(2,1)S(1)}, u32[]{:S(2)}, u32[]{:S(2)}) collective-permute-start(bf16[800,128]{1,0:T(8,128)(2,1)S(1)} %get-tuple-element.59), channel_id=1, source_target_pairs={{0,12},{4,8},{8,4},{12,0},{16,28},{20,24},{24,20},{28,16},{1,13},{... | collective-permute-start | bytes 614408 | tf_op jit(solution)/shard_map/ppermute | solution.py:872
  28.2 2.6 %collective-permute-start.9 = (bf16[4,128,128]{2,1,0:T(8,128)(2,1)S(1)}, bf16[4,128,128]{2,1,0:T(8,128)(2,1)S(1)}, u32[]{:S(2)}, u32[]{:S(2)}) collective-permute-start(bf16[4,128,128]{2,1,0:T(8,128)(2,1)S(1)} %get-tuple-element.71), channel_id=1, source_target_pairs={{0,16},{4,20},{8,24},{12,28},{16,0},{20,4},{24,8},{28,12},{1,17},{... | collective-permute-start | bytes 393224 | tf_op jit(solution)/shard_map/ppermute | solution.py:872
  32.7 1.6 %collective-permute-done.2.refs_3_ = bf16[800,128]{1,0:T(8,128)(2,1)S(1)} collective-permute-done((bf16[800,128]{1,0:T(8,128)(2,1)S(1)}, bf16[800,128]{1,0:T(8,128)(2,1)S(1)}, u32[]{:S(2)}, u32[]{:S(2)}) %collective-permute-start.2) | collective-permute-done | bytes 204832 | tf_op jit(solution)/shard_map/ppermute | solution.py:872
  34.3 1.6 %lin_local.1 = (bf16[4,800,128]{2,1,0:T(8,128)(2,1)S(1)}, f32[8,128]{1,0:T(8,128)S(1)}, f32[2,4,128,128]{3,2,1,0:T(8,128)S(1)}, bf16[2,4,128,128]{3,2,1,0:T(8,128)(2,1)S(1)}, bf16[2,128,128]{2,1,0:T(8,128)(2,1)S(1)}) custom-call(bf16[800,128]{1,0:T(8,128)(2,1)S(1)} %get-tuple-element.56.refs_0_, bf16[800,128]{1,0:T(8,128)(2,1)S(1)} %collective-permute-done.refs_4_.refs_1_, ...), custom_call_target="tpu_custom_call" | custom-call | flops 7360000000 | bytes 1024 | tf_op jit(solution)/shard_map/lin_local/lin_local/pallas_call | solution.py:844
  35.8 2.9 %collective-permute-start.10 = (bf16[2,128,128]{2,1,0:T(8,128)(2,1)S(1)}, bf16[2,128,128]{2,1,0:T(8,128)(2,1)S(1)}, u32[]{:S(2)}, u32[]{:S(2)}) collective-permute-start(bf16[2,128,128]{2,1,0:T(8,128)(2,1)S(1)} %get-tuple-element.76), channel_id=1, source_target_pairs={{0,16},{4,20},{8,24},{12,28},{16,0},{20,4},{24,8},{28,12},{1,17},{... | collective-permute-start | bytes 196616 | tf_op jit(solution)/shard_map/ppermute | solution.py:872
  38.7 2.3 %collective-permute-done.9.refs_2_ = bf16[4,128,128]{2,1,0:T(8,128)(2,1)S(1)} collective-permute-done((bf16[4,128,128]{2,1,0:T(8,128)(2,1)S(1)}, bf16[4,128,128]{2,1,0:T(8,128)(2,1)S(1)}, u32[]{:S(2)}, u32[]{:S(2)}) %collective-permute-start.9) | collective-permute-done | bytes 131104 | tf_op jit(solution)/shard_map/ppermute | solution.py:872
  41.0 1.8 %soft_rect.1 = (f32[3,512,128]{2,1,0:T(8,128)S(1)}, f32[8,512]{1,0:T(8,128)S(1)}) custom-call(bf16[4,1024,128]{2,1,0:T(8,128)(2,1)S(1)} %get-tuple-element.64.refs_0_.refs_2_, bf16[4,128,128]{2,1,0:T(8,128)(2,1)S(1)} %collective-permute-done.6.refs_1_, bf16[4,128,128]{2,1,0:T(8,128)(2,1)S(1)} %collective-permute-done.9.refs_2_, ...), custom_call_target="tpu_custom_call" | custom-call | flops 9200000000 | bytes 1024 | tf_op jit(solution)/shard_map/soft_rect/soft_rect/pallas_call | solution.py:844
  46.5 2.4 %collective-permute-done.12 = f32[8,128]{1,0:T(8,128)S(1)} collective-permute-done((f32[8,128]{1,0:T(8,128)S(1)}, f32[8,128]{1,0:T(8,128)S(1)}, u32[]{:S(2)}, u32[]{:S(2)}) %collective-permute-start.12) | collective-permute-done | bytes 4128 | tf_op jit(solution)/shard_map/ppermute | solution.py:949
  49.8 2.1 %collective-permute-start.11 = (bf16[512,128]{1,0:T(8,128)(2,1)S(1)}, bf16[512,128]{1,0:T(8,128)(2,1)S(1)}, u32[]{:S(2)}, u32[]{:S(2)}) collective-permute-start(bf16[512,128]{1,0:T(8,128)(2,1)S(1)} %pack_give.1), channel_id=1, source_target_pairs={{0,16},{4,20},{8,24},{12,28},{16,0},{20,4},{24,8},{28,12},{1,17},{... | collective-permute-start | bytes 393224 | tf_op jit(solution)/shard_map/ppermute | solution.py:872
  53.0 1.5 %collective-permute-start.14 = (f32[8,128]{1,0:T(8,128)S(1)}, f32[8,128]{1,0:T(8,128)S(1)}, u32[]{:S(2)}, u32[]{:S(2)}) collective-permute-start(f32[8,128]{1,0:T(8,128)S(1)} %add.13), channel_id=1, source_target_pairs={{0,2},{1,3},{2,0},{3,1},{4,6},{5,7},{6,4},{7,5},{8,10},{9,11},{10,... | collective-permute-start | bytes 12296 | tf_op jit(solution)/shard_map/ppermute | solution.py:949
  58.3 1.7 %collective-permute-start.22 = (bf16[768,128]{1,0:T(8,128)(2,1)S(1)}, bf16[768,128]{1,0:T(8,128)(2,1)S(1)}, u32[]{:S(2)}, u32[]{:S(2)}) collective-permute-start(bf16[768,128]{1,0:T(8,128)(2,1)S(1)} %get-tuple-element.95), channel_id=1, source_target_pairs={{0,8},{4,12},{8,0},{12,4},{16,24},{20,28},{24,16},{28,20},{1,9},{5... | collective-permute-start | bytes 589832 | tf_op jit(solution)/shard_map/ppermute | solution.py:872
  64.3 1.9 %lin_own.1 = (bf16[2,4,128,128]{3,2,1,0:T(8,128)(2,1)S(1)}, f32[2,2,4,128,128]{4,3,2,1,0:T(8,128)S(1)}) custom-call(bf16[4,800,128]{2,1,0:T(8,128)(2,1)S(1)} %get-tuple-element.68.refs_0_, f32[8,128]{1,0:T(8,128)S(1)} %get-tuple-element.69.refs_1_, bf16[2,4,128,128]{3,2,1,0:T(8,128)(2,1)S(1)} %get-tuple-element.83.refs_2_, ...), custom_call_target="tpu_custom_call" | custom-call | flops 1024 | bytes 1024 | tf_op jit(solution)/shard_map/lin_own/lin_own/pallas_call | solution.py:844
  66.2 3.3 %collective-permute-done.16.refs_4_ = bf16[2,128,128]{2,1,0:T(8,128)(2,1)S(1)} collective-permute-done((bf16[2,128,128]{2,1,0:T(8,128)(2,1)S(1)}, bf16[2,128,128]{2,1,0:T(8,128)(2,1)S(1)}, u32[]{:S(2)}, u32[]{:S(2)}) %collective-permute-start.16) | collective-permute-done | bytes 65568 | tf_op jit(solution)/shard_map/ppermute | solution.py:872
  70.6 2.6 %collective-permute-start.18 = (bf16[768,128]{1,0:T(8,128)(2,1)S(1)}, bf16[768,128]{1,0:T(8,128)(2,1)S(1)}, u32[]{:S(2)}, u32[]{:S(2)}) collective-permute-start(bf16[768,128]{1,0:T(8,128)(2,1)S(1)} %get-tuple-element.89), channel_id=1, source_target_pairs={{0,8},{4,12},{8,0},{12,4},{16,24},{20,28},{24,16},{28,20},{1,9},{5... | collective-permute-start | bytes 589832 | tf_op jit(solution)/shard_map/ppermute | solution.py:872
  75.3 3.9 %collective-permute-done.17.refs_0_ = bf16[768,128]{1,0:T(8,128)(2,1)S(1)} collective-permute-done((bf16[768,128]{1,0:T(8,128)(2,1)S(1)}, bf16[768,128]{1,0:T(8,128)(2,1)S(1)}, u32[]{:S(2)}, u32[]{:S(2)}) %collective-permute-start.17) | collective-permute-done | bytes 196640 | tf_op jit(solution)/shard_map/ppermute | solution.py:872
  79.2 3.0 %collective-permute-done.18.refs_1_ = bf16[768,128]{1,0:T(8,128)(2,1)S(1)} collective-permute-done((bf16[768,128]{1,0:T(8,128)(2,1)S(1)}, bf16[768,128]{1,0:T(8,128)(2,1)S(1)}, u32[]{:S(2)}, u32[]{:S(2)}) %collective-permute-start.18) | collective-permute-done | bytes 196640 | tf_op jit(solution)/shard_map/ppermute | solution.py:872
  (58 shorter events, 23.3 us)
Async XLA Ops:
  3.2 11.0 %collective-permute-start.3 = (bf16[1024,128]{1,0:T(8,128)(2,1)}, bf16[1024,128]{1,0:T(8,128)(2,1)S(1)}, u32[]{:S(2)}, u32[]{:S(2)}) collective-permute-start(bf16[1024,128]{1,0:T(8,128)(2,1)} %get-tuple-element.61), channel_id=1, source_target_pairs={{0,4},{4,0},{8,12},{12,8},{16,20},{20,16},{24,28},{28,24},{1,5},{5... | collective-permute-start | bytes 786440 | tf_op jit(solution)/shard_map/ppermute | solution.py:872
  6.2 9.4 %collective-permute-start.4 = (bf16[1024,128]{1,0:T(8,128)(2,1)}, bf16[1024,128]{1,0:T(8,128)(2,1)S(1)}, u32[]{:S(2)}, u32[]{:S(2)}) collective-permute-start(bf16[1024,128]{1,0:T(8,128)(2,1)} %get-tuple-element.62), channel_id=1, source_target_pairs={{0,8},{4,12},{8,0},{12,4},{16,24},{20,28},{24,16},{28,20},{1,9},{5... | collective-permute-start | bytes 786440 | tf_op jit(solution)/shard_map/ppermute | solution.py:872
  7.8 13.0 %collective-permute-start.5 = (bf16[1024,128]{1,0:T(8,128)(2,1)}, bf16[1024,128]{1,0:T(8,128)(2,1)S(1)}, u32[]{:S(2)}, u32[]{:S(2)}) collective-permute-start(bf16[1024,128]{1,0:T(8,128)(2,1)} %get-tuple-element.63), channel_id=1, source_target_pairs={{0,12},{4,8},{8,4},{12,0},{16,28},{20,24},{24,20},{28,16},{1,13},{... | collective-permute-start | bytes 786440 | tf_op jit(solution)/shard_map/ppermute | solution.py:872
  8.2 20.0 %collective-permute-start = (bf16[800,128]{1,0:T(8,128)(2,1)S(1)}, bf16[800,128]{1,0:T(8,128)(2,1)S(1)}, u32[]{:S(2)}, u32[]{:S(2)}) collective-permute-start(bf16[800,128]{1,0:T(8,128)(2,1)S(1)} %get-tuple-element.57), channel_id=1, source_target_pairs={{0,4},{4,0},{8,12},{12,8},{16,20},{20,16},{24,28},{28,24},{1,5},{5... | collective-permute-start | bytes 614408 | tf_op jit(solution)/shard_map/ppermute | solution.py:872
  10.2 20.6 %collective-permute-start.1 = (bf16[800,128]{1,0:T(8,128)(2,1)S(1)}, bf16[800,128]{1,0:T(8,128)(2,1)S(1)}, u32[]{:S(2)}, u32[]{:S(2)}) collective-permute-start(bf16[800,128]{1,0:T(8,128)(2,1)S(1)} %get-tuple-element.58), channel_id=1, source_target_pairs={{0,8},{4,12},{8,0},{12,4},{16,24},{20,28},{24,16},{28,20},{1,9},{5... | collective-permute-start | bytes 614408 | tf_op jit(solution)/shard_map/ppermute | solution.py:872
  20.9 9.9 %collective-permute-start.6 = (bf16[4,128,128]{2,1,0:T(8,128)(2,1)S(1)}, bf16[4,128,128]{2,1,0:T(8,128)(2,1)S(1)}, u32[]{:S(2)}, u32[]{:S(2)}) collective-permute-start(bf16[4,128,128]{2,1,0:T(8,128)(2,1)S(1)} %get-tuple-element.65), channel_id=1, source_target_pairs={{0,16},{4,20},{8,24},{12,28},{16,0},{20,4},{24,8},{28,12},{1,17},{... | collective-permute-start | bytes 393224 | tf_op jit(solution)/shard_map/ppermute | solution.py:872
  25.2 5.5 %collective-permute-start.7 = (f32[8,512]{1,0:T(8,128)S(1)}, f32[8,512]{1,0:T(8,128)S(1)}, u32[]{:S(2)}, u32[]{:S(2)}) collective-permute-start(f32[8,512]{1,0:T(8,128)S(1)} %get-tuple-element.66.refs_2_.refs_1_.refs_3_), channel_id=1, source_target_pairs={{0,16},{4,20},{8,24},{12,28},{16,0},{20,4},{24,8},{28,12},{1,17},{... | collective-permute-start | bytes 49160 | tf_op jit(solution)/shard_map/ppermute | solution.py:872
  25.3 9.0 %collective-permute-start.2 = (bf16[800,128]{1,0:T(8,128)(2,1)S(1)}, bf16[800,128]{1,0:T(8,128)(2,1)S(1)}, u32[]{:S(2)}, u32[]{:S(2)}) collective-permute-start(bf16[800,128]{1,0:T(8,128)(2,1)S(1)} %get-tuple-element.59), channel_id=1, source_target_pairs={{0,12},{4,8},{8,4},{12,0},{16,28},{20,24},{24,20},{28,16},{1,13},{... | collective-permute-start | bytes 614408 | tf_op jit(solution)/shard_map/ppermute | solution.py:872
  28.2 12.8 %collective-permute-start.9 = (bf16[4,128,128]{2,1,0:T(8,128)(2,1)S(1)}, bf16[4,128,128]{2,1,0:T(8,128)(2,1)S(1)}, u32[]{:S(2)}, u32[]{:S(2)}) collective-permute-start(bf16[4,128,128]{2,1,0:T(8,128)(2,1)S(1)} %get-tuple-element.71), channel_id=1, source_target_pairs={{0,16},{4,20},{8,24},{12,28},{16,0},{20,4},{24,8},{28,12},{1,17},{... | collective-permute-start | bytes 393224 | tf_op jit(solution)/shard_map/ppermute | solution.py:872
  31.7 12.0 %collective-permute-start.8 = (bf16[512,128]{1,0:T(8,128)(2,1)S(1)}, bf16[512,128]{1,0:T(8,128)(2,1)S(1)}, u32[]{:S(2)}, u32[]{:S(2)}) collective-permute-start(bf16[512,128]{1,0:T(8,128)(2,1)S(1)} %get-tuple-element.70), channel_id=1, source_target_pairs={{0,16},{4,20},{8,24},{12,28},{16,0},{20,4},{24,8},{28,12},{1,17},{... | collective-permute-start | bytes 393224 | tf_op jit(solution)/shard_map/ppermute | solution.py:872
  35.8 8.5 %collective-permute-start.10 = (bf16[2,128,128]{2,1,0:T(8,128)(2,1)S(1)}, bf16[2,128,128]{2,1,0:T(8,128)(2,1)S(1)}, u32[]{:S(2)}, u32[]{:S(2)}) collective-permute-start(bf16[2,128,128]{2,1,0:T(8,128)(2,1)S(1)} %get-tuple-element.76), channel_id=1, source_target_pairs={{0,16},{4,20},{8,24},{12,28},{16,0},{20,4},{24,8},{28,12},{1,17},{... | collective-permute-start | bytes 196616 | tf_op jit(solution)/shard_map/ppermute | solution.py:872
  45.3 3.7 %collective-permute-start.12 = (f32[8,128]{1,0:T(8,128)S(1)}, f32[8,128]{1,0:T(8,128)S(1)}, u32[]{:S(2)}, u32[]{:S(2)}) collective-permute-start(f32[8,128]{1,0:T(8,128)S(1)} %get-tuple-element.81), channel_id=1, source_target_pairs={{0,4},{4,0},{8,12},{12,8},{16,20},{20,16},{24,28},{28,24},{1,5},{5... | collective-permute-start | bytes 12296 | tf_op jit(solution)/shard_map/ppermute | solution.py:949
  45.5 9.0 %collective-permute-start.20 = (f32[8,512]{1,0:T(8,128)S(1)}, f32[8,512]{1,0:T(8,128)S(1)}, u32[]{:S(2)}, u32[]{:S(2)}) collective-permute-start(f32[8,512]{1,0:T(8,128)S(1)} %get-tuple-element.72.refs_2_), channel_id=1, source_target_pairs={{0,16},{4,20},{8,24},{12,28},{16,0},{20,4},{24,8},{28,12},{1,17},{... | collective-permute-start | bytes 49160 | tf_op jit(solution)/shard_map/ppermute | solution.py:872
  49.0 4.0 %collective-permute-start.13 = (f32[8,128]{1,0:T(8,128)S(1)}, f32[8,128]{1,0:T(8,128)S(1)}, u32[]{:S(2)}, u32[]{:S(2)}) collective-permute-start(f32[8,128]{1,0:T(8,128)S(1)} %add.12), channel_id=1, source_target_pairs={{0,8},{4,12},{8,0},{12,4},{16,24},{20,28},{24,16},{28,20},{1,9},{5... | collective-permute-start | bytes 12296 | tf_op jit(solution)/shard_map/ppermute | solution.py:949
  49.8 7.4 %collective-permute-start.11 = (bf16[512,128]{1,0:T(8,128)(2,1)S(1)}, bf16[512,128]{1,0:T(8,128)(2,1)S(1)}, u32[]{:S(2)}, u32[]{:S(2)}) collective-permute-start(bf16[512,128]{1,0:T(8,128)(2,1)S(1)} %pack_give.1), channel_id=1, source_target_pairs={{0,16},{4,20},{8,24},{12,28},{16,0},{20,4},{24,8},{28,12},{1,17},{... | collective-permute-start | bytes 393224 | tf_op jit(solution)/shard_map/ppermute | solution.py:872
  53.0 3.6 %collective-permute-start.14 = (f32[8,128]{1,0:T(8,128)S(1)}, f32[8,128]{1,0:T(8,128)S(1)}, u32[]{:S(2)}, u32[]{:S(2)}) collective-permute-start(f32[8,128]{1,0:T(8,128)S(1)} %add.13), channel_id=1, source_target_pairs={{0,2},{1,3},{2,0},{3,1},{4,6},{5,7},{6,4},{7,5},{8,10},{9,11},{10,... | collective-permute-start | bytes 12296 | tf_op jit(solution)/shard_map/ppermute | solution.py:949
  57.3 15.9 %collective-permute-start.21 = (bf16[768,128]{1,0:T(8,128)(2,1)S(1)}, bf16[768,128]{1,0:T(8,128)(2,1)S(1)}, u32[]{:S(2)}, u32[]{:S(2)}) collective-permute-start(bf16[768,128]{1,0:T(8,128)(2,1)S(1)} %get-tuple-element.94), channel_id=1, source_target_pairs={{0,12},{4,8},{8,4},{12,0},{16,28},{20,24},{24,20},{28,16},{1,13},{... | collective-permute-start | bytes 589832 | tf_op jit(solution)/shard_map/ppermute | solution.py:872
  58.3 15.7 %collective-permute-start.22 = (bf16[768,128]{1,0:T(8,128)(2,1)S(1)}, bf16[768,128]{1,0:T(8,128)(2,1)S(1)}, u32[]{:S(2)}, u32[]{:S(2)}) collective-permute-start(bf16[768,128]{1,0:T(8,128)(2,1)S(1)} %get-tuple-element.95), channel_id=1, source_target_pairs={{0,8},{4,12},{8,0},{12,4},{16,24},{20,28},{24,16},{28,20},{1,9},{5... | collective-permute-start | bytes 589832 | tf_op jit(solution)/shard_map/ppermute | solution.py:872
  60.0 14.0 %collective-permute-start.23 = (bf16[768,128]{1,0:T(8,128)(2,1)S(1)}, bf16[768,128]{1,0:T(8,128)(2,1)S(1)}, u32[]{:S(2)}, u32[]{:S(2)}) collective-permute-start(bf16[768,128]{1,0:T(8,128)(2,1)S(1)} %get-tuple-element.96), channel_id=1, source_target_pairs={{0,4},{4,0},{8,12},{12,8},{16,20},{20,16},{24,28},{28,24},{1,5},{5... | collective-permute-start | bytes 589832 | tf_op jit(solution)/shard_map/ppermute | solution.py:872
  60.8 1.2 %collective-permute-start.15 = (f32[8,128]{1,0:T(8,128)S(1)}, f32[8,128]{1,0:T(8,128)S(1)}, u32[]{:S(2)}, u32[]{:S(2)}) collective-permute-start(f32[8,128]{1,0:T(8,128)S(1)} %add.14), channel_id=1, source_target_pairs={{0,1},{1,0},{2,3},{3,2},{4,5},{5,4},{6,7},{7,6},{8,9},{9,8},{10,11... | collective-permute-start | bytes 12296 | tf_op jit(solution)/shard_map/ppermute | solution.py:949
  63.2 6.3 %collective-permute-start.16 = (bf16[2,128,128]{2,1,0:T(8,128)(2,1)S(1)}, bf16[2,128,128]{2,1,0:T(8,128)(2,1)S(1)}, u32[]{:S(2)}, u32[]{:S(2)}) collective-permute-start(bf16[2,128,128]{2,1,0:T(8,128)(2,1)S(1)} %get-tuple-element.87), channel_id=1, source_target_pairs={{0,16},{4,20},{8,24},{12,28},{16,0},{20,4},{24,8},{28,12},{1,17},{... | collective-permute-start | bytes 196616 | tf_op jit(solution)/shard_map/ppermute | solution.py:872
  70.4 8.8 %collective-permute-start.17 = (bf16[768,128]{1,0:T(8,128)(2,1)S(1)}, bf16[768,128]{1,0:T(8,128)(2,1)S(1)}, u32[]{:S(2)}, u32[]{:S(2)}) collective-permute-start(bf16[768,128]{1,0:T(8,128)(2,1)S(1)} %get-tuple-element.88), channel_id=1, source_target_pairs={{0,12},{4,8},{8,4},{12,0},{16,28},{20,24},{24,20},{28,16},{1,13},{... | collective-permute-start | bytes 589832 | tf_op jit(solution)/shard_map/ppermute | solution.py:872
  70.6 11.6 %collective-permute-start.18 = (bf16[768,128]{1,0:T(8,128)(2,1)S(1)}, bf16[768,128]{1,0:T(8,128)(2,1)S(1)}, u32[]{:S(2)}, u32[]{:S(2)}) collective-permute-start(bf16[768,128]{1,0:T(8,128)(2,1)S(1)} %get-tuple-element.89), channel_id=1, source_target_pairs={{0,8},{4,12},{8,0},{12,4},{16,24},{20,28},{24,16},{28,20},{1,9},{5... | collective-permute-start | bytes 589832 | tf_op jit(solution)/shard_map/ppermute | solution.py:872
  73.2 9.0 %collective-permute-start.19 = (bf16[768,128]{1,0:T(8,128)(2,1)S(1)}, bf16[768,128]{1,0:T(8,128)(2,1)S(1)}, u32[]{:S(2)}, u32[]{:S(2)}) collective-permute-start(bf16[768,128]{1,0:T(8,128)(2,1)S(1)} %get-tuple-element.90), channel_id=1, source_target_pairs={{0,4},{4,0},{8,12},{12,8},{16,20},{20,16},{24,28},{28,24},{1,5},{5... | collective-permute-start | bytes 589832 | tf_op jit(solution)/shard_map/ppermute | solution.py:872
  (6 other events, 46.2 us)

commit v5 on v4

--- a/solution.py
+++ b/solution.py
@@ -943,7 +943,7 @@
     steps += [("head", 1 << bit) for bit in reversed(range((lax.axis_size("head") - 1).bit_length()))]
     for place, (axis, step) in enumerate(steps):
         sums = after(sums)
-        if place == 3:
+        if place == 2:
             given, sums = after((given, sums))
         count = lax.axis_size(axis)
         sums = sums + lax.ppermute(sums, axis, [(i, i ^ step) for i in range(count)])

time: 83.7 us -> 83.5 us (level)
  waiting for transfers between devices: 29.7 us -> 25 us
  starting transfers between devices: 34.4 us -> 38.9 us
    ppermute x20, waiting for transfers between devices: 23.7 us -> 20.3 us  [moved(): return lax.ppermute(x, 'ctx', [(i, i ^ step) for i in range(spans)])]
    ppermute x20, starting transfers between devices: 31.9 us -> 34.7 us  [moved(): return lax.ppermute(x, 'ctx', [(i, i ^ step) for i in range(spans)])]
    ppermute x4, starting transfers between devices: 2.5 us -> 4.25 us  [by_halves(): lax.ppermute(sums, axis, [(i, i ^ step) for i in range(count)])]
    ppermute x4, waiting for transfers between devices: 5.96 us -> 4.64 us  [by_halves(): lax.ppermute(sums, axis, [(i, i ^ step) for i in range(count)])]
  transfers between devices with their start and end apart: 24 -> 24, of which waited for: 13 -> 13; matrix products, arithmetic and copies ran while one was open for 0% -> 0% of each run, Pallas kernels for 16% -> 18%
where the time goes in v5:
time: 83.5 us; the launch traced here: 83.4 us
  starting transfers between devices  38.9 us (47%)
  waiting for transfers between devices  25 us (30%)
  Pallas kernels  18.6 us (22%)
  between operations  0.84 us (1%)
    ppermute x20, starting transfers between devices, moved(): return lax.ppermute(x, 'ctx', [(i, i ^ step) for i in range(spans)])  34.7 us
    ppermute x20, waiting for transfers between devices, moved(): return lax.ppermute(x, 'ctx', [(i, i ^ step) for i in range(spans)])  20.3 us
    pallas_call x18, Pallas kernels, call(): pl.pallas_call(body, out_shape=out_shape, scratch_shapes=scratch, name=na...  18.6 us
    ppermute x4, waiting for transfers between devices, by_halves(): lax.ppermute(sums, axis, [(i, i ^ step) for i in range(count)])  4.64 us
    ppermute x4, starting transfers between devices, by_halves(): lax.ppermute(sums, axis, [(i, i ^ step) for i in range(count)])  4.25 us
  transfers between devices with their start and end apart: 24, of which 13 were waited for; matrix products, arithmetic and copies ran while one was open for 0% of the time, Pallas kernels for 18%

profile of v5, /device:TPU:0, one launch (start us, length us, event | category | flops | bytes accessed | tf_op | source)
XLA Modules:
  0.0 83.4 jit_solution(841058680158496459)
XLA Ops:
  0.7 2.6 %pack_soft.1 = (bf16[1024,128]{1,0:T(8,128)(2,1)}, bf16[1024,128]{1,0:T(8,128)(2,1)}, bf16[1024,128]{1,0:T(8,128)(2,1)}, bf16[1024,128]{1,0:T(8,128)(2,1)}) custom-call(bf16[128,8,128]{2,1,0:T(8,128)(2,1)} %refs_0_.3, bf16[128,8,128]{2,1,0:T(8,128)(2,1)} %refs_1_.3, bf16[128,8,128]{2,1,0:T(8,128)(2,1)} %refs_2_.3, bf16[128,8,128]{2,1,0:T(8,128)(2,1)} %refs_3_.3), custom_call_target="tpu_custom_call" | custom-call | flops 11960000512 | bytes 1024 | tf_op jit(solution)/shard_map/pack_soft/pack_soft/pallas_call | solution.py:844
  3.2 3.0 %collective-permute-start.3 = (bf16[1024,128]{1,0:T(8,128)(2,1)}, bf16[1024,128]{1,0:T(8,128)(2,1)S(1)}, u32[]{:S(2)}, u32[]{:S(2)}) collective-permute-start(bf16[1024,128]{1,0:T(8,128)(2,1)} %get-tuple-element.61), channel_id=1, source_target_pairs={{0,4},{4,0},{8,12},{12,8},{16,20},{20,16},{24,28},{28,24},{1,5},{5... | collective-permute-start | bytes 786440 | tf_op jit(solution)/shard_map/ppermute | solution.py:872
  6.2 1.6 %collective-permute-start.4 = (bf16[1024,128]{1,0:T(8,128)(2,1)}, bf16[1024,128]{1,0:T(8,128)(2,1)S(1)}, u32[]{:S(2)}, u32[]{:S(2)}) collective-permute-start(bf16[1024,128]{1,0:T(8,128)(2,1)} %get-tuple-element.62), channel_id=1, source_target_pairs={{0,8},{4,12},{8,0},{12,4},{16,24},{20,28},{24,16},{28,20},{1,9},{5... | collective-permute-start | bytes 786440 | tf_op jit(solution)/shard_map/ppermute | solution.py:872
  8.2 2.0 %collective-permute-start = (bf16[800,128]{1,0:T(8,128)(2,1)S(1)}, bf16[800,128]{1,0:T(8,128)(2,1)S(1)}, u32[]{:S(2)}, u32[]{:S(2)}) collective-permute-start(bf16[800,128]{1,0:T(8,128)(2,1)S(1)} %get-tuple-element.57), channel_id=1, source_target_pairs={{0,4},{4,0},{8,12},{12,8},{16,20},{20,16},{24,28},{28,24},{1,5},{5... | collective-permute-start | bytes 614408 | tf_op jit(solution)/shard_map/ppermute | solution.py:872
  10.2 1.6 %collective-permute-start.1 = (bf16[800,128]{1,0:T(8,128)(2,1)S(1)}, bf16[800,128]{1,0:T(8,128)(2,1)S(1)}, u32[]{:S(2)}, u32[]{:S(2)}) collective-permute-start(bf16[800,128]{1,0:T(8,128)(2,1)S(1)} %get-tuple-element.58), channel_id=1, source_target_pairs={{0,8},{4,12},{8,0},{12,4},{16,24},{20,28},{24,16},{28,20},{1,9},{5... | collective-permute-start | bytes 614408 | tf_op jit(solution)/shard_map/ppermute | solution.py:872
  11.8 2.5 %collective-permute-done.3.refs_1_ = bf16[1024,128]{1,0:T(8,128)(2,1)S(1)} collective-permute-done((bf16[1024,128]{1,0:T(8,128)(2,1)}, bf16[1024,128]{1,0:T(8,128)(2,1)S(1)}, u32[]{:S(2)}, u32[]{:S(2)}) %collective-permute-start.3) | collective-permute-done | bytes 262176 | tf_op jit(solution)/shard_map/ppermute | solution.py:872
  15.7 5.1 %collective-permute-done.5.refs_3_ = bf16[1024,128]{1,0:T(8,128)(2,1)S(1)} collective-permute-done((bf16[1024,128]{1,0:T(8,128)(2,1)}, bf16[1024,128]{1,0:T(8,128)(2,1)S(1)}, u32[]{:S(2)}, u32[]{:S(2)}) %collective-permute-start.5) | collective-permute-done | bytes 262176 | tf_op jit(solution)/shard_map/ppermute | solution.py:872
  20.9 3.1 %collective-permute-start.6 = (bf16[4,128,128]{2,1,0:T(8,128)(2,1)S(1)}, bf16[4,128,128]{2,1,0:T(8,128)(2,1)S(1)}, u32[]{:S(2)}, u32[]{:S(2)}) collective-permute-start(bf16[4,128,128]{2,1,0:T(8,128)(2,1)S(1)} %get-tuple-element.65), channel_id=1, source_target_pairs={{0,16},{4,20},{8,24},{12,28},{16,0},{20,4},{24,8},{28,12},{1,17},{... | collective-permute-start | bytes 393224 | tf_op jit(solution)/shard_map/ppermute | solution.py:872
  25.3 2.9 %collective-permute-start.2 = (bf16[800,128]{1,0:T(8,128)(2,1)S(1)}, bf16[800,128]{1,0:T(8,128)(2,1)S(1)}, u32[]{:S(2)}, u32[]{:S(2)}) collective-permute-start(bf16[800,128]{1,0:T(8,128)(2,1)S(1)} %get-tuple-element.59), channel_id=1, source_target_pairs={{0,12},{4,8},{8,4},{12,0},{16,28},{20,24},{24,20},{28,16},{1,13},{... | collective-permute-start | bytes 614408 | tf_op jit(solution)/shard_map/ppermute | solution.py:872
  28.2 2.6 %collective-permute-start.9 = (bf16[4,128,128]{2,1,0:T(8,128)(2,1)S(1)}, bf16[4,128,128]{2,1,0:T(8,128)(2,1)S(1)}, u32[]{:S(2)}, u32[]{:S(2)}) collective-permute-start(bf16[4,128,128]{2,1,0:T(8,128)(2,1)S(1)} %get-tuple-element.71), channel_id=1, source_target_pairs={{0,16},{4,20},{8,24},{12,28},{16,0},{20,4},{24,8},{28,12},{1,17},{... | collective-permute-start | bytes 393224 | tf_op jit(solution)/shard_map/ppermute | solution.py:872
  32.7 1.6 %collective-permute-done.2.refs_3_ = bf16[800,128]{1,0:T(8,128)(2,1)S(1)} collective-permute-done((bf16[800,128]{1,0:T(8,128)(2,1)S(1)}, bf16[800,128]{1,0:T(8,128)(2,1)S(1)}, u32[]{:S(2)}, u32[]{:S(2)}) %collective-permute-start.2) | collective-permute-done | bytes 204832 | tf_op jit(solution)/shard_map/ppermute | solution.py:872
  34.3 1.6 %lin_local.1 = (bf16[4,800,128]{2,1,0:T(8,128)(2,1)S(1)}, f32[8,128]{1,0:T(8,128)S(1)}, f32[2,4,128,128]{3,2,1,0:T(8,128)S(1)}, bf16[2,4,128,128]{3,2,1,0:T(8,128)(2,1)S(1)}, bf16[2,128,128]{2,1,0:T(8,128)(2,1)S(1)}) custom-call(bf16[800,128]{1,0:T(8,128)(2,1)S(1)} %get-tuple-element.56.refs_0_, bf16[800,128]{1,0:T(8,128)(2,1)S(1)} %collective-permute-done.refs_4_.refs_1_, ...), custom_call_target="tpu_custom_call" | custom-call | flops 7360000000 | bytes 1024 | tf_op jit(solution)/shard_map/lin_local/lin_local/pallas_call | solution.py:844
  35.8 2.9 %collective-permute-start.10 = (bf16[2,128,128]{2,1,0:T(8,128)(2,1)S(1)}, bf16[2,128,128]{2,1,0:T(8,128)(2,1)S(1)}, u32[]{:S(2)}, u32[]{:S(2)}) collective-permute-start(bf16[2,128,128]{2,1,0:T(8,128)(2,1)S(1)} %get-tuple-element.76), channel_id=1, source_target_pairs={{0,16},{4,20},{8,24},{12,28},{16,0},{20,4},{24,8},{28,12},{1,17},{... | collective-permute-start | bytes 196616 | tf_op jit(solution)/shard_map/ppermute | solution.py:872
  38.7 2.4 %collective-permute-done.9.refs_2_ = bf16[4,128,128]{2,1,0:T(8,128)(2,1)S(1)} collective-permute-done((bf16[4,128,128]{2,1,0:T(8,128)(2,1)S(1)}, bf16[4,128,128]{2,1,0:T(8,128)(2,1)S(1)}, u32[]{:S(2)}, u32[]{:S(2)}) %collective-permute-start.9) | collective-permute-done | bytes 131104 | tf_op jit(solution)/shard_map/ppermute | solution.py:872
  41.2 1.8 %soft_rect.1 = (f32[3,512,128]{2,1,0:T(8,128)S(1)}, f32[8,512]{1,0:T(8,128)S(1)}) custom-call(bf16[4,1024,128]{2,1,0:T(8,128)(2,1)S(1)} %get-tuple-element.64.refs_0_.refs_2_, bf16[4,128,128]{2,1,0:T(8,128)(2,1)S(1)} %collective-permute-done.6.refs_1_, bf16[4,128,128]{2,1,0:T(8,128)(2,1)S(1)} %collective-permute-done.9.refs_2_, ...), custom_call_target="tpu_custom_call" | custom-call | flops 9200000000 | bytes 1024 | tf_op jit(solution)/shard_map/soft_rect/soft_rect/pallas_call | solution.py:844
  45.9 2.8 %collective-permute-start.11 = (bf16[512,128]{1,0:T(8,128)(2,1)S(1)}, bf16[512,128]{1,0:T(8,128)(2,1)S(1)}, u32[]{:S(2)}, u32[]{:S(2)}) collective-permute-start(bf16[512,128]{1,0:T(8,128)(2,1)S(1)} %pack_give.1), channel_id=1, source_target_pairs={{0,16},{4,20},{8,24},{12,28},{16,0},{20,4},{24,8},{28,12},{1,17},{... | collective-permute-start | bytes 393224 | tf_op jit(solution)/shard_map/ppermute | solution.py:872
  49.2 2.5 %collective-permute-start.13 = (f32[8,128]{1,0:T(8,128)S(1)}, f32[8,128]{1,0:T(8,128)S(1)}, u32[]{:S(2)}, u32[]{:S(2)}) collective-permute-start(f32[8,128]{1,0:T(8,128)S(1)} %add.12), channel_id=1, source_target_pairs={{0,8},{4,12},{8,0},{12,4},{16,24},{20,28},{24,16},{28,20},{1,9},{5... | collective-permute-start | bytes 12296 | tf_op jit(solution)/shard_map/ppermute | solution.py:949
  53.4 3.5 %collective-permute-start.21 = (bf16[768,128]{1,0:T(8,128)(2,1)S(1)}, bf16[768,128]{1,0:T(8,128)(2,1)S(1)}, u32[]{:S(2)}, u32[]{:S(2)}) collective-permute-start(bf16[768,128]{1,0:T(8,128)(2,1)S(1)} %get-tuple-element.94), channel_id=1, source_target_pairs={{0,12},{4,8},{8,4},{12,0},{16,28},{20,24},{24,20},{28,16},{1,13},{... | collective-permute-start | bytes 589832 | tf_op jit(solution)/shard_map/ppermute | solution.py:872
  60.4 2.1 %collective-permute-done.14 = f32[8,128]{1,0:T(8,128)S(1)} collective-permute-done((f32[8,128]{1,0:T(8,128)S(1)}, f32[8,128]{1,0:T(8,128)S(1)}, u32[]{:S(2)}, u32[]{:S(2)}) %collective-permute-start.14) | collective-permute-done | bytes 4128 | tf_op jit(solution)/shard_map/ppermute | solution.py:949
  65.0 2.2 %collective-permute-start.16 = (bf16[2,128,128]{2,1,0:T(8,128)(2,1)S(1)}, bf16[2,128,128]{2,1,0:T(8,128)(2,1)S(1)}, u32[]{:S(2)}, u32[]{:S(2)}) collective-permute-start(bf16[2,128,128]{2,1,0:T(8,128)(2,1)S(1)} %get-tuple-element.87), channel_id=1, source_target_pairs={{0,16},{4,20},{8,24},{12,28},{16,0},{20,4},{24,8},{28,12},{1,17},{... | collective-permute-start | bytes 196616 | tf_op jit(solution)/shard_map/ppermute | solution.py:872
  67.1 1.9 %lin_own.1 = (bf16[2,4,128,128]{3,2,1,0:T(8,128)(2,1)S(1)}, f32[2,2,4,128,128]{4,3,2,1,0:T(8,128)S(1)}) custom-call(bf16[4,800,128]{2,1,0:T(8,128)(2,1)S(1)} %get-tuple-element.68.refs_0_, f32[8,128]{1,0:T(8,128)S(1)} %get-tuple-element.69.refs_1_, bf16[2,4,128,128]{3,2,1,0:T(8,128)(2,1)S(1)} %get-tuple-element.83.refs_2_, ...), custom_call_target="tpu_custom_call" | custom-call | flops 1024 | bytes 1024 | tf_op jit(solution)/shard_map/lin_own/lin_own/pallas_call | solution.py:844
  72.6 2.0 %collective-permute-start.18 = (bf16[768,128]{1,0:T(8,128)(2,1)S(1)}, bf16[768,128]{1,0:T(8,128)(2,1)S(1)}, u32[]{:S(2)}, u32[]{:S(2)}) collective-permute-start(bf16[768,128]{1,0:T(8,128)(2,1)S(1)} %get-tuple-element.89), channel_id=1, source_target_pairs={{0,8},{4,12},{8,0},{12,4},{16,24},{20,28},{24,16},{28,20},{1,9},{5... | collective-permute-start | bytes 589832 | tf_op jit(solution)/shard_map/ppermute | solution.py:872
  76.0 3.9 %collective-permute-done.17.refs_0_ = bf16[768,128]{1,0:T(8,128)(2,1)S(1)} collective-permute-done((bf16[768,128]{1,0:T(8,128)(2,1)S(1)}, bf16[768,128]{1,0:T(8,128)(2,1)S(1)}, u32[]{:S(2)}, u32[]{:S(2)}) %collective-permute-start.17) | collective-permute-done | bytes 196640 | tf_op jit(solution)/shard_map/ppermute | solution.py:872
  79.9 1.6 %collective-permute-done.18.refs_1_ = bf16[768,128]{1,0:T(8,128)(2,1)S(1)} collective-permute-done((bf16[768,128]{1,0:T(8,128)(2,1)S(1)}, bf16[768,128]{1,0:T(8,128)(2,1)S(1)}, u32[]{:S(2)}, u32[]{:S(2)}) %collective-permute-start.18) | collective-permute-done | bytes 196640 | tf_op jit(solution)/shard_map/ppermute | solution.py:872
  (58 shorter events, 22.7 us)
Async XLA Ops:
  3.2 11.0 %collective-permute-start.3 = (bf16[1024,128]{1,0:T(8,128)(2,1)}, bf16[1024,128]{1,0:T(8,128)(2,1)S(1)}, u32[]{:S(2)}, u32[]{:S(2)}) collective-permute-start(bf16[1024,128]{1,0:T(8,128)(2,1)} %get-tuple-element.61), channel_id=1, source_target_pairs={{0,4},{4,0},{8,12},{12,8},{16,20},{20,16},{24,28},{28,24},{1,5},{5... | collective-permute-start | bytes 786440 | tf_op jit(solution)/shard_map/ppermute | solution.py:872
  6.2 9.4 %collective-permute-start.4 = (bf16[1024,128]{1,0:T(8,128)(2,1)}, bf16[1024,128]{1,0:T(8,128)(2,1)S(1)}, u32[]{:S(2)}, u32[]{:S(2)}) collective-permute-start(bf16[1024,128]{1,0:T(8,128)(2,1)} %get-tuple-element.62), channel_id=1, source_target_pairs={{0,8},{4,12},{8,0},{12,4},{16,24},{20,28},{24,16},{28,20},{1,9},{5... | collective-permute-start | bytes 786440 | tf_op jit(solution)/shard_map/ppermute | solution.py:872
  7.8 13.0 %collective-permute-start.5 = (bf16[1024,128]{1,0:T(8,128)(2,1)}, bf16[1024,128]{1,0:T(8,128)(2,1)S(1)}, u32[]{:S(2)}, u32[]{:S(2)}) collective-permute-start(bf16[1024,128]{1,0:T(8,128)(2,1)} %get-tuple-element.63), channel_id=1, source_target_pairs={{0,12},{4,8},{8,4},{12,0},{16,28},{20,24},{24,20},{28,16},{1,13},{... | collective-permute-start | bytes 786440 | tf_op jit(solution)/shard_map/ppermute | solution.py:872
  8.2 20.0 %collective-permute-start = (bf16[800,128]{1,0:T(8,128)(2,1)S(1)}, bf16[800,128]{1,0:T(8,128)(2,1)S(1)}, u32[]{:S(2)}, u32[]{:S(2)}) collective-permute-start(bf16[800,128]{1,0:T(8,128)(2,1)S(1)} %get-tuple-element.57), channel_id=1, source_target_pairs={{0,4},{4,0},{8,12},{12,8},{16,20},{20,16},{24,28},{28,24},{1,5},{5... | collective-permute-start | bytes 614408 | tf_op jit(solution)/shard_map/ppermute | solution.py:872
  10.2 20.6 %collective-permute-start.1 = (bf16[800,128]{1,0:T(8,128)(2,1)S(1)}, bf16[800,128]{1,0:T(8,128)(2,1)S(1)}, u32[]{:S(2)}, u32[]{:S(2)}) collective-permute-start(bf16[800,128]{1,0:T(8,128)(2,1)S(1)} %get-tuple-element.58), channel_id=1, source_target_pairs={{0,8},{4,12},{8,0},{12,4},{16,24},{20,28},{24,16},{28,20},{1,9},{5... | collective-permute-start | bytes 614408 | tf_op jit(solution)/shard_map/ppermute | solution.py:872
  20.9 9.9 %collective-permute-start.6 = (bf16[4,128,128]{2,1,0:T(8,128)(2,1)S(1)}, bf16[4,128,128]{2,1,0:T(8,128)(2,1)S(1)}, u32[]{:S(2)}, u32[]{:S(2)}) collective-permute-start(bf16[4,128,128]{2,1,0:T(8,128)(2,1)S(1)} %get-tuple-element.65), channel_id=1, source_target_pairs={{0,16},{4,20},{8,24},{12,28},{16,0},{20,4},{24,8},{28,12},{1,17},{... | collective-permute-start | bytes 393224 | tf_op jit(solution)/shard_map/ppermute | solution.py:872
  25.2 5.5 %collective-permute-start.7 = (f32[8,512]{1,0:T(8,128)S(1)}, f32[8,512]{1,0:T(8,128)S(1)}, u32[]{:S(2)}, u32[]{:S(2)}) collective-permute-start(f32[8,512]{1,0:T(8,128)S(1)} %get-tuple-element.66.refs_2_.refs_1_.refs_3_), channel_id=1, source_target_pairs={{0,16},{4,20},{8,24},{12,28},{16,0},{20,4},{24,8},{28,12},{1,17},{... | collective-permute-start | bytes 49160 | tf_op jit(solution)/shard_map/ppermute | solution.py:872
  25.3 9.0 %collective-permute-start.2 = (bf16[800,128]{1,0:T(8,128)(2,1)S(1)}, bf16[800,128]{1,0:T(8,128)(2,1)S(1)}, u32[]{:S(2)}, u32[]{:S(2)}) collective-permute-start(bf16[800,128]{1,0:T(8,128)(2,1)S(1)} %get-tuple-element.59), channel_id=1, source_target_pairs={{0,12},{4,8},{8,4},{12,0},{16,28},{20,24},{24,20},{28,16},{1,13},{... | collective-permute-start | bytes 614408 | tf_op jit(solution)/shard_map/ppermute | solution.py:872
  28.2 13.0 %collective-permute-start.9 = (bf16[4,128,128]{2,1,0:T(8,128)(2,1)S(1)}, bf16[4,128,128]{2,1,0:T(8,128)(2,1)S(1)}, u32[]{:S(2)}, u32[]{:S(2)}) collective-permute-start(bf16[4,128,128]{2,1,0:T(8,128)(2,1)S(1)} %get-tuple-element.71), channel_id=1, source_target_pairs={{0,16},{4,20},{8,24},{12,28},{16,0},{20,4},{24,8},{28,12},{1,17},{... | collective-permute-start | bytes 393224 | tf_op jit(solution)/shard_map/ppermute | solution.py:872
  31.7 12.3 %collective-permute-start.8 = (bf16[512,128]{1,0:T(8,128)(2,1)S(1)}, bf16[512,128]{1,0:T(8,128)(2,1)S(1)}, u32[]{:S(2)}, u32[]{:S(2)}) collective-permute-start(bf16[512,128]{1,0:T(8,128)(2,1)S(1)} %get-tuple-element.70), channel_id=1, source_target_pairs={{0,16},{4,20},{8,24},{12,28},{16,0},{20,4},{24,8},{28,12},{1,17},{... | collective-permute-start | bytes 393224 | tf_op jit(solution)/shard_map/ppermute | solution.py:872
  35.8 8.8 %collective-permute-start.10 = (bf16[2,128,128]{2,1,0:T(8,128)(2,1)S(1)}, bf16[2,128,128]{2,1,0:T(8,128)(2,1)S(1)}, u32[]{:S(2)}, u32[]{:S(2)}) collective-permute-start(bf16[2,128,128]{2,1,0:T(8,128)(2,1)S(1)} %get-tuple-element.76), channel_id=1, source_target_pairs={{0,16},{4,20},{8,24},{12,28},{16,0},{20,4},{24,8},{28,12},{1,17},{... | collective-permute-start | bytes 196616 | tf_op jit(solution)/shard_map/ppermute | solution.py:872
  43.0 8.7 %collective-permute-start.20 = (f32[8,512]{1,0:T(8,128)S(1)}, f32[8,512]{1,0:T(8,128)S(1)}, u32[]{:S(2)}, u32[]{:S(2)}) collective-permute-start(f32[8,512]{1,0:T(8,128)S(1)} %get-tuple-element.72.refs_2_), channel_id=1, source_target_pairs={{0,16},{4,20},{8,24},{12,28},{16,0},{20,4},{24,8},{28,12},{1,17},{... | collective-permute-start | bytes 49160 | tf_op jit(solution)/shard_map/ppermute | solution.py:872
  45.5 3.7 %collective-permute-start.12 = (f32[8,128]{1,0:T(8,128)S(1)}, f32[8,128]{1,0:T(8,128)S(1)}, u32[]{:S(2)}, u32[]{:S(2)}) collective-permute-start(f32[8,128]{1,0:T(8,128)S(1)} %get-tuple-element.81), channel_id=1, source_target_pairs={{0,4},{4,0},{8,12},{12,8},{16,20},{20,16},{24,28},{28,24},{1,5},{5... | collective-permute-start | bytes 12296 | tf_op jit(solution)/shard_map/ppermute | solution.py:949
  45.9 7.5 %collective-permute-start.11 = (bf16[512,128]{1,0:T(8,128)(2,1)S(1)}, bf16[512,128]{1,0:T(8,128)(2,1)S(1)}, u32[]{:S(2)}, u32[]{:S(2)}) collective-permute-start(bf16[512,128]{1,0:T(8,128)(2,1)S(1)} %pack_give.1), channel_id=1, source_target_pairs={{0,16},{4,20},{8,24},{12,28},{16,0},{20,4},{24,8},{28,12},{1,17},{... | collective-permute-start | bytes 393224 | tf_op jit(solution)/shard_map/ppermute | solution.py:872
  49.2 4.1 %collective-permute-start.13 = (f32[8,128]{1,0:T(8,128)S(1)}, f32[8,128]{1,0:T(8,128)S(1)}, u32[]{:S(2)}, u32[]{:S(2)}) collective-permute-start(f32[8,128]{1,0:T(8,128)S(1)} %add.12), channel_id=1, source_target_pairs={{0,8},{4,12},{8,0},{12,4},{16,24},{20,28},{24,16},{28,20},{1,9},{5... | collective-permute-start | bytes 12296 | tf_op jit(solution)/shard_map/ppermute | solution.py:949
  53.4 21.2 %collective-permute-start.21 = (bf16[768,128]{1,0:T(8,128)(2,1)S(1)}, bf16[768,128]{1,0:T(8,128)(2,1)S(1)}, u32[]{:S(2)}, u32[]{:S(2)}) collective-permute-start(bf16[768,128]{1,0:T(8,128)(2,1)S(1)} %get-tuple-element.94), channel_id=1, source_target_pairs={{0,12},{4,8},{8,4},{12,0},{16,28},{20,24},{24,20},{28,16},{1,13},{... | collective-permute-start | bytes 589832 | tf_op jit(solution)/shard_map/ppermute | solution.py:872
  57.0 17.7 %collective-permute-start.22 = (bf16[768,128]{1,0:T(8,128)(2,1)S(1)}, bf16[768,128]{1,0:T(8,128)(2,1)S(1)}, u32[]{:S(2)}, u32[]{:S(2)}) collective-permute-start(bf16[768,128]{1,0:T(8,128)(2,1)S(1)} %get-tuple-element.95), channel_id=1, source_target_pairs={{0,8},{4,12},{8,0},{12,4},{16,24},{20,28},{24,16},{28,20},{1,9},{5... | collective-permute-start | bytes 589832 | tf_op jit(solution)/shard_map/ppermute | solution.py:872
  57.6 17.1 %collective-permute-start.23 = (bf16[768,128]{1,0:T(8,128)(2,1)S(1)}, bf16[768,128]{1,0:T(8,128)(2,1)S(1)}, u32[]{:S(2)}, u32[]{:S(2)}) collective-permute-start(bf16[768,128]{1,0:T(8,128)(2,1)S(1)} %get-tuple-element.96), channel_id=1, source_target_pairs={{0,4},{4,0},{8,12},{12,8},{16,20},{20,16},{24,28},{28,24},{1,5},{5... | collective-permute-start | bytes 589832 | tf_op jit(solution)/shard_map/ppermute | solution.py:872
  59.0 3.6 %collective-permute-start.14 = (f32[8,128]{1,0:T(8,128)S(1)}, f32[8,128]{1,0:T(8,128)S(1)}, u32[]{:S(2)}, u32[]{:S(2)}) collective-permute-start(f32[8,128]{1,0:T(8,128)S(1)} %add.13), channel_id=1, source_target_pairs={{0,2},{1,3},{2,0},{3,1},{4,6},{5,7},{6,4},{7,5},{8,10},{9,11},{10,... | collective-permute-start | bytes 12296 | tf_op jit(solution)/shard_map/ppermute | solution.py:949
  62.6 1.2 %collective-permute-start.15 = (f32[8,128]{1,0:T(8,128)S(1)}, f32[8,128]{1,0:T(8,128)S(1)}, u32[]{:S(2)}, u32[]{:S(2)}) collective-permute-start(f32[8,128]{1,0:T(8,128)S(1)} %add.14), channel_id=1, source_target_pairs={{0,1},{1,0},{2,3},{3,2},{4,5},{5,4},{6,7},{7,6},{8,9},{9,8},{10,11... | collective-permute-start | bytes 12296 | tf_op jit(solution)/shard_map/ppermute | solution.py:949
  65.0 5.2 %collective-permute-start.16 = (bf16[2,128,128]{2,1,0:T(8,128)(2,1)S(1)}, bf16[2,128,128]{2,1,0:T(8,128)(2,1)S(1)}, u32[]{:S(2)}, u32[]{:S(2)}) collective-permute-start(bf16[2,128,128]{2,1,0:T(8,128)(2,1)S(1)} %get-tuple-element.87), channel_id=1, source_target_pairs={{0,16},{4,20},{8,24},{12,28},{16,0},{20,4},{24,8},{28,12},{1,17},{... | collective-permute-start | bytes 196616 | tf_op jit(solution)/shard_map/ppermute | solution.py:872
  71.1 8.8 %collective-permute-start.17 = (bf16[768,128]{1,0:T(8,128)(2,1)S(1)}, bf16[768,128]{1,0:T(8,128)(2,1)S(1)}, u32[]{:S(2)}, u32[]{:S(2)}) collective-permute-start(bf16[768,128]{1,0:T(8,128)(2,1)S(1)} %get-tuple-element.88), channel_id=1, source_target_pairs={{0,12},{4,8},{8,4},{12,0},{16,28},{20,24},{24,20},{28,16},{1,13},{... | collective-permute-start | bytes 589832 | tf_op jit(solution)/shard_map/ppermute | solution.py:872
  72.6 8.9 %collective-permute-start.18 = (bf16[768,128]{1,0:T(8,128)(2,1)S(1)}, bf16[768,128]{1,0:T(8,128)(2,1)S(1)}, u32[]{:S(2)}, u32[]{:S(2)}) collective-permute-start(bf16[768,128]{1,0:T(8,128)(2,1)S(1)} %get-tuple-element.89), channel_id=1, source_target_pairs={{0,8},{4,12},{8,0},{12,4},{16,24},{20,28},{24,16},{28,20},{1,9},{5... | collective-permute-start | bytes 589832 | tf_op jit(solution)/shard_map/ppermute | solution.py:872
  74.7 7.4 %collective-permute-start.19 = (bf16[768,128]{1,0:T(8,128)(2,1)S(1)}, bf16[768,128]{1,0:T(8,128)(2,1)S(1)}, u32[]{:S(2)}, u32[]{:S(2)}) collective-permute-start(bf16[768,128]{1,0:T(8,128)(2,1)S(1)} %get-tuple-element.90), channel_id=1, source_target_pairs={{0,4},{4,0},{8,12},{12,8},{16,20},{20,16},{24,28},{28,24},{1,5},{5... | collective-permute-start | bytes 589832 | tf_op jit(solution)/shard_map/ppermute | solution.py:872
  (6 other events, 46.2 us)
